TPU v7x, 32 devices: a whole 2x2x4 slice. The times are simulated.
32 devices in a mesh: dp: 8 (over z, y), seq: 4 (over x, core).
Axes of the slice: x: 2, y: 2, z: 4, core: 2. Of those that a mesh axis runs over, the one named last changes fastest.
Arguments:
- clean_ids: int32 [32, 1024], P('dp', 'seq'), may hold values from 0 to 50303
- lengths: int32 [32], replicated, may hold values from 256 to 1024, as said below
- masked: int32 [32, 256], replicated, may hold values from 0 to 1023, as said below
- attn_in: float32 [768, 2304], P('dp'), may hold values from -0.21875 to 0.21875
- attn_out: float32 [768, 768], P('dp'), may hold values from -2.5 to 2.5
- mlp_in: float32 [768, 3072], P('dp'), may hold values from -0.21875 to 0.21875
- mlp_out: float32 [3072, 768], P('dp'), may hold values from -0.109375 to 0.109375
- table: float32 [50304, 768], P('dp')
- positions: float32 [1024, 768], P('dp'), may hold values from -0.75 to 0.75
- vectors: float32 [14, 768], replicated
- first_attn_in: float32 [768, 2304], P('dp'), may hold values from -2.0861626e-07 to 2.0861626e-07
- first_attn_out: float32 [768, 768], P('dp'), may hold values from -2.0861626e-07 to 2.0861626e-07
- first_mlp_in: float32 [768, 3072], P('dp'), may hold values from -2.0861626e-07 to 2.0861626e-07
- first_mlp_out: float32 [3072, 768], P('dp'), may hold values from -2.0861626e-07 to 2.0861626e-07
- first_table: float32 [50304, 768], P('dp'), may hold values from -2.0861626e-07 to 2.0861626e-07
- first_positions: float32 [1024, 768], P('dp'), may hold values from -2.0861626e-07 to 2.0861626e-07
- first_vectors: float32 [14, 768], replicated, may hold values from -8.34465e-07 to 8.34465e-07
- second_attn_in: float32 [768, 2304], P('dp'), may hold values from 8.60057e-17 to 3.440228e-16
- second_attn_out: float32 [768, 768], P('dp'), may hold values from 8.60057e-17 to 3.440228e-16
- second_mlp_in: float32 [768, 3072], P('dp'), may hold values from 8.60057e-17 to 3.440228e-16
- second_mlp_out: float32 [3072, 768], P('dp'), may hold values from 8.60057e-17 to 3.440228e-16
- second_table: float32 [50304, 768], P('dp'), may hold values from 8.60057e-17 to 3.440228e-16
- second_positions: float32 [1024, 768], P('dp'), may hold values from 8.60057e-17 to 3.440228e-16
- second_vectors: float32 [14, 768], replicated, may hold values from 1.3760912e-15 to 5.504365e-15
Outputs:
- new_attn_in: float32 [768, 2304], P('dp')
- new_attn_out: float32 [768, 768], P('dp')
- new_mlp_in: float32 [768, 3072], P('dp')
- new_mlp_out: float32 [3072, 768], P('dp')
- new_table: float32 [50304, 768], P('dp')
- new_positions: float32 [1024, 768], P('dp')
- new_vectors: float32 [14, 768], replicated
- moment_attn_in: float32 [768, 2304], P('dp')
- moment_attn_out: float32 [768, 768], P('dp')
- moment_mlp_in: float32 [768, 3072], P('dp')
- moment_mlp_out: float32 [3072, 768], P('dp')
- moment_table: float32 [50304, 768], P('dp')
- moment_positions: float32 [1024, 768], P('dp')
- moment_vectors: float32 [14, 768], replicated
- square_attn_in: float32 [768, 2304], P('dp')
- square_attn_out: float32 [768, 768], P('dp')
- square_mlp_in: float32 [768, 3072], P('dp')
- square_mlp_out: float32 [3072, 768], P('dp')
- square_table: float32 [50304, 768], P('dp')
- square_positions: float32 [1024, 768], P('dp')
- square_vectors: float32 [14, 768], replicated
- loss_sum: float32 [], replicated
- masked_count: float32 [], replicated
- grad_norm: float32 [], replicated
Inputs may be any that keep to these rules, and one draw needn't show every extreme that they name: `lengths`: each row's length is 256, 512, or between 897 and 1024; in every aligned block of 4 rows one row is longer than 896; some row has length 1024. `masked`: entries k * 64 to (k + 1) * 64 - 1 of a row are distinct slots of k * 256 to (k + 1) * 256 - 1, the first of them k * 256.
All inputs are finite; a program needn't handle non-finite values.
Results may differ from a plain program's by a relative error of at most 0.012.
The roundings to bfloat16 on the way count: a program that leaves them out, or rounds other values in their place, can miss the bound.
Values may be sent and summed in bfloat16 or wider, within the bound.
A program may use at most 576 MiB of HBM per device.

v0:
```python
import jax
import jax.numpy as jnp
from jax import lax
from jax.sharding import PartitionSpec as P

H = 12
V = 50304
STEP = 10


mask_fill = -1000000000.0
clip_at = 0.002
beta_one = 0.9
beta_two = 0.999
adam_eps = 1e-08


def passed_along(value, axis, steps):
    count = lax.axis_size(axis)
    first, last = (max(0, -steps), min(count, count - steps))
    return lax.ppermute(value, axis, [(source, source + steps) for source in range(first, last)])


def merged(value, axis, join):
    pieces = jax.tree.map(lambda part: lax.all_gather(part, axis), value)
    head = jax.tree.map(lambda part: part[0], pieces)
    tail = jax.tree.map(lambda part: part[1:], pieces)
    total, _ = lax.scan(lambda total, section: (join(total, section), None), head, tail)
    return total


def layer_norm(x, gain, shift):
    centre = x - jnp.mean(x, axis=-1, keepdims=True)
    var = jnp.mean(centre * centre, axis=-1, keepdims=True)
    return centre * lax.rsqrt(var + 1e-05) * gain + shift


def gelu_fn(x):
    return jax.nn.gelu(x, approximate=True)


def combine_softmax(first, second):
    top = jnp.maximum(first[0], second[0])
    total = first[1] * jnp.exp(first[0] - top) + second[1] * jnp.exp(second[0] - top)
    return (top, total, first[2] + second[2])


def adam_update(weight, grad, first, second, rate, decay):
    first_new = beta_one * first + (1.0 - beta_one) * grad
    second_new = beta_two * second + (1.0 - beta_two) * grad * grad
    mhat = first_new / (1.0 - beta_one**STEP)
    vhat = second_new / (1.0 - beta_two**STEP)
    return (
        weight - rate * (mhat / (jnp.sqrt(vhat) + adam_eps) + decay * weight),
        first_new,
        second_new,
    )


def on_device(
    clean_ids,
    lengths,
    masked,
    attn_in,
    attn_out,
    mlp_in,
    mlp_out,
    table,
    positions,
    vectors,
    first_attn_in,
    first_attn_out,
    first_mlp_in,
    first_mlp_out,
    first_table,
    first_positions,
    first_vectors,
    second_attn_in,
    second_attn_out,
    second_mlp_in,
    second_mlp_out,
    second_table,
    second_positions,
    second_vectors,
):
    f32 = jnp.float32
    bf16 = jnp.bfloat16
    rows, slots = clean_ids.shape
    n_dp = lax.axis_size("dp")
    n_seq = lax.axis_size("seq")
    dp_at = lax.axis_index("dp")
    seq_at = lax.axis_index("seq")
    total_len = slots * n_seq
    vocab_part, model = table.shape
    masks = masked.shape[1] // n_seq
    head_dim = model // H
    valid_all = ((masked >= 1) & (masked < lengths[:, None])).astype(f32)
    masked_count = jnp.sum(valid_all)
    my_lengths = lax.dynamic_slice_in_dim(lengths, dp_at * rows, rows)
    picks = lax.dynamic_slice_in_dim(
        lax.dynamic_slice_in_dim(masked, dp_at * rows, rows, 0), seq_at * masks, masks, 1
    )
    valid = lax.dynamic_slice_in_dim(
        lax.dynamic_slice_in_dim(valid_all, dp_at * rows, rows, 0), seq_at * masks, masks, 1
    )
    local = picks - seq_at * slots
    slot_iota = jnp.arange(slots, dtype=jnp.int32)
    is_masked = jnp.any(local[:, None, :] == slot_iota[None, :, None], axis=-1)
    noisy = jnp.where(is_masked, V - 1, clean_ids)
    targets = jnp.take_along_axis(clean_ids, local, axis=1)
    all_ids, all_targets, all_valid = (
        lax.all_gather(noisy, "dp", axis=0, tiled=True),
        lax.all_gather(targets, "dp", axis=0, tiled=True),
        lax.all_gather(valid.astype(jnp.int32), "dp", axis=0, tiled=True),
    )
    w_in, w_out, w_up, w_down, pos_all = (
        lax.all_gather(attn_in.astype(bf16), "dp", axis=0, tiled=True),
        lax.all_gather(attn_out.astype(bf16), "dp", axis=0, tiled=True),
        lax.all_gather(mlp_in.astype(bf16), "dp", axis=0, tiled=True),
        lax.all_gather(mlp_out.astype(bf16), "dp", axis=0, tiled=True),
        lax.all_gather(positions.astype(bf16), "dp", axis=0, tiled=True),
    )
    table_low = table.astype(bf16)
    vocab_start = dp_at * vocab_part
    local_ids = all_ids - vocab_start
    inside = (local_ids >= 0) & (local_ids < vocab_part)
    safe_ids = jnp.clip(local_ids, 0, vocab_part - 1)
    looked = jnp.where(inside[..., None], jnp.take(table_low, safe_ids, axis=0).astype(f32), 0.0)
    embedded = lax.psum_scatter(
        looked.astype(jnp.bfloat16), "dp", scatter_dimension=0, tiled=True
    ).astype(jnp.float32)
    pos_rows = lax.dynamic_slice_in_dim(pos_all, seq_at * slots, slots, 0).astype(f32)
    start = embedded + pos_rows[None]
    attn_normed, norm_one_back = jax.vjp(layer_norm, start, vectors[0], vectors[1])
    attn_low = attn_normed.astype(bf16)
    in_bias = jnp.concatenate([vectors[6], jnp.zeros_like(vectors[6]), vectors[7]])
    qkv = (jnp.dot(attn_low, w_in, preferred_element_type=f32) + in_bias).astype(bf16)
    query_part = qkv[..., :model]
    key_part = qkv[..., model : 2 * model]
    value_part = qkv[..., 2 * model :]
    keys, values = (
        lax.all_gather(key_part, "seq", axis=1, tiled=True),
        lax.all_gather(value_part, "seq", axis=1, tiled=True),
    )
    q_heads = query_part.reshape(rows, slots, H, head_dim)
    k_heads = keys.reshape(rows, total_len, H, head_dim)
    v_heads = values.reshape(rows, total_len, H, head_dim)
    key_keep = (jnp.arange(total_len) < my_lengths[:, None])[:, None, None, :]

    def scores_of():
        raw = jnp.einsum("rshd,rkhd->rhsk", q_heads, k_heads, preferred_element_type=f32) * 0.125
        return jnp.where(key_keep, raw, mask_fill)

    scores = scores_of()
    log_total = jax.nn.logsumexp(scores, axis=-1, keepdims=True)
    probs_low = jnp.exp(scores - log_total).astype(bf16)
    mixed = jnp.einsum("rhsk,rkhd->rshd", probs_low, v_heads, preferred_element_type=f32)
    mixed = mixed.reshape(rows, slots, model).astype(bf16)
    after_attn = start + jnp.dot(mixed, w_out, preferred_element_type=f32) + vectors[8]
    mlp_normed, norm_two_back = jax.vjp(layer_norm, after_attn, vectors[2], vectors[3])
    mlp_low = mlp_normed.astype(bf16)
    up_pre = jnp.dot(mlp_low, w_up, preferred_element_type=f32) + vectors[10:14].reshape(-1)
    activated, gelu_back = jax.vjp(gelu_fn, up_pre)
    act_low = activated.astype(bf16)
    final_in = after_attn + jnp.dot(act_low, w_down, preferred_element_type=f32) + vectors[9]
    final_normed, norm_end_back = jax.vjp(layer_norm, final_in, vectors[4], vectors[5])
    final_low = final_normed.astype(bf16)
    previous = passed_along(final_low[:, -1, :], "seq", 1)
    extended = jnp.concatenate([previous[:, None, :], final_low], axis=1)
    sources = jnp.take_along_axis(extended, local[..., None], axis=1).reshape(rows * masks, model)
    gathered = lax.all_gather(sources, "dp", axis=0, tiled=True)
    logits = jnp.einsum("nd,vd->nv", gathered, table_low, preferred_element_type=f32)
    flat_targets = all_targets.reshape(-1) - vocab_start
    flat_valid = all_valid.reshape(-1).astype(f32)
    hit_mask = flat_targets[:, None] == jnp.arange(vocab_part, dtype=jnp.int32)[None, :]
    part_max = jnp.max(logits, axis=1)
    part_sum = jnp.sum(jnp.exp(logits - part_max[:, None]), axis=1)
    part_hit = jnp.sum(jnp.where(hit_mask, logits, 0.0), axis=1)
    top, summed, hit = merged((part_max, part_sum, part_hit), "dp", combine_softmax)
    log_norm = top + jnp.log(summed)
    loss_group = jnp.sum(flat_valid * (log_norm - hit))
    logit_grad = (
        (flat_valid / masked_count)[:, None]
        * (jnp.exp(logits - log_norm[:, None]) - hit_mask.astype(f32))
    ).astype(bf16)
    gathered_grad = jnp.dot(logit_grad, table_low, preferred_element_type=f32)
    table_grad = jnp.einsum("nv,nd->vd", logit_grad, gathered, preferred_element_type=f32)
    source_grad = lax.psum_scatter(gathered_grad, "dp", scatter_dimension=0, tiled=True).reshape(
        rows, masks, model
    )
    row_ix = jnp.broadcast_to(jnp.arange(rows, dtype=jnp.int32)[:, None], (rows, masks))
    extended_grad = jnp.zeros((rows, slots + 1, model), f32).at[row_ix, local].add(source_grad)
    carried = passed_along(extended_grad[:, 0, :], "seq", -1)
    final_grad = extended_grad[:, 1:, :].at[:, -1, :].add(carried)
    final_in_grad, gain_end, shift_end = norm_end_back(final_grad)
    down_grad = final_in_grad.astype(bf16)
    w_down_grad = jnp.einsum("rsf,rsd->fd", act_low, down_grad, preferred_element_type=f32)
    down_bias = jnp.sum(down_grad.astype(f32), axis=(0, 1))
    act_grad = jnp.einsum("rsd,fd->rsf", down_grad, w_down, preferred_element_type=f32)
    up_grad = gelu_back(act_grad)[0].astype(bf16)
    up_bias = jnp.sum(up_grad.astype(f32), axis=(0, 1))
    w_up_grad = jnp.einsum("rsd,rsf->df", mlp_low, up_grad, preferred_element_type=f32)
    mlp_grad = jnp.einsum("rsf,df->rsd", up_grad, w_up, preferred_element_type=f32)
    attn_res_grad, gain_two, shift_two = norm_two_back(mlp_grad)
    after_grad = final_in_grad + attn_res_grad
    out_grad = after_grad.astype(bf16)
    out_bias = jnp.sum(out_grad.astype(f32), axis=(0, 1))
    w_out_grad = jnp.einsum("rse,rsd->ed", mixed, out_grad, preferred_element_type=f32)
    mixed_flat = jnp.einsum("rsd,ed->rse", out_grad, w_out, preferred_element_type=f32).astype(bf16)
    mixed_grad = mixed_flat.reshape(rows, slots, H, head_dim)
    prob_grad = jnp.einsum("rshd,rkhd->rhsk", mixed_grad, v_heads, preferred_element_type=f32)
    probs = jnp.exp(scores_of() - log_total)
    correction = jnp.sum(prob_grad * probs, axis=-1, keepdims=True)
    score_grad = (probs * (prob_grad - correction)).astype(bf16)
    query_grad = (
        jnp.einsum("rhsk,rkhd->rshd", score_grad, k_heads, preferred_element_type=f32) * 0.125
    )
    key_terms = (
        jnp.einsum("rhsk,rshd->rkhd", score_grad, q_heads, preferred_element_type=f32) * 0.125
    )
    value_terms = jnp.einsum("rhsk,rshd->rkhd", probs_low, mixed_grad, preferred_element_type=f32)
    key_grad, value_grad = (
        lax.psum_scatter(
            key_terms.reshape(rows, total_len, model).astype(jnp.bfloat16),
            "seq",
            scatter_dimension=1,
            tiled=True,
        ).astype(jnp.float32),
        lax.psum_scatter(
            value_terms.reshape(rows, total_len, model).astype(jnp.bfloat16),
            "seq",
            scatter_dimension=1,
            tiled=True,
        ).astype(jnp.float32),
    )
    qkv_grad = jnp.concatenate(
        [query_grad.reshape(rows, slots, model), key_grad, value_grad], axis=-1
    ).astype(bf16)
    qkv_bias = jnp.sum(qkv_grad.astype(f32), axis=(0, 1))
    w_in_grad = jnp.einsum("rsd,rse->de", attn_low, qkv_grad, preferred_element_type=f32)
    normed_grad = jnp.einsum("rse,de->rsd", qkv_grad, w_in, preferred_element_type=f32)
    start_extra, gain_one, shift_one = norm_one_back(normed_grad)
    start_grad = after_grad + start_extra
    pos_grad = jnp.sum(start_grad, axis=0)
    embed_all = lax.all_gather(start_grad.astype(bf16), "dp", axis=0, tiled=True)
    embed_terms = jnp.where(inside[..., None], embed_all.astype(f32), 0.0).reshape(-1, model)
    table_grad = table_grad + jax.ops.segment_sum(
        embed_terms, safe_ids.reshape(-1), num_segments=vocab_part
    )
    pos_full_grad = lax.dynamic_update_slice(
        jnp.zeros((total_len, model), f32), pos_grad, (seq_at * slots, 0)
    )
    vec_grad = jnp.concatenate(
        [
            jnp.stack(
                [
                    gain_one,
                    shift_one,
                    gain_two,
                    shift_two,
                    gain_end,
                    shift_end,
                    qkv_bias[:model],
                    qkv_bias[2 * model :],
                    out_bias,
                    down_bias,
                ]
            ),
            up_bias.reshape(-1, model),
        ],
        axis=0,
    )
    parts = (
        lax.psum_scatter(w_in_grad.reshape(n_dp, -1), "dp", scatter_dimension=0, tiled=True),
        lax.psum_scatter(w_out_grad.reshape(n_dp, -1), "dp", scatter_dimension=0, tiled=True),
        lax.psum_scatter(w_up_grad.reshape(n_dp, -1), "dp", scatter_dimension=0, tiled=True),
        lax.psum_scatter(w_down_grad.reshape(n_dp, -1), "dp", scatter_dimension=0, tiled=True),
        lax.psum_scatter(pos_full_grad.reshape(n_dp, -1), "dp", scatter_dimension=0, tiled=True),
    )
    g_in, g_out, g_up, g_down, g_pos, table_sum, vec_sum, loss_sum = lax.psum(
        (parts[0], parts[1], parts[2], parts[3], parts[4], table_grad, vec_grad, loss_group), "seq"
    )
    shard_grads = (
        g_in.reshape(attn_in.shape),
        g_out.reshape(attn_out.shape),
        g_up.reshape(mlp_in.shape),
        g_down.reshape(mlp_out.shape),
        table_sum,
        g_pos.reshape(positions.shape),
    )
    shard_square = sum((jnp.sum(g * g) for g in shard_grads))
    vec_total, square_total = lax.psum((vec_sum, shard_square), "dp")
    grad_norm = jnp.sqrt(square_total + jnp.sum(vec_total * vec_total))
    factor = clip_at / jnp.maximum(grad_norm, clip_at)
    weights = (attn_in, attn_out, mlp_in, mlp_out, table, positions, vectors)
    all_grads = shard_grads + (vec_total,)
    firsts = (
        first_attn_in,
        first_attn_out,
        first_mlp_in,
        first_mlp_out,
        first_table,
        first_positions,
        first_vectors,
    )
    seconds = (
        second_attn_in,
        second_attn_out,
        second_mlp_in,
        second_mlp_out,
        second_table,
        second_positions,
        second_vectors,
    )
    news, moments, squares = ([], [], [])
    for index in range(7):
        rate, decay = (1.0, 0.0) if index == 6 else (0.1, 0.1)
        new_w, new_m, new_v = adam_update(
            weights[index], all_grads[index] * factor, firsts[index], seconds[index], rate, decay
        )
        news.append(new_w)
        moments.append(new_m)
        squares.append(new_v)
    return (
        news[0],
        news[1],
        news[2],
        news[3],
        news[4],
        news[5],
        news[6],
        moments[0],
        moments[1],
        moments[2],
        moments[3],
        moments[4],
        moments[5],
        moments[6],
        squares[0],
        squares[1],
        squares[2],
        squares[3],
        squares[4],
        squares[5],
        squares[6],
        loss_sum,
        masked_count,
        grad_norm,
    )


def solution(mesh):
    in_specs = (
        P("dp", "seq"),
        P(),
        P(),
        P("dp", None),
        P("dp", None),
        P("dp", None),
        P("dp", None),
        P("dp", None),
        P("dp", None),
        P(),
        P("dp", None),
        P("dp", None),
        P("dp", None),
        P("dp", None),
        P("dp", None),
        P("dp", None),
        P(),
        P("dp", None),
        P("dp", None),
        P("dp", None),
        P("dp", None),
        P("dp", None),
        P("dp", None),
        P(),
    )
    out_specs = (
        P("dp", None),
        P("dp", None),
        P("dp", None),
        P("dp", None),
        P("dp", None),
        P("dp", None),
        P(),
        P("dp", None),
        P("dp", None),
        P("dp", None),
        P("dp", None),
        P("dp", None),
        P("dp", None),
        P(),
        P("dp", None),
        P("dp", None),
        P("dp", None),
        P("dp", None),
        P("dp", None),
        P("dp", None),
        P(),
        P(),
        P(),
        P(),
    )
    return jax.shard_map(
        on_device, mesh=mesh, in_specs=in_specs, out_specs=out_specs, check_vma=False
    )
```

profile of v0, /device:TPU:0, one launch (start us, length us, event | category | flops | bytes accessed | tf_op | source)
XLA Modules:
  0.0 3040.6 jit_solution(6659057034161861517)
XLA Ops:
  11.2 32.3 %all-gather.3 = s32[8,4,256]{2,1,0:T(4,128)S(1)} all-gather(s32[1,4,256]{2,1,0:T(4,128)S(1)} %select_bitcast_fusion), channel_id=1, replica_groups=mesh['dp'=8,'seq'=4] {'dp'}, dimensions={0}, use_global_device_ids=true | all-gather | bytes 36864 | tf_op jit(solution)/shard_map/all_gather | solution.py:112
  55.0 42.0 %gather_fusion = bf16[8192,768]{1,0:T(8,128)(2,1)} fusion(bf16[6288,768]{1,0:T(8,128)(2,1)} %convert_element_type.133, s32[8192]{0:T(1024)S(1)} %broadcast_clamp_fusion), kind=kCustom, calls=%fused_computation | custom fusion | bytes 25198592 | tf_op jit(solution)/shard_map/jit(_take)/gather | solution.py:128
  110.7 205.0 %reduce-scatter.5.cloned.1.call-done = bf16[4,256,768]{2,1,0:T(8,128)(2,1)} async-done(((bf16[32,256,768]{2,1,0:T(8,128)(2,1)}), bf16[4,256,768]{2,1,0:T(8,128)(2,1)}) %reduce-scatter.5.cloned.1.call-update) | async-done | bytes 1572880 | tf_op jit(solution)/shard_map/reduce_scatter | solution.py:129
  318.4 64.5 %all-gather.18.cloned.1.call-done = bf16[768,2304]{1,0:T(8,128)(2,1)} async-done(((bf16[96,2304]{1,0:T(8,128)(2,1)}), bf16[768,2304]{1,0:T(8,128)(2,1)}) %all-gather.18.cloned.1.call-update) | async-done | bytes 3538960 | tf_op jit(solution)/shard_map/all_gather | solution.py:117
  398.3 38.5 %all-gather.20.cloned.1.call-done = bf16[4,1024,768]{2,1,0:T(8,128)(2,1)} async-done(((bf16[4,256,768]{2,1,0:T(8,128)(2,1)}), bf16[4,1024,768]{2,1,0:T(8,128)(2,1)}) %all-gather.20.cloned.1.call-update) | async-done | bytes 6291472 | tf_op jit(solution)/shard_map/all_gather | solution.py:142
  540.9 69.3 %all-gather.26.cloned.1.call-done = bf16[768,3072]{1,0:T(8,128)(2,1)} async-done(((bf16[96,3072]{1,0:T(8,128)(2,1)}), bf16[768,3072]{1,0:T(8,128)(2,1)}) %all-gather.26.cloned.1.call-update) | async-done | bytes 4718608 | tf_op jit(solution)/shard_map/all_gather | solution.py:119
  620.7 70.3 %all-gather.28.cloned.1.call-done = bf16[3072,768]{1,0:T(8,128)(2,1)} async-done(((bf16[384,768]{1,0:T(8,128)(2,1)}), bf16[3072,768]{1,0:T(8,128)(2,1)}) %all-gather.28.cloned.1.call-update) | async-done | bytes 4718608 | tf_op jit(solution)/shard_map/all_gather | solution.py:120
  741.4 26.4 all-gather.4
  773.7 30.0 fusion.75
  826.3 30.5 %all-gather.2 = f32[16384]{0:T(1024)S(1)} all-gather(f32[2048]{0:T(1024)S(1)} %get-tuple-element.78), channel_id=4, replica_groups=mesh['dp'=8,'seq'=4] {'dp'}, dimensions={0}, use_global_device_ids=true | all-gather | bytes 73728 | tf_op jit(solution)/shard_map/all_gather | solution.py:25
  856.8 30.5 %all-gather = f32[16384]{0:T(1024)S(1)} all-gather(f32[2048]{0:T(1024)S(1)} %get-tuple-element.183), channel_id=2, replica_groups=mesh['dp'=8,'seq'=4] {'dp'}, dimensions={0}, use_global_device_ids=true | all-gather | bytes 73728 | tf_op jit(solution)/shard_map/all_gather | solution.py:25
  887.3 30.5 %all-gather.1 = f32[16384]{0:T(1024)S(1)} all-gather(f32[2048]{0:T(1024)S(1)} %get-tuple-element.79), channel_id=3, replica_groups=mesh['dp'=8,'seq'=4] {'dp'}, dimensions={0}, use_global_device_ids=true | all-gather | bytes 73728 | tf_op jit(solution)/shard_map/all_gather | solution.py:25
  920.0 32.1 %fusion.59 = f32[2048,768]{1,0:T(8,128)} fusion(bf16[6288,768]{1,0:T(8,128)(2,1)} %convert_element_type.133, f32[2048,6288]{0,1:T(8,128)} %get-tuple-element.184, f32[2048]{0:T(1024)S(1)} %get-tuple-element.155, s32[2048]{0:T(1024)S(1)} %sub.147, f32[2048]{0:T(1024)S(1)} %get-tuple-element.174), kind=kOutput, calls=%fused_computation.205 | convolution fusion | flops 19857604608 | bytes 67485696 | tf_op jit(solution)/shard_map/dot_general | solution.py:186
  952.9 115.9 %reduce-scatter.7.cloned.1.call-done = f32[256,768]{1,0:T(8,128)} async-done(((f32[2048,768]{1,0:T(8,128)}), f32[256,768]{1,0:T(8,128)}) %reduce-scatter.7.cloned.1.call-update) | async-done | bytes 786448 | tf_op jit(solution)/shard_map/reduce_scatter | solution.py:188
  1165.9 38.5 %multiply_reduce_fusion = (f32[4,12,256]{2,1,0:T(8,128)S(1)}, f32[4,12,256,1024]{3,2,1,0:T(8,128)}) fusion(f32[4,12,256,1024]{3,2,1,0:T(8,128)} %get-tuple-element.178, f32[4,12,256]{2,1,0:T(8,128)S(1)} %copy-done.47, pred[4,1024]{1,0:T(4,128)(4,1)S(1)} %copy-done.54, bf16[4,256,12,64]{1,3,2,0:T(8,128)(2,1)S(1)} %bitcast.137, ...), kind=kOutput, calls=%fused_computation.14 | convolution fusion | flops 1673515008 | bytes 108630016 | tf_op jit(solution)/shard_map/rshd,rkhd->rhsk/dot_general | solution.py:211
  1204.4 40.9 %multiply_convert_fusion.1 = bf16[4,12,256,1024]{3,2,1,0:T(8,128)(2,1)} fusion(f32[4,12,256,1024]{3,2,1,0:T(8,128)} %get-tuple-element.187, f32[4,12,256,1024]{3,2,1,0:T(8,128)} %get-tuple-element.178, f32[4,12,256]{2,1,0:T(8,128)S(1)} %get-tuple-element.186, f32[4,12,256]{2,1,0:T(8,128)S(1)} %copy-done.47, pred[4,1024]{1,0:T(4,128)(4,1)S(1)} %copy-done.54), kind=kLoop, calls=%fused_computation.13 | loop fusion | flops 75497472 | bytes 125931520 | tf_op jit(solution)/shard_map/convert_element_type | solution.py:214
  1290.4 37.2 %reduce-scatter.9.cloned.1.call-done = bf16[4,256,768]{2,1,0:T(8,128)(2,1)} async-done(((bf16[4,1024,768]{2,1,0:T(8,128)(2,1)}), bf16[4,256,768]{2,1,0:T(8,128)(2,1)}) %reduce-scatter.9.cloned.1.call-update) | async-done | bytes 1572880 | tf_op jit(solution)/shard_map/reduce_scatter | solution.py:223
  1418.8 38.1 %fusion.58 = f32[6288,768]{1,0:T(8,128)} fusion(bf16[2048,768]{1,0:T(8,128)(2,1)S(1)} %copy-done.97, f32[2048,6288]{0,1:T(8,128)} %get-tuple-element.184, f32[2048]{0:T(1024)S(1)} %copy-done.87, s32[2048]{0:T(1024)S(1)} %copy-done.78, f32[2048]{0:T(1024)S(1)} %copy-done.89), kind=kOutput, calls=%fused_computation.204 | convolution fusion | flops 19857604608 | bytes 73998336 | tf_op jit(solution)/shard_map/nv,nd->vd/dot_general | solution.py:187
  1456.9 60.9 %all-gather.32.cloned.1.call-done = bf16[32,256,768]{2,1,0:T(8,128)(2,1)} async-done(((bf16[4,256,768]{2,1,0:T(8,128)(2,1)}), bf16[32,256,768]{2,1,0:T(8,128)(2,1)}) %all-gather.32.cloned.1.call-update) | async-done | bytes 12582928 | tf_op jit(solution)/shard_map/all_gather | solution.py:245
  1532.1 69.1 %scatter_fusion.1 = f32[6288,768]{1,0:T(8,128)} fusion(f32[6288,768]{1,0:T(8,128)} %fusion.58, s32[8192]{0:T(1024)S(1)} %bitcast.142, f32[8192,768]{1,0:T(8,128)} %bitcast.125), kind=kCustom, calls=%fused_computation.4 | custom fusion | flops 6291456 | bytes 75530240 | tf_op jit(solution)/shard_map/scatter-add | solution.py:247
  1601.2 846.0 %all-reduce.12.cloned.1.call-done = (f32[8,221184]{1,0:T(8,128)}, f32[8,73728]{1,0:T(8,128)}, f32[8,294912]{1,0:T(8,128)}, f32[8,294912]{1,0:T(8,128)}, f32[8,98304]{1,0:T(8,128)}) async-done(((f32[8,221184]{1,0:T(8,128)}, f32[8,73728]{1,0:T(8,128)}, f32[8,294912]{1,0:T(8,128)}, f32[8,294912]{1,0:T(8,128)}, f32[8,98304]{1,0:T(8,128)}), (f32[8,221184]{1,0:T(8,128)}, f32[8,73728]{1,0:T(8,128)}, ...) | async-done | bytes 31457296
  2489.9 376.7 %all-reduce.14.cloned.1.call-done = (f32[1,221184]{1,0:T(1,128)}, f32[1,73728]{1,0:T(1,128)}, f32[1,294912]{1,0:T(1,128)}, f32[1,294912]{1,0:T(1,128)}, f32[6288,768]{1,0:T(8,128)}, /*index=5*/f32[1,98304]{1,0:T(1,128)}) async-done(((f32[1,221184]{1,0:T(1,128)}, f32[1,73728]{1,0:T(1,128)}, f32[1,294912]{1,0:T(1,128)}, f32[1,294912]{1,0:T(1,128)}, f32[6288,768]{1,0:T(8,128)}, ...) | async-done | bytes 23248912 | tf_op jit(solution)/shard_map/psum | solution.py:280
  2894.8 38.9 %all-reduce.5 = (f32[]{:T(128)}, f32[14,768]{1,0:T(8,128)}) all-reduce(f32[]{:T(128)S(6)} %add.407, f32[14,768]{1,0:T(8,128)} %get-tuple-element.123), channel_id=1, replica_groups=mesh['dp'=8,'seq'=4] {'dp'}, use_global_device_ids=true, to_apply=%region_46.47 | all-reduce | flops 10753 | bytes 86024 | tf_op jit(solution)/shard_map/psum | solution.py:292
  2972.0 47.2 %multiply_subtract_fusion = (f32[6288,768]{1,0:T(8,128)}, f32[6288,768]{1,0:T(8,128)}, f32[6288,768]{1,0:T(8,128)}) fusion(f32[6288,768]{1,0:T(8,128)} %param.35, f32[6288,768]{1,0:T(8,128)} %get-tuple-element.129, f32[]{:T(128)S(6)} %div.189, f32[6288,768]{1,0:T(8,128)} %param.42, f32[6288,768]{1,0:T(8,128)} %param.49), kind=kLoop, calls=%fused_computation.24 | loop fusion | flops 77266944 | bytes 135217152 | tf_op jit(solution)/shard_map/sub | solution.py:54
  (445 shorter events, 607.7 us)
Async XLA Ops:
  7.2 102.5 %all-gather.16.cloned.1.call-start = ((), (), s32[]{:S(2)}) async-start(), calls=%async_computation.5 | async-start | bytes 1769472 | tf_op jit(solution)/shard_map/all_gather | solution.py:121
  9.0 306.8 %reduce-scatter.5.cloned.1.call-start = ((), (), s32[]{:S(2)}) async-start(), calls=%async_computation.4 | async-start | bytes 14155776 | tf_op jit(solution)/shard_map/reduce_scatter | solution.py:129
  107.4 275.4 %all-gather.18.cloned.1.call-start = ((), (), s32[]{:S(2)}) async-start(), calls=%async_computation.6 | async-start | bytes 3981312 | tf_op jit(solution)/shard_map/all_gather | solution.py:117
  109.4 327.3 %all-gather.20.cloned.1.call-start = ((), (), s32[]{:S(2)}) async-start(), calls=%async_computation.7 | async-start | bytes 7864320 | tf_op jit(solution)/shard_map/all_gather | solution.py:142
  109.6 279.7 %copy-start.69 = (f32[768]{0:T(1024)}, f32[768]{0:T(1024)S(1)}, u32[]{:S(2)}) copy-start(f32[768]{0:T(1024)S(1)} %get-tuple-element.100) | copy-start | bytes 9220
  109.6 279.7 %copy-start.92 = (f32[768]{0:T(1024)}, f32[768]{0:T(1024)S(1)}, u32[]{:S(2)}) copy-start(f32[768]{0:T(1024)S(1)} %get-tuple-element.99) | copy-start | bytes 9220
  109.6 500.7 %copy-start.50 = (f32[768]{0:T(1024)}, f32[768]{0:T(1024)S(1)}, u32[]{:S(2)}) copy-start(f32[768]{0:T(1024)S(1)} %get-tuple-element.95) | copy-start | bytes 9220
  109.6 500.7 %copy-start.55 = (f32[768]{0:T(1024)}, f32[768]{0:T(1024)S(1)}, u32[]{:S(2)}) copy-start(f32[768]{0:T(1024)S(1)} %get-tuple-element.94) | copy-start | bytes 9220
  110.7 278.6 %copy-start.11 = (f32[256,768]{1,0:T(8,128)}, f32[256,768]{1,0:T(8,128)S(1)}, u32[]{:S(2)}) copy-start(f32[256,768]{1,0:T(8,128)S(1)} %dynamic-slice_convert_fusion) | copy-start | bytes 2359300
  391.7 93.4 %all-gather.22.cloned.1.call-start = ((), (), s32[]{:S(2)}) async-start(), calls=%async_computation.8 | async-start | bytes 7864320 | tf_op jit(solution)/shard_map/all_gather | solution.py:143
  392.3 143.7 %all-gather.24.cloned.1.call-start = ((), (), s32[]{:S(2)}) async-start(), calls=%async_computation.9 | async-start | bytes 1327104 | tf_op jit(solution)/shard_map/all_gather | solution.py:118
  393.3 216.9 %all-gather.26.cloned.1.call-start = ((), (), s32[]{:S(2)}) async-start(), calls=%async_computation.10 | async-start | bytes 5308416 | tf_op jit(solution)/shard_map/all_gather | solution.py:119
  394.3 296.8 %all-gather.28.cloned.1.call-start = ((), (), s32[]{:S(2)}) async-start(), calls=%async_computation.11 | async-start | bytes 5308416 | tf_op jit(solution)/shard_map/all_gather | solution.py:120
  396.5 377.2 %all-gather.30.cloned.1.call-start = ((), (), s32[]{:S(2)}) async-start(), calls=%async_computation.12 | async-start | bytes 3538944 | tf_op jit(solution)/shard_map/all_gather | solution.py:171
  540.4 150.7 %copy-start.1 = (f32[4,256,768]{2,1,0:T(8,128)}, f32[4,256,768]{2,1,0:T(8,128)S(1)}, u32[]{:S(2)}) copy-start(f32[4,256,768]{2,1,0:T(8,128)S(1)} %get-tuple-element.180) | copy-start | bytes 9437188
  705.3 2.1 collective-permute-start
  711.7 357.0 %reduce-scatter.7.cloned.1.call-start = ((), (), s32[]{:S(2)}) async-start(), calls=%async_computation.13 | async-start | bytes 7077888 | tf_op jit(solution)/shard_map/reduce_scatter | solution.py:188
  740.7 179.3 %copy-start.77 = (s32[2048]{0:T(1024)}, s32[2048]{0:T(1024)S(1)}, u32[]{:S(2)}) copy-start(s32[2048]{0:T(1024)S(1)} %sub.147) | copy-start | bytes 24580
  952.1 338.3 %reduce-scatter.11.cloned.1.call-start = ((), (), s32[]{:S(2)}) async-start(), calls=%async_computation.15 | async-start | bytes 7864320 | tf_op jit(solution)/shard_map/reduce_scatter | solution.py:229
  1093.3 4.1 collective-permute-start.1
  1165.9 161.8 %reduce-scatter.9.cloned.1.call-start = ((), (), s32[]{:S(2)}) async-start(), calls=%async_computation.14 | async-start | bytes 7864320 | tf_op jit(solution)/shard_map/reduce_scatter | solution.py:223
  1269.3 248.5 %all-gather.32.cloned.1.call-start = ((), (), s32[]{:S(2)}) async-start(), calls=%async_computation.16 | async-start | bytes 14155776 | tf_op jit(solution)/shard_map/all_gather | solution.py:245
  1341.2 1106.1 %all-reduce.12.cloned.1.call-start = ((), (), s32[]{:S(2)}) async-start(), calls=%async_computation.17 | async-start | bytes 62914560
  1416.9 1449.7 %all-reduce.14.cloned.1.call-start = ((), (), s32[]{:S(2)}) async-start(), calls=%async_computation.18 | async-start | bytes 46497792 | tf_op jit(solution)/shard_map/psum | solution.py:280
  (95 other events, 1705.8 us)
Sparse Core Ops, SparseCore 0:
  10.8 46.9 all-gather.15
  107.6 208.1 reduce-scatter.4
  318.5 64.2 all-gather.17
  391.8 44.8 all-gather.19
  438.7 46.3 all-gather.21
  487.7 41.0 all-gather.23
  531.6 78.6 all-gather.25
  613.0 78.0 all-gather.27
  711.8 61.8 all-gather.29
  952.2 116.4 reduce-scatter.6
  1166.0 58.3 reduce-scatter.10
  1269.4 58.1 reduce-scatter.8
  1341.3 176.4 all-gather.31
  1524.0 923.1 all-reduce.11
  2471.4 395.1 all-reduce.13
where the time goes:
time: 3050 us; the launch traced here: 3040 us
  waiting for transfers between devices  1910 us (63%)
  other arithmetic  362 us (12%)
  matrix products  340 us (11%)
  blocking collectives  230 us (8%)
  local copies, waits for them, and re-layouts  173 us (6%)
    unnamed x16, waiting for transfers between devices  847 us
    psum x1, waiting for transfers between devices, on_device(): lax.psum((parts[0], parts[1], parts[2], parts[3], parts[4], table_grad, v...  377 us
    reduce_scatter x1, waiting for transfers between devices, on_device(): lax.psum_scatter(looked.astype(jnp.bfloat16), 'dp', scatter_dimension=0,...  205 us
    reduce_scatter x1, waiting for transfers between devices, on_device(): lax.psum_scatter(gathered_grad, 'dp', scatter_dimension=0, tiled=True)  116 us
    all_gather x3, blocking collectives, merged(): pieces = jax.tree.map(lambda part: lax.all_gather(part, axis), value)  91.5 us
    all_gather x1, waiting for transfers between devices, on_device(): lax.all_gather(mlp_out.astype(bf16), 'dp', axis=0, tiled=True)  70.3 us
    all_gather x1, waiting for transfers between devices, on_device(): lax.all_gather(mlp_in.astype(bf16), 'dp', axis=0, tiled=True)  69.3 us
    scatter-add x1, other arithmetic, on_device(): jax.ops.segment_sum(embed_terms, safe_ids.reshape(-1), num_segments=vocab...  69.1 us
  transfers between devices with their start and end apart: 17, of which 13 were waited for; matrix products, arithmetic and copies ran while one was open for 17% of the time, Pallas kernels for 0%

commit v1 on v0

v1 whole, which is shorter than its diff:
```python
import math

import jax
import jax.numpy as jnp
from jax import lax
from jax.experimental import pallas as pl
from jax.experimental.pallas import tpu as pltpu
from jax.sharding import PartitionSpec as P

H = 12
STEP = 10
FETCH = 96
GIVE = 64

mask_fill = -1000000000.0
clip_at = 0.002
beta_one = 0.9
beta_two = 0.999
adam_eps = 1e-08

f32 = jnp.float32
bf16 = jnp.bfloat16
i32 = jnp.int32
HBM = pl.BlockSpec(memory_space=pl.ANY)
MESH = pl.DeviceIdType.MESH


def deliver(x, axes, call_id, block_of=None):
    sizes = [lax.axis_size(axis) for axis in axes]
    count = math.prod(sizes)
    block = x.shape if block_of is None else x.shape[1:]

    def body(x_ref, o_ref, sent, came, own):
        here = [lax.axis_index(axis) for axis in axes]

        def flat(place):
            index = place[0]
            for size, along in zip(sizes[1:], place[1:]):
                index = index * size + along
            return index

        def peer(step):
            place = []
            for size, at in zip(reversed(sizes), reversed(here)):
                place.append(lax.rem(at + lax.rem(step, size), size))
                step = step // size
            return place[::-1]

        def source(place):
            return x_ref if block_of is None else x_ref.at[block_of(place)]

        mine = flat(here)

        def copy(step):
            place = peer(step)
            return pltpu.make_async_remote_copy(
                source(place),
                o_ref.at[mine],
                sent.at[step],
                came.at[step],
                device_id=dict(zip(axes, place)),
                device_id_type=MESH,
            )

        barrier = pltpu.get_barrier_semaphore()

        @pl.loop(1, count)
        def _(step):
            pl.semaphore_signal(
                barrier, inc=1, device_id=dict(zip(axes, peer(step))), device_id_type=MESH
            )

        local = pltpu.make_async_copy(source(here), o_ref.at[mine], own)
        local.start()
        pl.semaphore_wait(barrier, count - 1)

        @pl.loop(1, count)
        def _(step):
            copy(step).start()

        local.wait()

        @pl.loop(1, count)
        def _(step):
            copy(step).wait()

    return pl.pallas_call(
        body,
        out_shape=jax.ShapeDtypeStruct((count,) + block, x.dtype),
        in_specs=[HBM],
        out_specs=HBM,
        scratch_shapes=[
            pltpu.SemaphoreType.DMA((count,)),
            pltpu.SemaphoreType.DMA((count,)),
            pltpu.SemaphoreType.DMA,
        ],
        compiler_params=pltpu.CompilerParams(collective_id=call_id, has_side_effects=True),
    )(x)


def flip(x, axis, span):
    count = lax.axis_size(axis)
    pairs = [(at, at // (2 * span) * 2 * span + (at + span) % (2 * span)) for at in range(count)]
    return lax.ppermute(x, axis, pairs)


def layer_norm(x, gain, shift):
    centre = x - jnp.mean(x, axis=-1, keepdims=True)
    var = jnp.mean(centre * centre, axis=-1, keepdims=True)
    return centre * lax.rsqrt(var + 1e-05) * gain + shift


def gelu_fn(x):
    return jax.nn.gelu(x, approximate=True)


def adam_update(weight, grad, first, second, rate, decay):
    first_new = beta_one * first + (1.0 - beta_one) * grad
    second_new = beta_two * second + (1.0 - beta_two) * grad * grad
    mhat = first_new / (1.0 - beta_one**STEP)
    vhat = second_new / (1.0 - beta_two**STEP)
    return (
        weight - rate * (mhat / (jnp.sqrt(vhat) + adam_eps) + decay * weight),
        first_new,
        second_new,
    )


def as_rows(flat):
    return jnp.pad(flat, (0, -flat.size % 1024)).reshape(-1, 128)


def on_device(
    clean_ids,
    lengths,
    masked,
    attn_in,
    attn_out,
    mlp_in,
    mlp_out,
    table,
    positions,
    vectors,
    first_attn_in,
    first_attn_out,
    first_mlp_in,
    first_mlp_out,
    first_table,
    first_positions,
    first_vectors,
    second_attn_in,
    second_attn_out,
    second_mlp_in,
    second_mlp_out,
    second_table,
    second_positions,
    second_vectors,
):
    rows, slots = clean_ids.shape
    n_dp = lax.axis_size("dp")
    n_seq = lax.axis_size("seq")
    dp_at = lax.axis_index("dp")
    seq_at = lax.axis_index("seq")
    core = lax.rem(seq_at, 2)
    length = slots * n_seq
    vocab_part, model = table.shape
    vocab = vocab_part * n_dp
    head_dim = model // H
    sharers = max(1, n_seq // rows)
    n_pick = masked.shape[1] // sharers
    row_at = seq_at // sharers
    share = lax.rem(seq_at, sharers)
    half = -(-vocab_part // 32) * 16

    def gathered(weight):
        piece = weight.shape[0] // n_seq
        part = lax.dynamic_slice_in_dim(weight, seq_at * piece, piece, 0).astype(bf16)
        return lax.all_gather(part, ("dp", "seq"), axis=0, tiled=True)

    pos_all = gathered(positions)
    w_in = gathered(attn_in)
    w_out = gathered(attn_out)
    w_up = gathered(mlp_in)
    w_down = gathered(mlp_out)

    all_rows = deliver(clean_ids, ("seq",), 1)
    row_ids = lax.dynamic_index_in_dim(all_rows, row_at, 1, keepdims=False).reshape(length)
    row = dp_at * rows + row_at
    row_length = lax.dynamic_index_in_dim(lengths, row, 0, keepdims=False)
    row_masked = lax.dynamic_index_in_dim(masked, row, 0, keepdims=False)
    picks = lax.dynamic_slice_in_dim(row_masked, share * n_pick, n_pick, 0)
    slot = jnp.arange(length, dtype=i32)
    is_masked = jnp.any(slot[:, None] == row_masked[None, :], axis=1)
    noisy = jnp.where(is_masked, vocab - 1, row_ids)
    targets = jnp.sum(jnp.where(picks[:, None] == slot[None, :], row_ids[None, :], 0), axis=1)
    valid_all = ((masked >= 1) & (masked < lengths[:, None])).astype(f32)
    masked_count = jnp.sum(valid_all)

    owner = noisy // vocab_part
    within = noisy - owner * vocab_part
    owner_half = owner * 2 + (within >= half).astype(i32)
    within_half = jnp.where(within >= half, within - half, within)
    same = noisy[:, None] == noisy[None, :]
    leader = jnp.min(jnp.where(same, slot[None, :], length), axis=1)
    leads = leader == slot
    before = (slot[None, :] < slot[:, None]) & leads[None, :]
    rank = jnp.sum((before & (owner[:, None] == owner[None, :])).astype(i32), axis=1)
    rank_half = jnp.sum((before & (owner_half[:, None] == owner_half[None, :])).astype(i32), axis=1)
    lead_of = leader[:, None] == slot[None, :]
    place = jnp.sum(jnp.where(lead_of, rank[None, :], 0), axis=1)
    place_half = jnp.sum(jnp.where(lead_of, rank_half[None, :], 0), axis=1)

    def asked(owners, ranks, names, count, size, turn):
        spot = jnp.where(ranks // size == turn, owners * size + lax.rem(ranks, size), -1)
        spots = jnp.arange(count * size, dtype=i32)
        listed = leads[None, :] & (spots[:, None] == spot[None, :])
        return spot, jnp.sum(jnp.where(listed, names[None, :], 0), axis=1)

    spot, ask = asked(owner, place, within, n_dp, FETCH, 0)
    spot_half, ask_half = asked(owner_half, place_half, within_half, 2 * n_dp, GIVE, 0)
    turns = jnp.stack([jnp.max(place) // FETCH + 1, jnp.max(place_half) // GIVE + 1])
    pieces = [as_rows(piece) for piece in (ask, ask_half, targets, turns)]
    ends = [0]
    for piece in pieces:
        ends.append(ends[-1] + piece.shape[0])
    told = deliver(jnp.concatenate(pieces), ("dp", "seq"), 2)

    def heard(index, size):
        return told[:, ends[index] : ends[index + 1]].reshape(n_dp * n_seq, -1)[:, :size]

    turns = jnp.max(heard(3, 2), axis=0)
    asks = lax.dynamic_index_in_dim(heard(0, n_dp * FETCH).reshape(n_dp, n_seq, n_dp, FETCH), seq_at, 1, False)
    asks = lax.dynamic_index_in_dim(asks, dp_at, 1, False)
    half_at = dp_at * 2 + core
    asks_half = lax.dynamic_index_in_dim(heard(1, 2 * n_dp * GIVE).reshape(-1, 2 * n_dp, GIVE), half_at, 1, False)
    all_targets = lax.dynamic_index_in_dim(heard(2, n_pick).reshape(n_dp, n_seq, n_pick), seq_at, 1, False)

    def one_hot(spots, count):
        return (spots[:, None] == jnp.arange(count, dtype=i32)[None, :]).astype(bf16)

    found = jnp.take(table, asks, axis=0).astype(bf16)
    fetched = deliver(found, ("dp",), 3, lambda place: place[0]).reshape(n_dp * FETCH, model)
    embedded = jnp.dot(one_hot(spot, n_dp * FETCH), fetched, preferred_element_type=f32)

    def fetch_more(state):
        turn, total = state
        next_spot, next_ask = asked(owner, place, within, n_dp, FETCH, turn)
        wanted = lax.all_to_all(next_ask.reshape(n_dp, FETCH), "dp", 0, 0)
        sent = jnp.take(table, wanted, axis=0).astype(bf16)
        got = lax.all_to_all(sent, "dp", 0, 0).reshape(n_dp * FETCH, model)
        return turn + 1, total + jnp.dot(one_hot(next_spot, n_dp * FETCH), got, preferred_element_type=f32)

    _, embedded = lax.while_loop(lambda state: state[0] < turns[0], fetch_more, (jnp.int32(1), embedded))

    start = embedded + pos_all.astype(f32)
    attn_normed, norm_one_back = jax.vjp(layer_norm, start, vectors[0], vectors[1])
    attn_low = attn_normed.astype(bf16)
    in_bias = jnp.concatenate([vectors[6], jnp.zeros_like(vectors[6]), vectors[7]])
    qkv = (jnp.dot(attn_low, w_in, preferred_element_type=f32) + in_bias).astype(bf16)
    chosen = one_hot(picks - 1, length)
    query = jnp.dot(chosen, qkv[:, :model], preferred_element_type=f32).astype(bf16)
    start_picked = jnp.dot(chosen.astype(f32), start, precision=lax.Precision.HIGHEST)
    q_heads = query.reshape(n_pick, H, head_dim)
    k_heads = qkv[:, model : 2 * model].reshape(length, H, head_dim)
    v_heads = qkv[:, 2 * model :].reshape(length, H, head_dim)
    key_keep = (slot < row_length)[None, None, :]
    raw = jnp.einsum("shd,khd->hsk", q_heads, k_heads, preferred_element_type=f32) * 0.125
    scores = jnp.where(key_keep, raw, mask_fill)
    log_total = jax.nn.logsumexp(scores, axis=-1, keepdims=True)
    probs = jnp.exp(scores - log_total)
    probs_low = probs.astype(bf16)
    mixed = jnp.einsum("hsk,khd->shd", probs_low, v_heads, preferred_element_type=f32)
    mixed = mixed.reshape(n_pick, model).astype(bf16)
    after_attn = start_picked + jnp.dot(mixed, w_out, preferred_element_type=f32) + vectors[8]
    mlp_normed, norm_two_back = jax.vjp(layer_norm, after_attn, vectors[2], vectors[3])
    mlp_low = mlp_normed.astype(bf16)
    up_pre = jnp.dot(mlp_low, w_up, preferred_element_type=f32) + vectors[10:14].reshape(-1)
    activated, gelu_back = jax.vjp(gelu_fn, up_pre)
    act_low = activated.astype(bf16)
    final_in = after_attn + jnp.dot(act_low, w_down, preferred_element_type=f32) + vectors[9]
    final_normed, norm_end_back = jax.vjp(layer_norm, final_in, vectors[4], vectors[5])
    sources = final_normed.astype(bf16)

    table_low = table.astype(bf16)
    heads = deliver(sources, ("dp",), 4).reshape(n_dp * n_pick, model)
    logits = jnp.einsum("nd,vd->nv", heads, table_low, preferred_element_type=f32)
    flat_targets = all_targets.reshape(-1) - dp_at * vocab_part
    rows_here = valid_all.reshape(n_dp, rows, sharers, n_pick)
    rows_here = lax.dynamic_index_in_dim(rows_here, row_at, 1, False)
    flat_valid = lax.dynamic_index_in_dim(rows_here, share, 1, False).reshape(-1)
    hit_mask = flat_targets[:, None] == jnp.arange(vocab_part, dtype=i32)[None, :]
    part_max = jnp.max(logits, axis=1)
    part_sum = jnp.sum(jnp.exp(logits - part_max[:, None]), axis=1)
    part_hit = jnp.sum(jnp.where(hit_mask, logits, 0.0), axis=1)
    stats = jnp.stack([part_max, part_sum, part_hit]).reshape(3, -1, 128)
    stats = deliver(stats, ("dp",), 5).reshape(n_dp, 3, -1)
    top = jnp.max(stats[:, 0], axis=0)
    summed = jnp.sum(stats[:, 1] * jnp.exp(stats[:, 0] - top[None]), axis=0)
    log_norm = top + jnp.log(summed)
    loss_group = jnp.sum(flat_valid * (log_norm - jnp.sum(stats[:, 2], axis=0)))
    logit_grad = (
        (flat_valid / masked_count)[:, None]
        * (jnp.exp(logits - log_norm[:, None]) - hit_mask.astype(f32))
    ).astype(bf16)
    heads_grad = jnp.dot(logit_grad, table_low, preferred_element_type=f32)
    final_grad = deliver(
        heads_grad.astype(bf16).reshape(n_dp, n_pick, model), ("dp",), 6, lambda place: place[0]
    )
    final_grad = jnp.sum(final_grad.astype(f32), axis=0)
    table_grad = jnp.einsum("nv,nd->vd", logit_grad, heads, preferred_element_type=f32)
    table_grad = jnp.pad(table_grad, ((0, 2 * half - vocab_part), (0, 0)))
    half_own = lax.dynamic_slice_in_dim(table_grad, core * half, half, 0)
    half_other = lax.dynamic_slice_in_dim(table_grad, (1 - core) * half, half, 0).astype(bf16)
    half_low = (half_own + flip(half_other, "seq", 1).astype(f32)).astype(bf16)
    if n_seq == 4:
        half_sum = half_low.astype(f32) + flip(half_low, "seq", 2).astype(f32)
    else:
        groups = [list(range(at, n_seq, 2)) for at in range(2)]
        half_sum = jnp.sum(lax.all_gather(half_low, "seq", axis_index_groups=groups).astype(f32), axis=0)

    final_in_grad, gain_end, shift_end = norm_end_back(final_grad)
    down_grad = final_in_grad.astype(bf16)
    w_down_grad = jnp.einsum("sf,sd->fd", act_low, down_grad, preferred_element_type=f32)
    down_bias = jnp.sum(down_grad.astype(f32), axis=0)
    act_grad = jnp.einsum("sd,fd->sf", down_grad, w_down, preferred_element_type=f32)
    up_grad = gelu_back(act_grad)[0].astype(bf16)
    up_bias = jnp.sum(up_grad.astype(f32), axis=0)
    w_up_grad = jnp.einsum("sd,sf->df", mlp_low, up_grad, preferred_element_type=f32)
    mlp_grad = jnp.einsum("sf,df->sd", up_grad, w_up, preferred_element_type=f32)
    attn_res_grad, gain_two, shift_two = norm_two_back(mlp_grad)
    after_grad = final_in_grad + attn_res_grad
    out_grad = after_grad.astype(bf16)
    out_bias = jnp.sum(out_grad.astype(f32), axis=0)
    w_out_grad = jnp.einsum("se,sd->ed", mixed, out_grad, preferred_element_type=f32)
    mixed_grad = jnp.einsum("sd,ed->se", out_grad, w_out, preferred_element_type=f32).astype(bf16)
    mixed_grad = mixed_grad.reshape(n_pick, H, head_dim)
    prob_grad = jnp.einsum("shd,khd->hsk", mixed_grad, v_heads, preferred_element_type=f32)
    correction = jnp.sum(prob_grad * probs, axis=-1, keepdims=True)
    score_grad = (probs * (prob_grad - correction)).astype(bf16)
    query_grad = jnp.einsum("hsk,khd->shd", score_grad, k_heads, preferred_element_type=f32) * 0.125
    key_grad = jnp.einsum("hsk,shd->khd", score_grad, q_heads, preferred_element_type=f32) * 0.125
    value_grad = jnp.einsum("hsk,shd->khd", probs_low, mixed_grad, preferred_element_type=f32)
    query_grad = query_grad.reshape(n_pick, model).astype(bf16)
    query_full = jnp.einsum("st,sd->td", chosen, query_grad, preferred_element_type=f32).astype(bf16)
    qkv_grad = jnp.concatenate(
        [
            query_full,
            key_grad.reshape(length, model).astype(bf16),
            value_grad.reshape(length, model).astype(bf16),
        ],
        axis=-1,
    )
    qkv_bias = jnp.sum(qkv_grad.astype(f32), axis=0)
    w_in_grad = jnp.einsum("sd,se->de", attn_low, qkv_grad, preferred_element_type=f32)
    normed_grad = jnp.einsum("se,de->sd", qkv_grad, w_in, preferred_element_type=f32)
    start_extra, gain_one, shift_one = norm_one_back(normed_grad)
    after_full = jnp.einsum(
        "st,sd->td", chosen.astype(f32), after_grad, precision=lax.Precision.HIGHEST
    )
    start_grad = after_full + start_extra
    start_grad_low = start_grad.astype(bf16)

    def given(spots):
        summed_ids = jnp.einsum(
            "ts,td->sd", one_hot(spots, 2 * n_dp * GIVE), start_grad_low, preferred_element_type=f32
        )
        return summed_ids.astype(bf16).reshape(2 * n_dp, GIVE, model)

    def taken(names, values):
        names = names.reshape(1, -1)
        where = (jnp.arange(half, dtype=i32)[:, None] == names).astype(bf16)
        return jnp.dot(where, values.reshape(-1, model), preferred_element_type=f32)

    came = deliver(
        given(spot_half), ("dp", "seq"), 7, lambda place: place[0] * 2 + lax.rem(place[1], 2)
    )
    half_sum = half_sum + taken(asks_half, came)

    def give_more(state):
        turn, total = state
        next_spot, next_ask = asked(owner_half, place_half, within_half, 2 * n_dp, GIVE, turn)
        names = lax.all_gather(next_ask.reshape(2 * n_dp, GIVE), ("dp", "seq"))
        names = lax.dynamic_index_in_dim(names, half_at, 1, False)
        sent = given(next_spot).reshape(n_dp, 1, 2, GIVE, model)
        sent = jnp.broadcast_to(sent, (n_dp, n_seq // 2, 2, GIVE, model)).reshape(-1, GIVE, model)
        got = lax.all_to_all(sent, ("dp", "seq"), 0, 0)
        return turn + 1, total + taken(names, got)

    _, half_sum = lax.while_loop(lambda state: state[0] < turns[1], give_more, (jnp.int32(1), half_sum))

    def spread_sum(grad):
        pieces = grad.reshape(n_dp, n_seq, -1, grad.shape[1]).astype(bf16)
        pieces = pieces.reshape(-1, grad.shape[1])
        part = lax.psum_scatter(pieces, ("dp", "seq"), scatter_dimension=0, tiled=True)
        return lax.all_gather(part, "seq", axis=0, tiled=True).astype(f32)

    g_down = spread_sum(w_down_grad)
    g_up = spread_sum(w_up_grad)
    g_out = spread_sum(w_out_grad)
    g_in = spread_sum(w_in_grad)
    g_pos = spread_sum(start_grad)
    vec_grad = jnp.concatenate(
        [
            jnp.stack(
                [
                    gain_one,
                    shift_one,
                    gain_two,
                    shift_two,
                    gain_end,
                    shift_end,
                    qkv_bias[:model],
                    qkv_bias[2 * model :],
                    out_bias,
                    down_bias,
                ]
            ),
            up_bias.reshape(-1, model),
        ],
        axis=0,
    )
    vec_total = lax.psum(vec_grad, ("dp", "seq"))
    half_square = jnp.sum(half_sum * half_sum)
    half_low = half_sum.astype(bf16)
    half_pair = flip(half_low, "seq", 1)
    table_sum = jnp.where(
        core == 0, jnp.concatenate([half_low, half_pair]), jnp.concatenate([half_pair, half_low])
    )[:vocab_part].astype(f32)
    layer_grads = (g_in, g_out, g_up, g_down, g_pos)
    layer_square = sum(jnp.sum(g * g) for g in layer_grads)
    said = jnp.concatenate(
        [
            jnp.full((1, 128), half_square),
            jnp.full((1, 128), layer_square),
            jnp.full((1, 128), loss_group),
            jnp.zeros((5, 128), f32),
        ]
    )
    said = deliver(said, ("dp", "seq"), 8)[:, :3, 0].reshape(n_dp, n_seq, 3)
    square_total = jnp.sum(said[:, :2, 0]) + jnp.sum(said[:, 0, 1])
    loss_sum = jnp.sum(said[0, :, 2])
    grad_norm = jnp.sqrt(square_total + jnp.sum(vec_total * vec_total))
    factor = clip_at / jnp.maximum(grad_norm, clip_at)
    weights = (attn_in, attn_out, mlp_in, mlp_out, table, positions, vectors)
    all_grads = (g_in, g_out, g_up, g_down, table_sum, g_pos, vec_total)
    firsts = (
        first_attn_in,
        first_attn_out,
        first_mlp_in,
        first_mlp_out,
        first_table,
        first_positions,
        first_vectors,
    )
    seconds = (
        second_attn_in,
        second_attn_out,
        second_mlp_in,
        second_mlp_out,
        second_table,
        second_positions,
        second_vectors,
    )
    news, moments, squares = ([], [], [])
    for index in range(7):
        rate, decay = (1.0, 0.0) if index == 6 else (0.1, 0.1)
        new_w, new_m, new_v = adam_update(
            weights[index], all_grads[index] * factor, firsts[index], seconds[index], rate, decay
        )
        news.append(new_w)
        moments.append(new_m)
        squares.append(new_v)
    return (*news, *moments, *squares, loss_sum, masked_count, grad_norm)


def solution(mesh):
    part = P("dp", None)
    six = (part,) * 6 + (P(),)
    return jax.shard_map(
        on_device,
        mesh=mesh,
        in_specs=(P("dp", "seq"), P(), P()) + six * 3,
        out_specs=six * 3 + (P(), P(), P()),
        check_vma=False,
    )
```

time: 3050 us -> 1290 us (0.42)
  waiting for transfers between devices: 1910 us -> 366 us
  Pallas kernels: 0 us -> 331 us
  other arithmetic: 362 us -> 178 us
  blocking collectives: 230 us -> 93.5 us
  matrix products: 340 us -> 224 us
  local copies, waits for them, and re-layouts: 173 us -> 57.5 us
    unnamed x16 -> x10, waiting for transfers between devices: 847 us -> 0.16 us
    psum x1 -> x0, waiting for transfers between devices: 377 us -> none  [on_device(): lax.psum((parts[0], parts[1], parts[2], parts[3], parts[4], table_grad, v...]
    pallas_call x0 -> x8, Pallas kernels: none -> 331 us  [deliver(): pl.pallas_call(body, out_shape=jax.ShapeDtypeStruct((count,) + block, x.d...]
    reduce_scatter x4 -> x5, waiting for transfers between devices: 358 us -> 187 us  [spread_sum(): lax.psum_scatter(pieces, ('dp', 'seq'), scatter_dimension=0, tiled=True)]
    all_gather x9 -> x5, waiting for transfers between devices: 328 us -> 175 us  [gathered(): return lax.all_gather(part, ('dp', 'seq'), axis=0, tiled=True)]
    all_gather x6 -> x5, blocking collectives: 176 us -> 37.9 us  [spread_sum(): return lax.all_gather(part, 'seq', axis=0, tiled=True).astype(f32)]
    dot_general x17 -> x24, matrix products: 306 us -> 205 us  [the longest x1 38.6 us: on_device(): heads_grad = jnp.dot(logit_grad, table_low, preferred_element_type=f32)]
    scatter-add x2 -> x0, other arithmetic: 93.3 us -> none  [the longest x1 69.1 us: on_device(): jax.ops.segment_sum(embed_terms, safe_ids.reshape(-1), num_segments=vocab...]
  transfers between devices with their start and end apart: 17 -> 13, of which waited for: 13 -> 7; matrix products, arithmetic and copies ran while one was open for 17% -> 19% of each run, Pallas kernels for 0% -> 15%
where the time goes in v1:
time: 1290 us; the launch traced here: 1280 us
  waiting for transfers between devices  366 us (28%)
  Pallas kernels  331 us (26%)
  matrix products  224 us (17%)
  other arithmetic  178 us (14%)
  blocking collectives  93.5 us (7%)
  local copies, waits for them, and re-layouts  57.5 us (4%)
  between operations  26.9 us (2%)
    pallas_call x8, Pallas kernels, deliver(): pl.pallas_call(body, out_shape=jax.ShapeDtypeStruct((count,) + block, x.d...  331 us
    reduce_scatter x5, waiting for transfers between devices, spread_sum(): lax.psum_scatter(pieces, ('dp', 'seq'), scatter_dimension=0, tiled=True)  187 us
    all_gather x5, waiting for transfers between devices, gathered(): return lax.all_gather(part, ('dp', 'seq'), axis=0, tiled=True)  175 us
    sub x7, other arithmetic, adam_update(): weight - rate * (mhat / (jnp.sqrt(vhat) + adam_eps) + decay * weight)  59.7 us
    psum x1, blocking collectives, on_device(): vec_total = lax.psum(vec_grad, ('dp', 'seq'))  55.6 us
    dot_general x1, matrix products, on_device(): heads_grad = jnp.dot(logit_grad, table_low, preferred_element_type=f32)  38.6 us
    all_gather x5, blocking collectives, spread_sum(): return lax.all_gather(part, 'seq', axis=0, tiled=True).astype(f32)  37.9 us
    dot_general x1, matrix products, on_device(): jnp.einsum('nv,nd->vd', logit_grad, heads, preferred_element_type=f32)  37.7 us
  transfers between devices with their start and end apart: 13, of which 7 were waited for; matrix products, arithmetic and copies ran while one was open for 19% of the time, Pallas kernels for 15%

profile of v1, /device:TPU:0, one launch (start us, length us, event | category | flops | bytes accessed | tf_op | source)
XLA Modules:
  0.0 1280.8 jit_solution(3054933595355172398)
XLA Ops:
  40.7 16.4 %shard_map.416 = s32[32,32,128]{2,1,0:T(8,128)} custom-call(s32[32,128]{1,0:T(8,128)} %pad_add_fusion.x_ref), custom_call_target="tpu_custom_call" | custom-call | tf_op jit(solution)/shard_map/pallas_call | solution.py:87
  59.2 11.4 convert.3
  70.6 9.8 gather_fusion.1
  81.8 27.7 %shard_map.417 = bf16[8,96,768]{2,1,0:T(8,128)(2,1)} custom-call(bf16[8,96,768]{2,1,0:T(8,128)(2,1)} %select_convert_fusion.1.x_ref), custom_call_target="tpu_custom_call" | custom-call | tf_op jit(solution)/shard_map/pallas_call | solution.py:87
  125.1 21.6 %all-gather.8.cloned.1.call-done = bf16[768,2304]{1,0:T(8,128)(2,1)} async-done(((bf16[24,2304]{1,0:T(8,128)(2,1)}), bf16[768,2304]{1,0:T(8,128)(2,1)}) %all-gather.8.cloned.1.call-update) | async-done | bytes 3538960 | tf_op jit(solution)/shard_map/all_gather | solution.py:178
  173.8 29.3 %all-gather.10.cloned.1.call-done = bf16[768,768]{1,0:T(8,128)(2,1)} async-done(((bf16[24,768]{1,0:T(8,128)(2,1)}), bf16[768,768]{1,0:T(8,128)(2,1)}) %all-gather.10.cloned.1.call-update) | async-done | bytes 1179664 | tf_op jit(solution)/shard_map/all_gather | solution.py:178
  205.3 63.7 %all-gather.12.cloned.1.call-done = bf16[768,3072]{1,0:T(8,128)(2,1)} async-done(((bf16[24,3072]{1,0:T(8,128)(2,1)}), bf16[768,3072]{1,0:T(8,128)(2,1)}) %all-gather.12.cloned.1.call-update) | async-done | bytes 4718608 | tf_op jit(solution)/shard_map/all_gather | solution.py:178
  274.5 60.4 %all-gather.14.cloned.1.call-done = bf16[3072,768]{1,0:T(8,128)(2,1)} async-done(((bf16[96,768]{1,0:T(8,128)(2,1)}), bf16[3072,768]{1,0:T(8,128)(2,1)}) %all-gather.14.cloned.1.call-update) | async-done | bytes 4718608 | tf_op jit(solution)/shard_map/all_gather | solution.py:178
  342.5 54.5 %shard_map.418 = bf16[8,256,768]{2,1,0:T(8,128)(2,1)} custom-call(bf16[256,768]{1,0:T(8,128)(2,1)} %add_convert_fusion.3.x_ref), custom_call_target="tpu_custom_call" | custom-call | tf_op jit(solution)/shard_map/pallas_call | solution.py:87
  397.1 32.2 %fusion.133 = (f32[2048]{0:T(1024)}, f32[2048,6288]{0,1:T(8,128)}) fusion(bf16[2048,768]{1,0:T(8,128)(2,1)} %bitcast.189, f32[6288,768]{1,0:T(8,128)} %param.35), kind=kOutput, calls=%fused_computation.330 | convolution fusion | flops 19798042624 | bytes 73981952 | tf_op jit(solution)/shard_map/nd,vd->nv/dot_general | solution.py:286
  429.2 23.4 %exponential_reduce_fusion = (f32[2048]{0:T(1024)S(1)}, f32[2048]{0:T(1024)S(1)}) fusion(f32[2048,6288]{0,1:T(8,128)} %get-tuple-element.476, f32[2048]{0:T(1024)} %get-tuple-element.475, s32[2048]{0:T(1024)} %bitcast.229), kind=kLoop, calls=%fused_computation.53 | loop fusion | flops 64385024 | bytes 51544064 | tf_op jit(solution)/shard_map/reduce_sum | solution.py:293
  453.3 25.7 %shard_map.419 = f32[8,3,16,128]{3,2,1,0:T(8,128)} custom-call(f32[3,16,128]{2,1,0:T(8,128)} %pad_maximum_fusion.3.x_ref), custom_call_target="tpu_custom_call" | custom-call | tf_op jit(solution)/shard_map/pallas_call | solution.py:87
  487.3 38.6 %fusion.35 = bf16[2048,768]{1,0:T(8,128)(2,1)} fusion(f32[6288,768]{1,0:T(8,128)} %param.35, f32[2048,6288]{0,1:T(8,128)} %get-tuple-element.476, f32[2048]{0:T(1024)} %get-tuple-element.432, s32[2048]{0:T(1024)} %bitcast.230, f32[2048]{0:T(1024)} %bitcast.238), kind=kOutput, calls=%fused_computation.110 | convolution fusion | flops 19864006656 | bytes 73998336 | tf_op jit(solution)/shard_map/dot_general | solution.py:305
  525.9 53.7 %shard_map.420 = bf16[8,256,768]{2,1,0:T(8,128)(2,1)} custom-call(bf16[8,256,768]{2,1,0:T(8,128)(2,1)} %bitcast.192), custom_call_target="tpu_custom_call" | custom-call | tf_op jit(solution)/shard_map/pallas_call | solution.py:87
  596.6 11.8 multiply_reduce_fusion
  651.8 37.7 %fusion.105 = f32[6288,768]{1,0:T(8,128)} fusion(bf16[2048,768]{1,0:T(8,128)(2,1)S(1)} %bitcast.190, f32[2048,6288]{0,1:T(8,128)} %get-tuple-element.476, f32[2048]{0:T(1024)S(1)} %copy-done.74, s32[2048]{0:T(1024)S(1)} %bitcast.231, f32[2048]{0:T(1024)S(1)} %bitcast.239), kind=kOutput, calls=%fused_computation.315 | convolution fusion | flops 19857604608 | bytes 73998336 | tf_op jit(solution)/shard_map/nv,nd->vd/dot_general | solution.py:310
  721.0 138.4 %shard_map.421 = bf16[32,64,768]{2,1,0:T(8,128)(2,1)} custom-call(bf16[16,64,768]{2,1,0:T(8,128)(2,1)} %bitcast.197), custom_call_target="tpu_custom_call" | custom-call | tf_op jit(solution)/shard_map/pallas_call | solution.py:87
  866.0 55.6 %psum.7 = f32[14,768]{1,0:T(8,128)} all-reduce(f32[14,768]{1,0:T(8,128)S(1)} %concatenate.26), channel_id=1, replica_groups=mesh['dp'=8,'seq'=4] {'dp','seq'}, use_global_device_ids=true, to_apply=%region_65.66 | all-reduce | flops 10752 | bytes 86016 | tf_op jit(solution)/shard_map/psum | solution.py:422
  921.5 13.9 %fusion.17 = f32[3152,768]{1,0:T(8,128)} fusion(bf16[2048,768]{1,0:T(8,128)(2,1)S(1)} %bitcast.191, s32[2048]{0:T(1024)S(1)} %eq.392), kind=kOutput, calls=%fused_computation.56 | convolution fusion | flops 9921789952 | bytes 12836864 | tf_op jit(solution)/shard_map/dot_general | solution.py:372
  935.5 11.8 add_add_fusion
  949.5 11.8 fusion.125
  987.6 83.9 %reduce-scatter.10.cloned.1.call-done = bf16[24,3072]{1,0:T(8,128)(2,1)} async-done(((bf16[768,3072]{1,0:T(8,128)(2,1)}), bf16[24,3072]{1,0:T(8,128)(2,1)}) %reduce-scatter.10.cloned.1.call-update) | async-done | bytes 147472 | tf_op jit(solution)/shard_map/reduce_scatter | solution.py:394
  1080.8 103.0 %reduce-scatter.12.cloned.1.call-done = bf16[96,768]{1,0:T(8,128)(2,1)} async-done(((bf16[3072,768]{1,0:T(8,128)(2,1)}), bf16[96,768]{1,0:T(8,128)(2,1)}) %reduce-scatter.12.cloned.1.call-update) | async-done | bytes 147472 | tf_op jit(solution)/shard_map/reduce_scatter | solution.py:394
  1225.6 46.8 %multiply_subtract_fusion = (f32[6288,768]{1,0:T(8,128)}, f32[6288,768]{1,0:T(8,128)}, f32[6288,768]{1,0:T(8,128)}) fusion(f32[6288,768]{1,0:T(8,128)} %param.35, f32[]{:T(128)S(6)} %div.311, bf16[3152,768]{1,0:T(8,128)(2,1)} %get-tuple-element.447, bf16[3152,768]{1,0:T(8,128)(2,1)} %collective-permute-done.2, pred[]{:T(512)S(6)} %eq.397, ...), kind=kLoop, calls=%fused_computation.58 | loop fusion | flops 125558784 | bytes 125583368 | tf_op jit(solution)/shard_map/sub | solution.py:123
  (378 shorter events, 272.1 us)
Async XLA Ops:
  7.2 111.3 %all-gather.6.cloned.1.call-start = ((), (), s32[]{:S(2)}) async-start(), calls=%async_computation.8 | async-start | bytes 1622016 | tf_op jit(solution)/shard_map/all_gather | solution.py:178
  8.8 138.0 %all-gather.8.cloned.1.call-start = ((), (), s32[]{:S(2)}) async-start(), calls=%async_computation.9 | async-start | bytes 3649536 | tf_op jit(solution)/shard_map/all_gather | solution.py:178
  10.5 192.6 %all-gather.10.cloned.1.call-start = ((), (), s32[]{:S(2)}) async-start(), calls=%async_computation.10 | async-start | bytes 1216512 | tf_op jit(solution)/shard_map/all_gather | solution.py:178
  12.1 257.0 %all-gather.12.cloned.1.call-start = ((), (), s32[]{:S(2)}) async-start(), calls=%async_computation.11 | async-start | bytes 4866048 | tf_op jit(solution)/shard_map/all_gather | solution.py:178
  13.8 321.1 %all-gather.14.cloned.1.call-start = ((), (), s32[]{:S(2)}) async-start(), calls=%async_computation.12 | async-start | bytes 4866048 | tf_op jit(solution)/shard_map/all_gather | solution.py:178
  15.5 946.4 %reduce-scatter.8.cloned.1.call-start = ((), (), s32[]{:S(2)}) async-start(), calls=%async_computation.14 | async-start | bytes 1216512 | tf_op jit(solution)/shard_map/reduce_scatter | solution.py:394
  32.4 126.1 %copy-start.62 = (s32[256]{0:T(256)}, s32[256]{0:T(256)S(1)}, u32[]{:S(2)}) copy-start(s32[256]{0:T(256)S(1)} %broadcast_add_fusion) | copy-start | bytes 3076
  34.3 112.5 %copy-start.51 = (f32[768]{0:T(1024)}, f32[768]{0:T(1024)S(1)}, u32[]{:S(2)}) copy-start(f32[768]{0:T(1024)S(1)} %get-tuple-element.350) | copy-start | bytes 9220
  34.3 112.5 %copy-start.76 = (f32[768]{0:T(1024)}, f32[768]{0:T(1024)S(1)}, u32[]{:S(2)}) copy-start(f32[768]{0:T(1024)S(1)} %get-tuple-element.349) | copy-start | bytes 9220
  34.3 234.8 %copy-start.41 = (f32[768]{0:T(1024)}, f32[768]{0:T(1024)S(1)}, u32[]{:S(2)}) copy-start(f32[768]{0:T(1024)S(1)} %get-tuple-element.344) | copy-start | bytes 9220
  205.1 388.8 %copy-start.3 = (f32[256,768]{1,0:T(8,128)}, f32[256,768]{1,0:T(8,128)S(1)}, u32[]{:S(2)}) copy-start(f32[256,768]{1,0:T(8,128)S(1)} %get-tuple-element.472) | copy-start | bytes 2359300
  205.3 69.2 %copy-start.70 = (f32[256]{0:T(256)}, f32[256]{0:T(256)S(1)}, u32[]{:S(2)}) copy-start(f32[256]{0:T(256)S(1)} %multiply_reduce_fusion.10) | copy-start | bytes 3076
  205.3 69.1 %copy-start.64 = (f32[256]{0:T(256)}, f32[256]{0:T(256)S(1)}, u32[]{:S(2)}) copy-start(f32[256]{0:T(256)S(1)} %fusion.96) | copy-start | bytes 3076
  628.1 343.0 %reduce-scatter.14.cloned.1.call-start = ((), (), s32[]{:S(2)}) async-start(), calls=%async_computation.17 | async-start | bytes 1622016 | tf_op jit(solution)/shard_map/reduce_scatter | solution.py:394
  641.2 336.9 %reduce-scatter.6.cloned.1.call-start = ((), (), s32[]{:S(2)}) async-start(), calls=%async_computation.13 | async-start | bytes 3649536 | tf_op jit(solution)/shard_map/reduce_scatter | solution.py:394
  649.9 421.5 %reduce-scatter.10.cloned.1.call-start = ((), (), s32[]{:S(2)}) async-start(), calls=%async_computation.15 | async-start | bytes 4866048 | tf_op jit(solution)/shard_map/reduce_scatter | solution.py:394
  696.2 8.4 collective-permute-start
  700.0 483.8 %reduce-scatter.12.cloned.1.call-start = ((), (), s32[]{:S(2)}) async-start(), calls=%async_computation.16 | async-start | bytes 4866048 | tf_op jit(solution)/shard_map/reduce_scatter | solution.py:394
  713.1 222.4 %collective-permute-start.1 = (bf16[3152,768]{1,0:T(8,128)(2,1)}, bf16[3152,768]{1,0:T(8,128)(2,1)}, u32[]{:S(2)}, u32[]{:S(2)}) collective-permute-start(bf16[3152,768]{1,0:T(8,128)(2,1)} %fusion.21), channel_id=1, source_target_pairs={{0,2},{1,3},{2,0},{3,1},{4,6},{5,7},{6,4},{7,5},{8,10},{9,11},{10,... | collective-permute-start | bytes 14524424 | tf_op jit(solution)/shard_map/ppermute | solution.py:104
  721.0 138.5 %copy-start.34 = (bf16[256,768]{1,0:T(8,128)(2,1)S(1)}, bf16[256,768]{1,0:T(8,128)(2,1)}, u32[]{:S(2)}) copy-start(bf16[256,768]{1,0:T(8,128)(2,1)} %copy-done.33) | copy-start | bytes 1179652
  865.9 55.7 %copy-start.13 = (bf16[32,64,768]{2,1,0:T(8,128)(2,1)S(1)}, bf16[32,64,768]{2,1,0:T(8,128)(2,1)}, u32[]{:S(2)}) copy-start(bf16[32,64,768]{2,1,0:T(8,128)(2,1)} %shard_map.421) | copy-start | bytes 9437188
  961.2 264.4 %collective-permute-start.2 = (bf16[3152,768]{1,0:T(8,128)(2,1)}, bf16[3152,768]{1,0:T(8,128)(2,1)}, u32[]{:S(2)}, u32[]{:S(2)}) collective-permute-start(bf16[3152,768]{1,0:T(8,128)(2,1)} %get-tuple-element.447), channel_id=1, source_target_pairs={{0,1},{1,0},{2,3},{3,2},{4,5},{5,4},{6,7},{7,6},{8,9},{9,8},{10,11... | collective-permute-start | bytes 14524424 | tf_op jit(solution)/shard_map/ppermute | solution.py:104
  978.2 237.4 %copy-start.29 = (f32[128,768]{1,0:T(8,128)S(1)}, f32[128,768]{1,0:T(8,128)}, u32[]{:S(2)}) copy-start(f32[128,768]{1,0:T(8,128)} %param.36) | copy-start | bytes 1179652
  1080.8 137.1 %copy-start.19 = (f32[384,768]{1,0:T(8,128)S(1)}, f32[384,768]{1,0:T(8,128)}, u32[]{:S(2)}) copy-start(f32[384,768]{1,0:T(8,128)} %param.34) | copy-start | bytes 3538948
  (81 other events, 637.2 us)
Sparse Core Ops, SparseCore 0:
  11.5 60.4 all-gather.5
  75.4 71.2 all-gather.7
  150.2 52.8 all-gather.9
  206.4 62.5 all-gather.11
  272.3 62.4 all-gather.13
  628.2 113.1 reduce-scatter.7
  746.6 105.3 reduce-scatter.13
  857.4 102.0 reduce-scatter.5
  965.5 105.8 reduce-scatter.9
  1077.7 106.0 reduce-scatter.11

commit v2 on v1

--- a/solution.py
+++ b/solution.py
@@ -22,6 +22,7 @@
 bf16 = jnp.bfloat16
 i32 = jnp.int32
 HBM = pl.BlockSpec(memory_space=pl.ANY)
+VMEM = pl.BlockSpec(memory_space=pltpu.VMEM)
 MESH = pl.DeviceIdType.MESH
 
 
@@ -98,10 +99,420 @@
     )(x)
 
 
-def flip(x, axis, span):
-    count = lax.axis_size(axis)
-    pairs = [(at, at // (2 * span) * 2 * span + (at + span) % (2 * span)) for at in range(count)]
+def from_peer(x, axis, span, size, step):
+    pairs = []
+    for at in range(lax.axis_size(axis)):
+        digit = at // span % size
+        pairs.append((at, at + ((digit + step) % size - digit) * span))
     return lax.ppermute(x, axis, pairs)
+
+
+def group_sum(x, dim, axis, span):
+    size = x.shape[dim]
+    at = lax.rem(lax.axis_index(axis) // span, size)
+    total = lax.dynamic_index_in_dim(x, at, dim, False).astype(f32)
+    for step in range(1, size):
+        block = lax.dynamic_index_in_dim(x, lax.rem(at + step, size), dim, False)
+        total = total + from_peer(block, axis, span, size, step).astype(f32)
+    return total.astype(bf16)
+
+
+def group_join(x, dim, axis, span, size):
+    at = lax.rem(lax.axis_index(axis) // span, size)
+    parts = [x] + [from_peer(x, axis, span, size, size - step) for step in range(1, size)]
+    if size == 2:
+        first = jnp.where(at == 0, parts[0], parts[1])
+        second = jnp.where(at == 0, parts[1], parts[0])
+        return jnp.stack([first, second], axis=dim)
+    turned = jnp.stack(parts + parts, axis=dim)
+    return lax.dynamic_slice_in_dim(turned, size - at, size, dim)
+
+
+def settle(grads, given, vector, n_x, n_y, n_z, call_id):
+    n_dp, _, _, chunks, height, width = grads.shape
+    n_seq = 2 * n_x
+    count = n_dp * n_seq
+    near = n_dp * 2
+    n_most = max(n_x, n_y)
+    blocks = n_x * n_y * n_z
+
+    def body(g_ref, e_ref, v_ref, o_ref, came_ref, vec_ref, *scratch):
+        own, got, first, second, third = scratch[:5]
+        v_core, v_x, v_y, v_z = scratch[5:9]
+        core_out, core_in, core_own = scratch[9:12]
+        one_out, one_in, two_out, two_in, three_out, three_in = scratch[12:18]
+        x_out, x_in, pair_out, pair_in, last_own = scratch[18:23]
+        e_out, e_in, far_out, far_in, v_out, v_in, side_own = scratch[23:]
+        dp_at, seq_at = lax.axis_index("dp"), lax.axis_index("seq")
+        x_at, c_at = seq_at // 2, lax.rem(seq_at, 2)
+        z_at, y_at = dp_at // n_y, lax.rem(dp_at, n_y)
+        partner = {"seq": x_at * 2 + 1 - c_at}
+
+        def send(source, target, out_sem, in_sem, device):
+            copy = pltpu.make_async_remote_copy(
+                source, target, out_sem, in_sem, device_id=device, device_id_type=MESH
+            )
+            copy.start()
+            return copy
+
+        barrier = pltpu.get_barrier_semaphore()
+
+        @pl.loop(1, count)
+        def _(step):
+            seq_to = lax.rem(seq_at + lax.rem(step, n_seq), n_seq)
+            peer = {"dp": lax.rem(dp_at + step // n_seq, n_dp), "seq": seq_to}
+            pl.semaphore_signal(barrier, inc=1, device_id=peer, device_id_type=MESH)
+
+        def x_first(chunk):
+            return chunk % 2 == 0
+
+        def order(chunk):
+            return (n_x, x_at, n_y, y_at) if x_first(chunk) else (n_y, y_at, n_x, x_at)
+
+        def places(chunk, block):
+            z, y, x = block // (n_y * n_x), lax.rem(block // n_x, n_y), lax.rem(block, n_x)
+            at = (x * n_y + y) * n_z + z if x_first(chunk) else (y * n_x + x) * n_z + z
+            return z * n_y + y, x, at
+
+        for chunk in range(chunks):
+
+            @pl.loop(0, blocks)
+            def _(block):
+                owner, x, at = places(chunk, block)
+                source = g_ref.at[owner, c_at, x, chunk]
+                pltpu.make_async_copy(source, own.at[chunk, at], core_own.at[chunk]).start()
+
+        v_core[c_at] = v_ref[...]
+        mine = came_ref.at[dp_at * n_seq + seq_at]
+        side = pltpu.make_async_copy(e_ref.at[dp_at * 2 + c_at], mine, side_own)
+        side.start()
+        pl.semaphore_wait(barrier, count - 1)
+        for chunk in range(chunks):
+
+            @pl.loop(0, blocks)
+            def _(block):
+                owner, x, at = places(chunk, block)
+                source = g_ref.at[owner, 1 - c_at, x, chunk]
+                send(source, got.at[chunk, at], core_out.at[chunk], core_in.at[chunk], partner)
+
+        v_turn = [
+            (v_core, c_at, 2, lambda to: {"seq": x_at * 2 + to}),
+            (v_x, x_at, n_x, lambda to: {"seq": to * 2 + c_at}),
+            (v_y, y_at, n_y, lambda to: {"dp": z_at * n_y + to}),
+            (v_z, z_at, n_z, lambda to: {"dp": to * n_y + y_at}),
+        ]
+
+        def vector_out(turn):
+            buffer, at, size, device = v_turn[turn]
+            return [
+                send(
+                    buffer.at[at],
+                    buffer.at[at],
+                    v_out.at[turn, step - 1],
+                    v_in.at[turn, step - 1],
+                    device(lax.rem(at + step, size)),
+                )
+                for step in range(1, size)
+            ]
+
+        def vector_sum(turn, copies):
+            buffer, _, size, _ = v_turn[turn]
+            for copy in copies:
+                copy.wait()
+            total = buffer[0]
+            for place in range(1, size):
+                total = total + buffer[place]
+            return total
+
+        v_copies = vector_out(0)
+
+        def near_copy(step):
+            owner = lax.rem(dp_at + step // 2, n_dp)
+            core = lax.rem(c_at + lax.rem(step, 2), 2)
+            return pltpu.make_async_remote_copy(
+                e_ref.at[owner * 2 + core],
+                mine,
+                e_out.at[step],
+                e_in.at[step],
+                device_id={"dp": owner, "seq": x_at * 2 + core},
+                device_id_type=MESH,
+            )
+
+        def far_copy(step, turn):
+            origin = lax.rem(dp_at + n_dp - step // 2, n_dp)
+            core = lax.rem(c_at + lax.rem(step, 2), 2)
+            block = came_ref.at[origin * n_seq + x_at * 2 + core]
+            to = lax.rem(x_at + turn, n_x) * 2 + c_at
+            return pltpu.make_async_remote_copy(
+                block,
+                block,
+                far_out.at[step, turn - 1],
+                far_in.at[step, turn - 1],
+                device_id={"seq": to},
+                device_id_type=MESH,
+            )
+
+        @pl.loop(1, near)
+        def _(step):
+            near_copy(step).start()
+
+        kept = {}
+        for chunk in range(chunks):
+            n_first, at_first, n_second, at_second = order(chunk)
+            span = n_second * n_z
+            whole = own.at[chunk]
+            pltpu.make_async_copy(whole, whole, core_own.at[chunk]).wait()
+            pltpu.make_async_remote_copy(
+                whole, whole, core_out.at[chunk], core_in.at[chunk], device_id=partner, device_id_type=MESH
+            ).wait()
+
+            @pl.loop(0, blocks)
+            def _(block):
+                total = own[chunk, block].astype(f32) + got[chunk, block].astype(f32)
+                own[chunk, block] = total.astype(bf16)
+
+            for step in range(1, n_first):
+                to = lax.rem(at_first + step, n_first)
+                if x_first(chunk):
+                    device = {"seq": to * 2 + c_at}
+                else:
+                    device = {"dp": z_at * n_y + to}
+                copy = send(
+                    own.at[chunk, pl.ds(to * span, span)],
+                    first.at[chunk, step - 1, pl.ds(0, span)],
+                    one_out.at[chunk, step - 1],
+                    one_in.at[chunk, step - 1],
+                    device,
+                )
+                kept[1, chunk, step] = copy
+        v_x[x_at] = vector_sum(0, v_copies)
+        v_copies = vector_out(1)
+        side.wait()
+        for turn in range(1, n_x):
+            far_copy(0, turn).start()
+        for chunk in range(chunks):
+            n_first, at_first, n_second, at_second = order(chunk)
+            span = n_second * n_z
+            for step in range(1, n_first):
+                kept[1, chunk, step].wait_recv()
+            base = at_first * span
+
+            @pl.loop(0, span)
+            def _(block):
+                total = own[chunk, base + block].astype(f32)
+                for step in range(1, n_first):
+                    total = total + first[chunk, step - 1, block].astype(f32)
+                own[chunk, base + block] = total.astype(bf16)
+
+            for step in range(1, n_second):
+                to = lax.rem(at_second + step, n_second)
+                if x_first(chunk):
+                    device = {"dp": z_at * n_y + to}
+                else:
+                    device = {"seq": to * 2 + c_at}
+                kept[2, chunk, step] = send(
+                    own.at[chunk, pl.ds(base + to * n_z, n_z)],
+                    second.at[chunk, step - 1],
+                    two_out.at[chunk, step - 1],
+                    two_in.at[chunk, step - 1],
+                    device,
+                )
+            if chunk == 0:
+                v_y[y_at] = vector_sum(1, v_copies)
+                v_copies = vector_out(2)
+
+                @pl.loop(1, near)
+                def _(step):
+                    near_copy(step).wait()
+                    for turn in range(1, n_x):
+                        far_copy(step, turn).start()
+
+        v_z[z_at] = vector_sum(2, v_copies)
+        v_copies = vector_out(3)
+        for chunk in range(chunks):
+            n_first, at_first, n_second, at_second = order(chunk)
+            for step in range(1, n_second):
+                kept[2, chunk, step].wait_recv()
+            base = (at_first * n_second + at_second) * n_z
+
+            @pl.loop(0, n_z)
+            def _(block):
+                total = own[chunk, base + block].astype(f32)
+                for step in range(1, n_second):
+                    total = total + second[chunk, step - 1, block].astype(f32)
+                own[chunk, base + block] = total.astype(bf16)
+
+            for step in range(1, n_z):
+                to = lax.rem(z_at + step, n_z)
+                kept[3, chunk, step] = send(
+                    own.at[chunk, base + to],
+                    third.at[chunk, step - 1],
+                    three_out.at[chunk, step - 1],
+                    three_in.at[chunk, step - 1],
+                    {"dp": to * n_y + y_at},
+                )
+        vec_ref[...] = vector_sum(3, v_copies)
+        for chunk in range(chunks):
+            n_first, at_first, n_second, at_second = order(chunk)
+            for step in range(1, n_z):
+                kept[3, chunk, step].wait_recv()
+            here = (at_first * n_second + at_second) * n_z + z_at
+            total = own[chunk, here].astype(f32)
+            for step in range(1, n_z):
+                total = total + third[chunk, step - 1].astype(f32)
+            own[chunk, here] = total.astype(bf16)
+            result = o_ref.at[c_at, x_at, chunk]
+            copy = pltpu.make_async_copy(own.at[chunk, here], result, last_own.at[chunk])
+            copy.start()
+            kept[0, chunk] = copy
+            for step in range(1, n_x):
+                to = lax.rem(x_at + step, n_x)
+                kept[4, chunk, step] = send(
+                    own.at[chunk, here],
+                    result,
+                    x_out.at[chunk, step - 1],
+                    x_in.at[chunk, step - 1],
+                    {"seq": to * 2 + c_at},
+                )
+            kept[5, chunk, 0] = send(
+                own.at[chunk, here], result, pair_out.at[chunk, 0], pair_in.at[chunk, 0], partner
+            )
+        for chunk in range(chunks):
+            for step in range(1, n_x):
+                kept[4, chunk, step].wait_recv()
+                origin = lax.rem(x_at + n_x - step, n_x)
+                piece = o_ref.at[c_at, origin, chunk]
+                kept[5, chunk, step] = send(
+                    piece, piece, pair_out.at[chunk, step], pair_in.at[chunk, step], partner
+                )
+
+        @pl.loop(0, near)
+        def _(step):
+            for turn in range(1, n_x):
+                far_copy(step, turn).wait()
+
+        for chunk in range(chunks):
+            kept[0, chunk].wait()
+            for step in range(n_x):
+                kept[5, chunk, step].wait()
+        for key, copy in kept.items():
+            if 1 <= key[0] <= 4:
+                copy.wait_send()
+
+    def dma(*shape):
+        return pltpu.SemaphoreType.DMA(shape)
+
+    most = n_most * n_z
+    return pl.pallas_call(
+        body,
+        out_shape=(
+            jax.ShapeDtypeStruct((2, n_x, chunks, height, width), bf16),
+            jax.ShapeDtypeStruct((count,) + given.shape[1:], given.dtype),
+            jax.ShapeDtypeStruct(vector.shape, vector.dtype),
+        ),
+        in_specs=[HBM, HBM, VMEM],
+        out_specs=(HBM, HBM, VMEM),
+        scratch_shapes=[
+            pltpu.VMEM((chunks, blocks, height, width), bf16),
+            pltpu.VMEM((chunks, blocks, height, width), bf16),
+            pltpu.VMEM((chunks, n_most - 1, most, height, width), bf16),
+            pltpu.VMEM((chunks, n_most - 1, n_z, height, width), bf16),
+            pltpu.VMEM((chunks, n_z - 1, height, width), bf16),
+            pltpu.VMEM((2,) + vector.shape, f32),
+            pltpu.VMEM((n_x,) + vector.shape, f32),
+            pltpu.VMEM((n_y,) + vector.shape, f32),
+            pltpu.VMEM((n_z,) + vector.shape, f32),
+            dma(chunks),
+            dma(chunks),
+            dma(chunks),
+            dma(chunks, n_most - 1),
+            dma(chunks, n_most - 1),
+            dma(chunks, n_most - 1),
+            dma(chunks, n_most - 1),
+            dma(chunks, n_z - 1),
+            dma(chunks, n_z - 1),
+            dma(chunks, n_x - 1),
+            dma(chunks, n_x - 1),
+            dma(chunks, n_x),
+            dma(chunks, n_x),
+            dma(chunks),
+            dma(near),
+            dma(near),
+            dma(near, n_x - 1),
+            dma(near, n_x - 1),
+            dma(4, max(n_most, n_z) - 1),
+            dma(4, max(n_most, n_z) - 1),
+            pltpu.SemaphoreType.DMA,
+        ],
+        compiler_params=pltpu.CompilerParams(
+            collective_id=call_id, has_side_effects=True, vmem_limit_bytes=48 << 20
+        ),
+    )(grads, given, vector)
+
+
+def close_half(own, other, names, values, tile):
+    half, width = own.shape
+    count = names.shape[1]
+
+    def body(own_ref, other_ref, names_ref, values_ref, o_ref, square_ref):
+        step = pl.program_id(0)
+        row = lax.broadcasted_iota(i32, (tile, count), 0) + step * tile
+        where = jnp.where(row == names_ref[...], 1.0, 0.0).astype(bf16)
+        total = own_ref[...].astype(f32) + other_ref[...].astype(f32)
+        total = total + jnp.dot(where, values_ref[...], preferred_element_type=f32)
+        o_ref[...] = total.astype(bf16)
+
+        @pl.when(step == 0)
+        def _():
+            square_ref[...] = jnp.zeros_like(square_ref)
+
+        square_ref[...] += jnp.sum(total * total, axis=0, keepdims=True)
+
+    rows = pl.BlockSpec((tile, width), lambda step: (step, 0))
+    return pl.pallas_call(
+        body,
+        grid=(half // tile,),
+        in_specs=[
+            rows,
+            rows,
+            pl.BlockSpec((1, count), lambda step: (0, 0)),
+            pl.BlockSpec((count, width), lambda step: (0, 0)),
+        ],
+        out_specs=(rows, pl.BlockSpec((1, width), lambda step: (0, 0))),
+        out_shape=(jax.ShapeDtypeStruct((half, width), bf16), jax.ShapeDtypeStruct((1, width), f32)),
+        compiler_params=pltpu.CompilerParams(vmem_limit_bytes=48 << 20),
+    )(own, other, names, values)
+
+
+def adam_table(core, factor, weight, first, second, mine, other, tile):
+    size, width = weight.shape
+    turns = mine.shape[0] // tile
+
+    def body(core_ref, factor_ref, w_ref, m_ref, v_ref, mine_ref, other_ref, new_w, new_m, new_v):
+        from_mine = pl.program_id(0) // turns == core_ref[0]
+        grad = jnp.where(from_mine, mine_ref[...], other_ref[...]).astype(f32) * factor_ref[0]
+        new_w[...], new_m[...], new_v[...] = adam_update(
+            w_ref[...], grad, m_ref[...], v_ref[...], 0.1, 0.1
+        )
+
+    def mine_at(step, core_ref, factor_ref):
+        return (jnp.clip(step - core_ref[0] * turns, 0, turns - 1), 0)
+
+    def other_at(step, core_ref, factor_ref):
+        return (jnp.clip(step - (1 - core_ref[0]) * turns, 0, turns - 1), 0)
+
+    rows = pl.BlockSpec((tile, width), lambda step, core_ref, factor_ref: (step, 0))
+    return pl.pallas_call(
+        body,
+        grid_spec=pltpu.PrefetchScalarGridSpec(
+            num_scalar_prefetch=2,
+            grid=(pl.cdiv(size, tile),),
+            in_specs=[rows, rows, rows, pl.BlockSpec((tile, width), mine_at), pl.BlockSpec((tile, width), other_at)],
+            out_specs=(rows, rows, rows),
+        ),
+        out_shape=(jax.ShapeDtypeStruct((size, width), f32),) * 3,
+        compiler_params=pltpu.CompilerParams(vmem_limit_bytes=56 << 20),
+    )(core.reshape(1), factor.reshape(1), weight, first, second, mine, other)
 
 
 def layer_norm(x, gain, shift):
@@ -170,18 +581,40 @@
     n_pick = masked.shape[1] // sharers
     row_at = seq_at // sharers
     share = lax.rem(seq_at, sharers)
-    half = -(-vocab_part // 32) * 16
-
-    def gathered(weight):
+    tiles = -(-vocab_part // 1056)
+    tile = -(-vocab_part // (32 * tiles)) * 16
+    half = tiles * tile
+    n_x = n_seq // 2
+    n_y = 1 << (n_dp.bit_length() - 1) // 2
+    n_z = n_dp // n_y
+
+    def piece_of(weight):
         piece = weight.shape[0] // n_seq
-        part = lax.dynamic_slice_in_dim(weight, seq_at * piece, piece, 0).astype(bf16)
-        return lax.all_gather(part, ("dp", "seq"), axis=0, tiled=True)
-
-    pos_all = gathered(positions)
-    w_in = gathered(attn_in)
-    w_out = gathered(attn_out)
-    w_up = gathered(mlp_in)
-    w_down = gathered(mlp_out)
+        return lax.dynamic_slice_in_dim(weight, seq_at * piece, piece, 0).astype(bf16)
+
+    thin = attn_in.shape[0] // n_seq
+    hidden = mlp_in.shape[1]
+
+    def blocks_of(piece):
+        return [piece[:, at : at + model] for at in range(0, piece.shape[1], model)]
+
+    pieces = [piece_of(mlp_out), piece_of(positions)]
+    for weight in (attn_in, attn_out, mlp_in):
+        pieces += blocks_of(piece_of(weight))
+    ends = [0]
+    for piece in pieces:
+        ends.append(ends[-1] + piece.shape[0])
+    packed = lax.all_gather(jnp.concatenate(pieces), ("dp", "seq"))
+
+    def unpacked(begin, count):
+        parts = [packed[:, ends[at] : ends[at + 1]].reshape(-1, model) for at in range(begin, begin + count)]
+        return parts[0] if count == 1 else jnp.concatenate(parts, axis=1)
+
+    w_down = unpacked(0, 1)
+    pos_all = unpacked(1, 1)
+    w_in = unpacked(2, 3)
+    w_out = unpacked(5, 1)
+    w_up = unpacked(6, hidden // model)
 
     all_rows = deliver(clean_ids, ("seq",), 1)
     row_ids = lax.dynamic_index_in_dim(all_rows, row_at, 1, keepdims=False).reshape(length)
@@ -282,7 +715,7 @@
     sources = final_normed.astype(bf16)
 
     table_low = table.astype(bf16)
-    heads = deliver(sources, ("dp",), 4).reshape(n_dp * n_pick, model)
+    heads = deliver(sources, ("dp",), 9).reshape(n_dp * n_pick, model)
     logits = jnp.einsum("nd,vd->nv", heads, table_low, preferred_element_type=f32)
     flat_targets = all_targets.reshape(-1) - dp_at * vocab_part
     rows_here = valid_all.reshape(n_dp, rows, sharers, n_pick)
@@ -302,21 +735,26 @@
         (flat_valid / masked_count)[:, None]
         * (jnp.exp(logits - log_norm[:, None]) - hit_mask.astype(f32))
     ).astype(bf16)
-    heads_grad = jnp.dot(logit_grad, table_low, preferred_element_type=f32)
-    final_grad = deliver(
-        heads_grad.astype(bf16).reshape(n_dp, n_pick, model), ("dp",), 6, lambda place: place[0]
-    )
-    final_grad = jnp.sum(final_grad.astype(f32), axis=0)
     table_grad = jnp.einsum("nv,nd->vd", logit_grad, heads, preferred_element_type=f32)
     table_grad = jnp.pad(table_grad, ((0, 2 * half - vocab_part), (0, 0)))
     half_own = lax.dynamic_slice_in_dim(table_grad, core * half, half, 0)
     half_other = lax.dynamic_slice_in_dim(table_grad, (1 - core) * half, half, 0).astype(bf16)
-    half_low = (half_own + flip(half_other, "seq", 1).astype(f32)).astype(bf16)
-    if n_seq == 4:
-        half_sum = half_low.astype(f32) + flip(half_low, "seq", 2).astype(f32)
+    logit_grad, half_other = lax.optimization_barrier((logit_grad, half_other))
+    half_low = (half_own + from_peer(half_other, "seq", 1, 2, 1).astype(f32)).astype(bf16)
+    heads_grad = jnp.dot(logit_grad, table_low, preferred_element_type=f32).astype(bf16)
+    heads_grad, half_low = lax.optimization_barrier((heads_grad, half_low))
+    if n_x == 2:
+        half_across = from_peer(half_low, "seq", 2, 2, 1)
     else:
         groups = [list(range(at, n_seq, 2)) for at in range(2)]
-        half_sum = jnp.sum(lax.all_gather(half_low, "seq", axis_index_groups=groups).astype(f32), axis=0)
+        half_low = jnp.sum(lax.all_gather(half_low, "seq", axis_index_groups=groups).astype(f32), axis=0)
+        half_across = jnp.zeros_like(half_low)
+    final_grad = heads_grad.reshape(n_dp, n_pick, model)
+    final_own = lax.dynamic_index_in_dim(final_grad, dp_at, 0, False).astype(f32)
+    for step in range(1, n_dp):
+        block = lax.dynamic_index_in_dim(final_grad, lax.rem(dp_at + step, n_dp), 0, False)
+        final_own = final_own + from_peer(block, "dp", 1, n_dp, step).astype(f32)
+    final_grad = final_own
 
     final_in_grad, gain_end, shift_end = norm_end_back(final_grad)
     down_grad = final_in_grad.astype(bf16)
@@ -366,39 +804,6 @@
         )
         return summed_ids.astype(bf16).reshape(2 * n_dp, GIVE, model)
 
-    def taken(names, values):
-        names = names.reshape(1, -1)
-        where = (jnp.arange(half, dtype=i32)[:, None] == names).astype(bf16)
-        return jnp.dot(where, values.reshape(-1, model), preferred_element_type=f32)
-
-    came = deliver(
-        given(spot_half), ("dp", "seq"), 7, lambda place: place[0] * 2 + lax.rem(place[1], 2)
-    )
-    half_sum = half_sum + taken(asks_half, came)
-
-    def give_more(state):
-        turn, total = state
-        next_spot, next_ask = asked(owner_half, place_half, within_half, 2 * n_dp, GIVE, turn)
-        names = lax.all_gather(next_ask.reshape(2 * n_dp, GIVE), ("dp", "seq"))
-        names = lax.dynamic_index_in_dim(names, half_at, 1, False)
-        sent = given(next_spot).reshape(n_dp, 1, 2, GIVE, model)
-        sent = jnp.broadcast_to(sent, (n_dp, n_seq // 2, 2, GIVE, model)).reshape(-1, GIVE, model)
-        got = lax.all_to_all(sent, ("dp", "seq"), 0, 0)
-        return turn + 1, total + taken(names, got)
-
-    _, half_sum = lax.while_loop(lambda state: state[0] < turns[1], give_more, (jnp.int32(1), half_sum))
-
-    def spread_sum(grad):
-        pieces = grad.reshape(n_dp, n_seq, -1, grad.shape[1]).astype(bf16)
-        pieces = pieces.reshape(-1, grad.shape[1])
-        part = lax.psum_scatter(pieces, ("dp", "seq"), scatter_dimension=0, tiled=True)
-        return lax.all_gather(part, "seq", axis=0, tiled=True).astype(f32)
-
-    g_down = spread_sum(w_down_grad)
-    g_up = spread_sum(w_up_grad)
-    g_out = spread_sum(w_out_grad)
-    g_in = spread_sum(w_in_grad)
-    g_pos = spread_sum(start_grad)
     vec_grad = jnp.concatenate(
         [
             jnp.stack(
@@ -416,33 +821,61 @@
                 ]
             ),
             up_bias.reshape(-1, model),
+            jnp.full((1, model), loss_group),
+            jnp.zeros((1, model), f32),
         ],
         axis=0,
     )
-    vec_total = lax.psum(vec_grad, ("dp", "seq"))
-    half_square = jnp.sum(half_sum * half_sum)
-    half_low = half_sum.astype(bf16)
-    half_pair = flip(half_low, "seq", 1)
-    table_sum = jnp.where(
-        core == 0, jnp.concatenate([half_low, half_pair]), jnp.concatenate([half_pair, half_low])
-    )[:vocab_part].astype(f32)
-    layer_grads = (g_in, g_out, g_up, g_down, g_pos)
-    layer_square = sum(jnp.sum(g * g) for g in layer_grads)
-    said = jnp.concatenate(
-        [
-            jnp.full((1, 128), half_square),
-            jnp.full((1, 128), layer_square),
-            jnp.full((1, 128), loss_group),
-            jnp.zeros((5, 128), f32),
-        ]
+
+    def columns(grad):
+        return [part.astype(bf16).reshape(n_dp, -1, model) for part in blocks_of(grad)]
+
+    layer_parts = [w_down_grad, start_grad, w_in_grad, w_out_grad, w_up_grad]
+    whole = jnp.concatenate([part for grad in layer_parts for part in columns(grad)], axis=1)
+    chunks = 4
+    layer_sum, came, vec_total = settle(
+        whole.reshape(n_dp, 2, n_x, chunks, -1, model), given(spot_half), vec_grad, n_x, n_y, n_z, 7
     )
-    said = deliver(said, ("dp", "seq"), 8)[:, :3, 0].reshape(n_dp, n_seq, 3)
-    square_total = jnp.sum(said[:, :2, 0]) + jnp.sum(said[:, 0, 1])
-    loss_sum = jnp.sum(said[0, :, 2])
+    def give_more(state):
+        turn, total, _ = state
+        next_spot, next_ask = asked(owner_half, place_half, within_half, 2 * n_dp, GIVE, turn)
+        names = lax.all_gather(next_ask.reshape(2 * n_dp, GIVE), ("dp", "seq"))
+        names = lax.dynamic_index_in_dim(names, half_at, 1, False).reshape(1, -1)
+        sent = given(next_spot).reshape(n_dp, 1, 2, GIVE, model)
+        sent = jnp.broadcast_to(sent, (n_dp, n_x, 2, GIVE, model)).reshape(-1, GIVE, model)
+        got = lax.all_to_all(sent, ("dp", "seq"), 0, 0).reshape(-1, model)
+        total, squares = close_half(total, jnp.zeros_like(total), names, got, tile)
+        return turn + 1, total, jnp.sum(squares)
+
+    names = asks_half.reshape(1, -1)
+    values = came.reshape(-1, model)
+    half_own, squares_own = close_half(half_low, half_across, names, values, tile)
+    half_square = jnp.sum(squares_own)
+
+    _, half_own, half_square = lax.while_loop(
+        lambda state: state[0] < turns[1], give_more, (jnp.int32(1), half_own, half_square)
+    )
+    layer_sum = layer_sum.reshape(-1, model).astype(f32)
+    layer_square = jnp.sum(layer_sum * layer_sum)
+    loss_sum = vec_total[14, 0] / n_dp
+    vec_total = vec_total[:14]
+
+    def side_by_side(rows_of, count):
+        return jnp.concatenate(jnp.split(rows_of, count, axis=0), axis=1)
+
+    ends = [0]
+    for grad in layer_parts:
+        ends.append(ends[-1] + grad.shape[0] * grad.shape[1] // (model * n_dp))
+    g_down, g_pos, g_in, g_out, g_up = [layer_sum[begin:end] for begin, end in zip(ends, ends[1:])]
+    g_in = side_by_side(g_in, 3)
+    g_up = side_by_side(g_up, hidden // model)
+    half_other = from_peer(half_own, "seq", 1, 2, 1)
+    said = jnp.full((8, 128), half_square / n_x + layer_square / n_seq)
+    square_total = jnp.sum(deliver(said, ("dp", "seq"), 8)[:, 0, 0])
     grad_norm = jnp.sqrt(square_total + jnp.sum(vec_total * vec_total))
     factor = clip_at / jnp.maximum(grad_norm, clip_at)
     weights = (attn_in, attn_out, mlp_in, mlp_out, table, positions, vectors)
-    all_grads = (g_in, g_out, g_up, g_down, table_sum, g_pos, vec_total)
+    all_grads = (g_in, g_out, g_up, g_down, None, g_pos, vec_total)
     firsts = (
         first_attn_in,
         first_attn_out,
@@ -464,9 +897,14 @@
     news, moments, squares = ([], [], [])
     for index in range(7):
         rate, decay = (1.0, 0.0) if index == 6 else (0.1, 0.1)
-        new_w, new_m, new_v = adam_update(
-            weights[index], all_grads[index] * factor, firsts[index], seconds[index], rate, decay
-        )
+        if index == 4:
+            new_w, new_m, new_v = adam_table(
+                core, factor, table, first_table, second_table, half_own, half_other, tile
+            )
+        else:
+            new_w, new_m, new_v = adam_update(
+                weights[index], all_grads[index] * factor, firsts[index], seconds[index], rate, decay
+            )
         news.append(new_w)
         moments.append(new_m)
         squares.append(new_v)

time: 1290 us -> 871 us (0.68)
  waiting for transfers between devices: 366 us -> 63.9 us
  blocking collectives: 93.5 us -> 0 us
  matrix products: 224 us -> 158 us
  other arithmetic: 178 us -> 134 us
  Pallas kernels: 331 us -> 366 us
  local copies, waits for them, and re-layouts: 57.5 us -> 86.6 us
  starting transfers between devices: 1.53 us -> 24.5 us
    pallas_call x0 -> x3, Pallas kernels: none -> 197 us  [the longest x1 136 us: settle(): pl.pallas_call(body, out_shape=(jax.ShapeDtypeStruct((2, n_x, chunks, hei...]
    reduce_scatter x5 -> x0, waiting for transfers between devices: 187 us -> none  [spread_sum(): lax.psum_scatter(pieces, ('dp', 'seq'), scatter_dimension=0, tiled=True)]
    pallas_call x8 -> x6, Pallas kernels: 331 us -> 170 us  [deliver(): pl.pallas_call(body, out_shape=jax.ShapeDtypeStruct((count,) + block, x.d...]
    all_gather x5 -> x1, waiting for transfers between devices: 175 us -> 14.9 us  [on_device(): packed = lax.all_gather(jnp.concatenate(pieces), ('dp', 'seq'))]
    psum x1 -> x0, blocking collectives: 55.6 us -> none  [on_device(): vec_total = lax.psum(vec_grad, ('dp', 'seq'))]
    sub x7 -> x6, other arithmetic: 59.7 us -> 14.7 us  [adam_update(): weight - rate * (mhat / (jnp.sqrt(vhat) + adam_eps) + decay * weight)]
    ppermute x3 -> x10, waiting for transfers between devices: 4.11 us -> 49.1 us  [from_peer(): return lax.ppermute(x, axis, pairs)]
    all_gather x5 -> x0, blocking collectives: 37.9 us -> none  [spread_sum(): return lax.all_gather(part, 'seq', axis=0, tiled=True).astype(f32)]
  transfers between devices with their start and end apart: 13 -> 11, of which waited for: 7 -> 4; matrix products, arithmetic and copies ran while one was open for 19% -> 21% of each run, Pallas kernels for 15% -> 26%
where the time goes in v2:
time: 871 us; the launch traced here: 862 us
  Pallas kernels  366 us (42%)
  matrix products  158 us (18%)
  other arithmetic  134 us (15%)
  local copies, waits for them, and re-layouts  86.6 us (10%)
  waiting for transfers between devices  63.9 us (7%)
  between operations  26.5 us (3%)
  starting transfers between devices  24.5 us (3%)
    pallas_call x6, Pallas kernels, deliver(): pl.pallas_call(body, out_shape=jax.ShapeDtypeStruct((count,) + block, x.d...  170 us
    pallas_call x1, Pallas kernels, settle(): pl.pallas_call(body, out_shape=(jax.ShapeDtypeStruct((2, n_x, chunks, hei...  136 us
    ppermute x10, waiting for transfers between devices, from_peer(): return lax.ppermute(x, axis, pairs)  49.1 us
    pallas_call x1, Pallas kernels, adam_table(): pl.pallas_call(body, grid_spec=pltpu.PrefetchScalarGridSpec(num_scalar_pr...  46.9 us
    dot_general x1, matrix products, on_device(): jnp.einsum('nd,vd->nv', heads, table_low, preferred_element_type=f32)  31.6 us
    unnamed x263, local copies, waits for them, and re-layouts  31.2 us
    convert_element_type x1, other arithmetic, on_device(): logit_grad = ((flat_valid / masked_count)[:, None] * (jnp.exp(logits - lo...  26.7 us
    dot_general x1, matrix products, on_device(): jnp.einsum('nv,nd->vd', logit_grad, heads, preferred_element_type=f32)  26.3 us
  transfers between devices with their start and end apart: 11, of which 4 were waited for; matrix products, arithmetic and copies ran while one was open for 21% of the time, Pallas kernels for 26%

profile of v2, /device:TPU:0, one launch (start us, length us, event | category | flops | bytes accessed | tf_op | source)
XLA Modules:
  0.0 861.6 jit_solution(17373328930074524932)
XLA Ops:
  38.0 24.3 %shard_map.416 = s32[32,32,128]{2,1,0:T(8,128)} custom-call(s32[32,128]{1,0:T(8,128)} %pad_add_fusion.x_ref), custom_call_target="tpu_custom_call" | custom-call | tf_op jit(solution)/shard_map/pallas_call | solution.py:88
  64.5 11.4 %convert.38 = bf16[6288,768]{1,0:T(8,128)(2,1)} convert(f32[6288,768]{1,0:T(8,128)} %w_ref.1) | non-fusion elementwise | flops 4829184 | bytes 28975104
  75.8 9.8 %gather_fusion.1 = bf16[768,768]{1,0:T(8,128)(2,1)S(1)} fusion(f32[6288,768]{1,0:T(8,128)} %w_ref.1, s32[1024]{0:T(1024)S(1)} %pad_clamp_fusion.1), kind=kCustom, calls=%fused_computation.1 | custom fusion | bytes 2362368 | tf_op jit(solution)/shard_map/jit(_take)/gather | solution.py:674
  87.0 46.7 %shard_map.417 = bf16[8,96,768]{2,1,0:T(8,128)(2,1)} custom-call(bf16[8,96,768]{2,1,0:T(8,128)(2,1)} %select_convert_fusion.1.x_ref), custom_call_target="tpu_custom_call" | custom-call | tf_op jit(solution)/shard_map/pallas_call | solution.py:88
  140.6 14.9 %all-gather.3.cloned.1.call-done = bf16[10240,768]{1,0:T(8,128)(2,1)} async-done(((bf16[320,768]{1,0:T(8,128)(2,1)}), bf16[10240,768]{1,0:T(8,128)(2,1)}) %all-gather.3.cloned.1.call-update) | async-done | bytes 15728656 | tf_op jit(solution)/shard_map/all_gather | solution.py:607
  163.0 6.8 fusion.109
  207.2 57.0 %shard_map.418 = bf16[8,256,768]{2,1,0:T(8,128)(2,1)} custom-call(bf16[256,768]{1,0:T(8,128)(2,1)} %add_convert_fusion.3.x_ref), custom_call_target="tpu_custom_call" | custom-call | tf_op jit(solution)/shard_map/pallas_call | solution.py:88
  264.2 31.6 %fusion.120 = (f32[2048]{0:T(1024)S(1)}, f32[2048,6288]{0,1:T(8,128)}) fusion(bf16[2048,768]{1,0:T(8,128)(2,1)} %bitcast.245, f32[6288,768]{1,0:T(8,128)} %w_ref.1), kind=kOutput, calls=%fused_computation.337 | convolution fusion | flops 19798042624 | bytes 73981952 | tf_op jit(solution)/shard_map/nd,vd->nv/dot_general | solution.py:719
  295.8 22.6 %exponential_reduce_fusion = (f32[2048]{0:T(1024)S(1)}, f32[2048]{0:T(1024)S(1)}) fusion(f32[2048,6288]{0,1:T(8,128)} %get-tuple-element.540, f32[2048]{0:T(1024)S(1)} %get-tuple-element.539, s32[2048]{0:T(1024)S(1)} %bitcast.291), kind=kLoop, calls=%fused_computation.49 | loop fusion | flops 64385024 | bytes 51544064 | tf_op jit(solution)/shard_map/reduce_sum | solution.py:726
  318.9 25.1 %shard_map.419 = f32[8,3,16,128]{3,2,1,0:T(8,128)} custom-call(f32[3,16,128]{2,1,0:T(8,128)} %pad_maximum_fusion.7.x_ref), custom_call_target="tpu_custom_call" | custom-call | tf_op jit(solution)/shard_map/pallas_call | solution.py:88
  347.2 26.7 %multiply_convert_fusion = bf16[2048,6288]{0,1:T(8,128)(2,1)} fusion(f32[2048,6288]{0,1:T(8,128)} %get-tuple-element.540, f32[2048]{0:T(1024)S(1)} %get-tuple-element.460, s32[2048]{0:T(1024)S(1)} %bitcast.292, f32[2048]{0:T(1024)S(1)} %bitcast.298), kind=kLoop, calls=%fused_computation.46 | loop fusion | flops 77266944 | bytes 77291520 | tf_op jit(solution)/shard_map/convert_element_type | solution.py:737
  373.9 26.3 %fusion.121 = f32[6288,768]{1,0:T(8,128)} fusion(bf16[2048,6288]{0,1:T(8,128)(2,1)} %multiply_convert_fusion, bf16[2048,768]{1,0:T(8,128)(2,1)S(1)} %bitcast.246), kind=kOutput, calls=%fused_computation.339 | convolution fusion | flops 19780337664 | bytes 48218112 | tf_op jit(solution)/shard_map/nv,nd->vd/dot_general | solution.py:738
  406.6 25.9 %fusion.28 = bf16[2048,768]{1,0:T(8,128)(2,1)S(1)} fusion(bf16[2048,6288]{0,1:T(8,128)(2,1)} %multiply_convert_fusion, f32[6288,768]{1,0:T(8,128)} %w_ref.1), kind=kOutput, calls=%fused_computation.94 | convolution fusion | flops 19786739712 | bytes 48218112 | tf_op jit(solution)/shard_map/dot_general | solution.py:744
  432.6 9.6 %fusion.16.own_ref = bf16[3168,768]{1,0:T(8,128)(2,1)} fusion(s32[]{:T(128)S(6)} %select_n.432, f32[6288,768]{1,0:T(8,128)} %fusion.121, bf16[3168,768]{1,0:T(8,128)(2,1)} %collective-permute-done), kind=kLoop, calls=%fused_computation.59 | loop fusion | flops 7299072 | bytes 29048836 | tf_op jit(solution)/shard_map/convert_element_type | solution.py:743
  452.7 10.2 %collective-permute-done.1 = bf16[256,768]{1,0:T(8,128)(2,1)S(1)} collective-permute-done((bf16[256,768]{1,0:T(8,128)(2,1)S(1)}, bf16[256,768]{1,0:T(8,128)(2,1)S(1)}, u32[]{:S(2)}, u32[]{:S(2)}) %collective-permute-start.1) | collective-permute-done | bytes 393248 | tf_op jit(solution)/shard_map/ppermute | solution.py:107
  466.4 9.5 %collective-permute-start.2 = (bf16[256,768]{1,0:T(8,128)(2,1)S(1)}, bf16[256,768]{1,0:T(8,128)(2,1)}, u32[]{:S(2)}, u32[]{:S(2)}) collective-permute-start(bf16[256,768]{1,0:T(8,128)(2,1)S(1)} %get-tuple-element.507), channel_id=1, source_target_pairs={{0,8},{4,12},{8,16},{12,20},{16,24},{20,28},{24,0},{28,4},{1,9},{5... | collective-permute-start | bytes 1179656 | tf_op jit(solution)/shard_map/ppermute | solution.py:107
  477.8 38.6 %collective-permute-done.4 = bf16[256,768]{1,0:T(8,128)(2,1)} collective-permute-done((bf16[256,768]{1,0:T(8,128)(2,1)S(1)}, bf16[256,768]{1,0:T(8,128)(2,1)}, u32[]{:S(2)}, u32[]{:S(2)}) %collective-permute-start.4) | collective-permute-done | bytes 393248 | tf_op jit(solution)/shard_map/ppermute | solution.py:107
  534.5 8.0 convolution_convert_fusion.3
  542.4 9.6 %multiply_reduce_fusion = (f32[12,256]{1,0:T(8,128)S(1)}, f32[12,256,1024]{2,1,0:T(8,128)}) fusion(f32[12,256,1024]{2,1,0:T(8,128)} %copy-done.3, f32[12,256]{1,0:T(8,128)S(1)} %copy-done.73, pred[1024]{0:T(1024)(128)(4,1)S(1)} %copy-done.100, bf16[256,12,64]{0,2,1:T(8,128)(2,1)S(1)} %bitcast.254, bf16[1024,12,64]{0,2,1:T(8,128)(2,1)S(1)} %bitcast.226), kind=kOutput, calls=%fused_computation.53 | convolution fusion | flops 418378752 | bytes 27157504 | tf_op jit(solution)/shard_map/shd,khd->hsk/dot_general | solution.py:775
  552.1 6.7 multiply_convert_fusion.1
  608.7 135.6 %shard_map.420 = (bf16[2,2,4,80,768]{4,3,2,1,0:T(8,128)(2,1)S(1)}, bf16[32,64,768]{2,1,0:T(8,128)(2,1)}, f32[16,768]{1,0:T(8,128)S(1)}) custom-call(bf16[8,2,2,4,80,768]{5,4,3,2,1,0:T(8,128)(2,1)} %bitcast.77.g_ref, bf16[16,64,768]{2,1,0:T(8,128)(2,1)S(1)} %bitcast.206, f32[16,768]{1,0:T(8,128)S(1)} %concatenate.38.v_ref), custom_call_target="tpu_custom_call" | custom-call | tf_op jit(solution)/shard_map/pallas_call | solution.py:406
  747.5 14.3 %shard_map.421 = (bf16[3168,768]{1,0:T(8,128)(2,1)}, f32[1,768]{1,0:T(1,128)S(1)}) custom-call(bf16[3168,768]{1,0:T(8,128)(2,1)} %fusion.16.own_ref, bf16[3168,768]{1,0:T(8,128)(2,1)} %collective-permute-done.8.other_ref, s32[1,2048]{1,0:T(1,128)S(1)} %reshape.912.names_ref, bf16[2048,768]{1,0:T(8,128)(2,1)S(1)} %bitcast.205), custom_call_target="tpu_custom_call" | custom-call | tf_op jit(solution)/shard_map/pallas_call | solution.py:472
  775.2 11.4 %shard_map.422 = f32[32,8,128]{2,1,0:T(8,128)} custom-call(f32[8,128]{1,0:T(8,128)} %broadcast_in_dim.291.x_ref), custom_call_target="tpu_custom_call" | custom-call | tf_op jit(solution)/shard_map/pallas_call | solution.py:88
  805.3 46.9 %shard_map.423 = (f32[6288,768]{1,0:T(8,128)}, f32[6288,768]{1,0:T(8,128)}, f32[6288,768]{1,0:T(8,128)}) custom-call(s32[1]{0:T(128)} %bitcast.86.core_ref, f32[1]{0:T(128)} %bitcast.87.factor_ref, f32[6288,768]{1,0:T(8,128)} %w_ref.1, f32[6288,768]{1,0:T(8,128)} %m_ref.1, f32[6288,768]{1,0:T(8,128)} %v_ref.1, bf16[3168,768]{1,0:T(8,128)(2,1)S(1)} %bitcast.211, ...), custom_call_target="tpu_custom_call" | custom-call | tf_op jit(solution)/shard_map/pallas_call | solution.py:505
  (433 shorter events, 206.8 us)
Async XLA Ops:
  7.2 148.3 %all-gather.3.cloned.1.call-start = ((), (), s32[]{:S(2)}) async-start(), calls=%async_computation.3 | async-start | bytes 16220160 | tf_op jit(solution)/shard_map/all_gather | solution.py:607
  20.4 55.4 %copy-start.64 = (s32[1024]{0:T(1024)}, s32[1024]{0:T(1024)S(1)}, u32[]{:S(2)}) copy-start(s32[1024]{0:T(1024)S(1)} %get-tuple-element.746) | copy-start | bytes 12292
  24.3 51.6 %copy-start.66 = (s32[1024]{0:T(1024)}, s32[1024]{0:T(1024)S(1)}, u32[]{:S(2)}) copy-start(s32[1024]{0:T(1024)S(1)} %get-tuple-element.744) | copy-start | bytes 12292
  24.9 39.2 %copy-start.108 = (s32[1024]{0:T(1024)}, s32[1024]{0:T(1024)S(1)}, u32[]{:S(2)}) copy-start(s32[1024]{0:T(1024)S(1)} %get-tuple-element.747) | copy-start | bytes 12292
  85.7 49.2 %copy-start.68 = (f32[14,768]{1,0:T(8,128)S(1)}, f32[14,768]{1,0:T(8,128)}, u32[]{:S(2)}) copy-start(f32[14,768]{1,0:T(8,128)} %param.37) | copy-start | bytes 129028
  135.6 41.3 %copy-start.89 = (f32[768]{0:T(1024)}, f32[768]{0:T(1024)S(1)}, u32[]{:S(2)}) copy-start(f32[768]{0:T(1024)S(1)} %get-tuple-element.387) | copy-start | bytes 9220
  135.6 41.3 %copy-start.105 = (f32[768]{0:T(1024)}, f32[768]{0:T(1024)S(1)}, u32[]{:S(2)}) copy-start(f32[768]{0:T(1024)S(1)} %get-tuple-element.386) | copy-start | bytes 9220
  135.6 64.1 %copy-start.70 = (f32[768]{0:T(1024)}, f32[768]{0:T(1024)S(1)}, u32[]{:S(2)}) copy-start(f32[768]{0:T(1024)S(1)} %get-tuple-element.382) | copy-start | bytes 9220
  135.6 64.1 %copy-start.74 = (f32[768]{0:T(1024)}, f32[768]{0:T(1024)S(1)}, u32[]{:S(2)}) copy-start(f32[768]{0:T(1024)S(1)} %get-tuple-element.381) | copy-start | bytes 9220
  136.1 44.8 %copy-start.95 = (s32[256]{0:T(256)}, s32[256]{0:T(256)S(1)}, u32[]{:S(2)}) copy-start(s32[256]{0:T(256)S(1)} %broadcast_add_fusion) | copy-start | bytes 3076
  406.6 25.9 %collective-permute-start = (bf16[3168,768]{1,0:T(8,128)(2,1)}, bf16[3168,768]{1,0:T(8,128)(2,1)}, u32[]{:S(2)}, u32[]{:S(2)}) collective-permute-start(bf16[3168,768]{1,0:T(8,128)(2,1)} %fusion.14), channel_id=1, source_target_pairs={{0,1},{1,0},{2,3},{3,2},{4,5},{5,4},{6,7},{7,6},{8,9},{9,8},{10,11... | collective-permute-start | bytes 14598152 | tf_op jit(solution)/shard_map/ppermute | solution.py:107
  442.2 74.4 %copy-start.15 = (f32[256,768]{1,0:T(8,128)S(1)}, f32[256,768]{1,0:T(8,128)}, u32[]{:S(2)}) copy-start(f32[256,768]{1,0:T(8,128)} %copy-done.14) | copy-start | bytes 2359300
  442.2 74.4 %copy-start.77 = (f32[768]{0:T(1024)S(1)}, f32[768]{0:T(1024)}, u32[]{:S(2)}) copy-start(f32[768]{0:T(1024)} %get-tuple-element.379) | copy-start | bytes 9220
  442.2 74.4 %copy-start.85 = (f32[256]{0:T(256)S(1)}, f32[256]{0:T(256)}, u32[]{:S(2)}) copy-start(f32[256]{0:T(256)} %copy-done.84) | copy-start | bytes 3076
  443.3 19.7 %collective-permute-start.1 = (bf16[256,768]{1,0:T(8,128)(2,1)S(1)}, bf16[256,768]{1,0:T(8,128)(2,1)S(1)}, u32[]{:S(2)}, u32[]{:S(2)}) collective-permute-start(bf16[256,768]{1,0:T(8,128)(2,1)S(1)} %get-tuple-element.501), channel_id=1, source_target_pairs={{0,4},{4,8},{8,12},{12,16},{16,20},{20,24},{24,28},{28,0},{1,5},{5... | collective-permute-start | bytes 1179656 | tf_op jit(solution)/shard_map/ppermute | solution.py:107
  445.5 20.8 %collective-permute-start.7 = (bf16[256,768]{1,0:T(8,128)(2,1)S(1)}, bf16[256,768]{1,0:T(8,128)(2,1)S(1)}, u32[]{:S(2)}, u32[]{:S(2)}) collective-permute-start(bf16[256,768]{1,0:T(8,128)(2,1)S(1)} %get-tuple-element.502), channel_id=1, source_target_pairs={{0,28},{4,0},{8,4},{12,8},{16,12},{20,16},{24,20},{28,24},{1,29},{... | collective-permute-start | bytes 1179656 | tf_op jit(solution)/shard_map/ppermute | solution.py:107
  448.0 28.1 %collective-permute-start.6 = (bf16[256,768]{1,0:T(8,128)(2,1)}, bf16[256,768]{1,0:T(8,128)(2,1)S(1)}, u32[]{:S(2)}, u32[]{:S(2)}) collective-permute-start(bf16[256,768]{1,0:T(8,128)(2,1)} %get-tuple-element.503), channel_id=1, source_target_pairs={{0,24},{4,28},{8,0},{12,4},{16,8},{20,12},{24,16},{28,20},{1,25},{... | collective-permute-start | bytes 1179656 | tf_op jit(solution)/shard_map/ppermute | solution.py:107
  449.5 28.3 %collective-permute-start.5 = (bf16[256,768]{1,0:T(8,128)(2,1)}, bf16[256,768]{1,0:T(8,128)(2,1)}, u32[]{:S(2)}, u32[]{:S(2)}) collective-permute-start(bf16[256,768]{1,0:T(8,128)(2,1)} %get-tuple-element.504), channel_id=1, source_target_pairs={{0,20},{4,24},{8,28},{12,0},{16,4},{20,8},{24,12},{28,16},{1,21},{... | collective-permute-start | bytes 1179656 | tf_op jit(solution)/shard_map/ppermute | solution.py:107
  449.5 66.8 %collective-permute-start.4 = (bf16[256,768]{1,0:T(8,128)(2,1)S(1)}, bf16[256,768]{1,0:T(8,128)(2,1)}, u32[]{:S(2)}, u32[]{:S(2)}) collective-permute-start(bf16[256,768]{1,0:T(8,128)(2,1)S(1)} %get-tuple-element.505), channel_id=1, source_target_pairs={{0,16},{4,20},{8,24},{12,28},{16,0},{20,4},{24,8},{28,12},{1,17},{... | collective-permute-start | bytes 1179656 | tf_op jit(solution)/shard_map/ppermute | solution.py:107
  463.0 53.7 %collective-permute-start.3 = (bf16[256,768]{1,0:T(8,128)(2,1)S(1)}, bf16[256,768]{1,0:T(8,128)(2,1)}, u32[]{:S(2)}, u32[]{:S(2)}) collective-permute-start(bf16[256,768]{1,0:T(8,128)(2,1)S(1)} %get-tuple-element.506), channel_id=1, source_target_pairs={{0,12},{4,16},{8,20},{12,24},{16,28},{20,0},{24,4},{28,8},{1,13},{... | collective-permute-start | bytes 1179656 | tf_op jit(solution)/shard_map/ppermute | solution.py:107
  466.4 50.3 %collective-permute-start.2 = (bf16[256,768]{1,0:T(8,128)(2,1)S(1)}, bf16[256,768]{1,0:T(8,128)(2,1)}, u32[]{:S(2)}, u32[]{:S(2)}) collective-permute-start(bf16[256,768]{1,0:T(8,128)(2,1)S(1)} %get-tuple-element.507), channel_id=1, source_target_pairs={{0,8},{4,12},{8,16},{12,20},{16,24},{20,28},{24,0},{28,4},{1,9},{5... | collective-permute-start | bytes 1179656 | tf_op jit(solution)/shard_map/ppermute | solution.py:107
  476.1 44.6 %copy-start.113 = (f32[256,3072]{1,0:T(8,128)S(1)}, f32[256,3072]{1,0:T(8,128)}, u32[]{:S(2)}) copy-start(f32[256,3072]{1,0:T(8,128)} %copy-done.112) | copy-start | bytes 9437188
  476.1 269.5 %collective-permute-start.8 = (bf16[3168,768]{1,0:T(8,128)(2,1)}, bf16[3168,768]{1,0:T(8,128)(2,1)}, u32[]{:S(2)}, u32[]{:S(2)}) collective-permute-start(bf16[3168,768]{1,0:T(8,128)(2,1)} %fusion.16.own_ref), channel_id=1, source_target_pairs={{0,2},{1,3},{2,0},{3,1},{4,6},{5,7},{6,4},{7,5},{8,10},{9,11},{10,... | collective-permute-start | bytes 14598152 | tf_op jit(solution)/shard_map/ppermute | solution.py:107
  764.5 40.8 %collective-permute-start.9 = (bf16[3168,768]{1,0:T(8,128)(2,1)}, bf16[3168,768]{1,0:T(8,128)(2,1)}, u32[]{:S(2)}, u32[]{:S(2)}) collective-permute-start(bf16[3168,768]{1,0:T(8,128)(2,1)} %get-tuple-element.362.mine_ref), channel_id=1, source_target_pairs={{0,1},{1,0},{2,3},{3,2},{4,5},{5,4},{6,7},{7,6},{8,9},{9,8},{10,11... | collective-permute-start | bytes 14598152 | tf_op jit(solution)/shard_map/ppermute | solution.py:107
  (108 other events, 647.2 us)
Sparse Core Ops, SparseCore 0:
  13.0 142.4 all-gather.2

commit v3 on v2

--- a/solution.py
+++ b/solution.py
@@ -141,8 +141,7 @@
         v_core, v_x, v_y, v_z = scratch[5:9]
         core_out, core_in, core_own = scratch[9:12]
         one_out, one_in, two_out, two_in, three_out, three_in = scratch[12:18]
-        x_out, x_in, pair_out, pair_in, last_own = scratch[18:23]
-        e_out, e_in, far_out, far_in, v_out, v_in, side_own = scratch[23:]
+        last_own, e_out, e_in, far_out, far_in, v_out, v_in, side_own = scratch[18:]
         dp_at, seq_at = lax.axis_index("dp"), lax.axis_index("seq")
         x_at, c_at = seq_at // 2, lax.rem(seq_at, 2)
         z_at, y_at = dp_at // n_y, lax.rem(dp_at, n_y)
@@ -361,30 +360,9 @@
             for step in range(1, n_z):
                 total = total + third[chunk, step - 1].astype(f32)
             own[chunk, here] = total.astype(bf16)
-            result = o_ref.at[c_at, x_at, chunk]
-            copy = pltpu.make_async_copy(own.at[chunk, here], result, last_own.at[chunk])
+            copy = pltpu.make_async_copy(own.at[chunk, here], o_ref.at[chunk], last_own.at[chunk])
             copy.start()
             kept[0, chunk] = copy
-            for step in range(1, n_x):
-                to = lax.rem(x_at + step, n_x)
-                kept[4, chunk, step] = send(
-                    own.at[chunk, here],
-                    result,
-                    x_out.at[chunk, step - 1],
-                    x_in.at[chunk, step - 1],
-                    {"seq": to * 2 + c_at},
-                )
-            kept[5, chunk, 0] = send(
-                own.at[chunk, here], result, pair_out.at[chunk, 0], pair_in.at[chunk, 0], partner
-            )
-        for chunk in range(chunks):
-            for step in range(1, n_x):
-                kept[4, chunk, step].wait_recv()
-                origin = lax.rem(x_at + n_x - step, n_x)
-                piece = o_ref.at[c_at, origin, chunk]
-                kept[5, chunk, step] = send(
-                    piece, piece, pair_out.at[chunk, step], pair_in.at[chunk, step], partner
-                )
 
         @pl.loop(0, near)
         def _(step):
@@ -393,10 +371,8 @@
 
         for chunk in range(chunks):
             kept[0, chunk].wait()
-            for step in range(n_x):
-                kept[5, chunk, step].wait()
         for key, copy in kept.items():
-            if 1 <= key[0] <= 4:
+            if key[0] > 0:
                 copy.wait_send()
 
     def dma(*shape):
@@ -406,7 +382,7 @@
     return pl.pallas_call(
         body,
         out_shape=(
-            jax.ShapeDtypeStruct((2, n_x, chunks, height, width), bf16),
+            jax.ShapeDtypeStruct((chunks, height, width), bf16),
             jax.ShapeDtypeStruct((count,) + given.shape[1:], given.dtype),
             jax.ShapeDtypeStruct(vector.shape, vector.dtype),
         ),
@@ -431,10 +407,6 @@
             dma(chunks, n_most - 1),
             dma(chunks, n_z - 1),
             dma(chunks, n_z - 1),
-            dma(chunks, n_x - 1),
-            dma(chunks, n_x - 1),
-            dma(chunks, n_x),
-            dma(chunks, n_x),
             dma(chunks),
             dma(near),
             dma(near),
@@ -450,69 +422,844 @@
     )(grads, given, vector)
 
 
-def close_half(own, other, names, values, tile):
-    half, width = own.shape
-    count = names.shape[1]
-
-    def body(own_ref, other_ref, names_ref, values_ref, o_ref, square_ref):
-        step = pl.program_id(0)
-        row = lax.broadcasted_iota(i32, (tile, count), 0) + step * tile
-        where = jnp.where(row == names_ref[...], 1.0, 0.0).astype(bf16)
-        total = own_ref[...].astype(f32) + other_ref[...].astype(f32)
-        total = total + jnp.dot(where, values_ref[...], preferred_element_type=f32)
-        o_ref[...] = total.astype(bf16)
-
-        @pl.when(step == 0)
-        def _():
-            square_ref[...] = jnp.zeros_like(square_ref)
-
-        square_ref[...] += jnp.sum(total * total, axis=0, keepdims=True)
-
-    rows = pl.BlockSpec((tile, width), lambda step: (step, 0))
+def read_heads(source, table_low, targets, vocab_part, chunk, n_y, n_z, call_id):
+    n_pick, width = source.shape
+    size = table_low.shape[0]
+    n_dp = n_y * n_z
+    chunks = size // chunk
+
+    def body(s_ref, t_ref, target_ref, e_ref, h_ref, m_ref, stat_ref, e_buf, h_buf, t_buf, told, came, *sems):
+        z_out, z_in, y_out, y_in, stat_out, stat_in, e_sem, load_sem, h_sem = sems
+        dp_at = lax.axis_index("dp")
+        z_at, y_at = dp_at // n_y, lax.rem(dp_at, n_y)
+        load = pltpu.make_async_copy(t_ref, t_buf, load_sem)
+        load.start()
+        h_buf[dp_at] = s_ref[...]
+        barrier = pltpu.get_barrier_semaphore()
+
+        @pl.loop(1, n_dp)
+        def _(step):
+            to = lax.rem(dp_at + step, n_dp)
+            pl.semaphore_signal(barrier, inc=1, device_id={"dp": to}, device_id_type=MESH)
+
+        pl.semaphore_wait(barrier, n_dp - 1)
+
+        def z_copy(step):
+            mine = h_buf.at[dp_at]
+            to = lax.rem(z_at + step, n_z) * n_y + y_at
+            return pltpu.make_async_remote_copy(
+                mine, mine, z_out.at[step], z_in.at[step], device_id={"dp": to}, device_id_type=MESH
+            )
+
+        def y_copy(turn, step):
+            block = h_buf.at[lax.rem(z_at + n_z - turn, n_z) * n_y + y_at]
+            to = z_at * n_y + lax.rem(y_at + step, n_y)
+            return pltpu.make_async_remote_copy(
+                block,
+                block,
+                y_out.at[turn, step],
+                y_in.at[turn, step],
+                device_id={"dp": to},
+                device_id_type=MESH,
+            )
+
+        for step in range(1, n_y):
+            y_copy(0, step).start()
+        for step in range(1, n_z):
+            z_copy(step).start()
+        load.wait()
+
+        def logits(rows, index):
+            part = t_buf[index * chunk : (index + 1) * chunk]
+            return lax.dot_general(part, rows, (((1,), (1,)), ((), ())), preferred_element_type=f32)
+
+        @pl.loop(0, n_dp)
+        def _(turn):
+            z_turn, y_turn = turn // n_y, lax.rem(turn, n_y)
+
+            @pl.when((y_turn == 0) & (z_turn > 0))
+            def _():
+                z_copy(z_turn).wait_recv()
+                for step in range(1, n_y):
+                    y_copy(z_turn, step).start()
+
+            @pl.when(y_turn > 0)
+            def _():
+                y_copy(z_turn, y_turn).wait_recv()
+
+            origin = lax.rem(z_at + n_z - z_turn, n_z) * n_y + lax.rem(y_at + n_y - y_turn, n_y)
+            rows = h_buf[origin]
+            target = target_ref[origin]
+            row = lax.broadcasted_iota(i32, (chunk // 8, 8, n_pick), 0) * 8
+            row = row + lax.broadcasted_iota(i32, (chunk // 8, 8, n_pick), 1)
+            top = summed = hit = None
+            ahead = logits(rows, 0)
+            for index in range(chunks):
+                now = ahead.reshape(chunk // 8, 8, n_pick)
+                if index + 1 < chunks:
+                    ahead = logits(rows, index + 1)
+                first = index * chunk
+                if first + chunk > vocab_part:
+                    now = jnp.where(row < vocab_part - first, now, -jnp.inf)
+                chunk_top = jnp.max(now, axis=0)
+                new_top = chunk_top if top is None else jnp.maximum(top, chunk_top)
+                grown = jnp.exp(now - new_top[None])
+                chunk_sum = jnp.sum(grown, axis=0)
+                chunk_hit = jnp.sum(jnp.where(row == (target - first)[None], now, 0.0), axis=0)
+                if top is None:
+                    summed, hit = chunk_sum, chunk_hit
+                else:
+                    summed = summed * jnp.exp(top - new_top) + chunk_sum
+                    hit = hit + chunk_hit
+                top = new_top
+                e_buf[origin, first : first + chunk] = grown.reshape(chunk, n_pick).astype(bf16)
+                m_ref[origin, index] = top
+            best = jnp.max(top, axis=0, keepdims=True)
+            told[origin] = jnp.zeros((8, n_pick), f32)
+            told[origin, 0:1] = best
+            told[origin, 1:2] = jnp.sum(summed * jnp.exp(top - best), axis=0, keepdims=True)
+            told[origin, 2:3] = jnp.sum(hit, axis=0, keepdims=True)
+            pltpu.make_async_copy(e_buf.at[origin], e_ref.at[origin], e_sem.at[origin]).start()
+
+        def stat_copy(step):
+            to = lax.rem(dp_at + step, n_dp)
+            return pltpu.make_async_remote_copy(
+                told,
+                came.at[dp_at],
+                stat_out.at[step],
+                stat_in.at[step],
+                device_id={"dp": to},
+                device_id_type=MESH,
+            )
+
+        @pl.loop(1, n_dp)
+        def _(step):
+            stat_copy(step).start()
+
+        came[dp_at] = told[...]
+        keep = pltpu.make_async_copy(h_buf, h_ref, h_sem)
+        keep.start()
+        for step in range(1, n_z):
+            z_copy(step).wait_send()
+        for turn in range(n_z):
+            for step in range(1, n_y):
+                y_copy(turn, step).wait_send()
+
+        @pl.loop(0, n_dp)
+        def _(origin):
+            pltpu.make_async_copy(e_buf.at[origin], e_ref.at[origin], e_sem.at[origin]).wait()
+
+        @pl.loop(1, n_dp)
+        def _(step):
+            stat_copy(step).wait()
+
+        keep.wait()
+        stat_ref[...] = came[...]
+
+    def dma(*shape):
+        return pltpu.SemaphoreType.DMA(shape)
+
     return pl.pallas_call(
         body,
-        grid=(half // tile,),
+        out_shape=(
+            jax.ShapeDtypeStruct((n_dp, size, n_pick), bf16),
+            jax.ShapeDtypeStruct((n_dp, n_pick, width), bf16),
+            jax.ShapeDtypeStruct((n_dp, chunks, 8, n_pick), f32),
+            jax.ShapeDtypeStruct((n_dp, n_dp, 8, n_pick), f32),
+        ),
+        in_specs=[VMEM, HBM, VMEM],
+        out_specs=(HBM, HBM, VMEM, VMEM),
+        scratch_shapes=[
+            pltpu.VMEM((n_dp, size, n_pick), bf16),
+            pltpu.VMEM((n_dp, n_pick, width), bf16),
+            pltpu.VMEM((size, width), bf16),
+            pltpu.VMEM((n_dp, 8, n_pick), f32),
+            pltpu.VMEM((n_dp, n_dp, 8, n_pick), f32),
+            dma(n_z),
+            dma(n_z),
+            dma(n_z, n_y),
+            dma(n_z, n_y),
+            dma(n_dp),
+            dma(n_dp),
+            dma(n_dp),
+            pltpu.SemaphoreType.DMA,
+            pltpu.SemaphoreType.DMA,
+        ],
+        compiler_params=pltpu.CompilerParams(
+            collective_id=call_id, has_side_effects=True, vmem_limit_bytes=56 << 20
+        ),
+    )(source, table_low, targets)
+
+
+def write_heads(grown, heads, turned, tops, stats, targets, weights, chunk, call_id):
+    n_dp, size, n_pick = grown.shape
+    width = heads.shape[2]
+    chunks = size // chunk
+    turns = chunks // 2
+
+    def body(e_ref, h_ref, t_ref, m_ref, stat_ref, target_ref, w_ref, d_ref, half_ref, log_ref, *scratch):
+        buf, t_buf, df_buf, out_buf, got, res = scratch[:6]
+        e_sem, t_sem, df_out, df_in, df_own, pair_out, pair_in, res_sem = scratch[6:]
+        dp_at, seq_at = lax.axis_index("dp"), lax.axis_index("seq")
+        core = lax.rem(seq_at, 2)
+        partner = {"seq": seq_at + 1 - 2 * core}
+        load = pltpu.make_async_copy(t_ref, t_buf, t_sem)
+
+        def e_copy(turn):
+            origin = lax.rem(dp_at + 1 + turn, n_dp)
+            return pltpu.make_async_copy(e_ref.at[origin], buf.at[origin], e_sem.at[turn])
+
+        e_copy(0).start()
+        load.start()
+
+        @pl.loop(1, n_dp)
+        def _(turn):
+            e_copy(turn).start()
+
+        barrier = pltpu.get_barrier_semaphore()
+
+        @pl.loop(1, n_dp)
+        def _(step):
+            to = lax.rem(dp_at + step, n_dp)
+            pl.semaphore_signal(barrier, inc=1, device_id={"dp": to}, device_id_type=MESH)
+
+        pl.semaphore_signal(barrier, inc=1, device_id=partner, device_id_type=MESH)
+
+        @pl.loop(0, n_dp)
+        def _(origin):
+            top = stat_ref[0, origin, 0:1]
+            for sender in range(1, n_dp):
+                top = jnp.maximum(top, stat_ref[sender, origin, 0:1])
+            total = jnp.zeros((1, n_pick), f32)
+            hit = jnp.zeros((1, n_pick), f32)
+            for sender in range(n_dp):
+                total = total + stat_ref[sender, origin, 1:2] * jnp.exp(stat_ref[sender, origin, 0:1] - top)
+                hit = hit + stat_ref[sender, origin, 2:3]
+            log_ref[0, origin] = top + jnp.log(total)
+            log_ref[1, origin] = hit
+
+        load.wait()
+        pl.semaphore_wait(barrier, n_dp)
+
+        def df_copy(turn):
+            to = lax.rem(dp_at + 1 + turn, n_dp)
+            return pltpu.make_async_remote_copy(
+                df_buf.at[to],
+                d_ref.at[dp_at],
+                df_out.at[turn],
+                df_in.at[turn],
+                device_id={"dp": to},
+                device_id_type=MESH,
+            )
+
+        @pl.loop(0, n_dp)
+        def _(turn):
+            origin = lax.rem(dp_at + 1 + turn, n_dp)
+            e_copy(turn).wait()
+            log_total = log_ref[0, origin]
+            weight = w_ref[origin]
+            target = target_ref[origin]
+            row = lax.broadcasted_iota(i32, (chunk // 8, 8, n_pick), 0) * 8
+            row = row + lax.broadcasted_iota(i32, (chunk // 8, 8, n_pick), 1)
+
+            def gradient(index):
+                rows = pl.ds(index * chunk, chunk)
+                scale = jnp.exp(m_ref[origin, index] - log_total) * weight
+                part = buf[origin, rows].astype(f32).reshape(chunk // 8, 8, n_pick) * scale[None]
+                at_target = row == (target - index * chunk)[None]
+                part = part - jnp.where(at_target, weight[None], 0.0)
+                part = part.reshape(chunk, n_pick).astype(bf16)
+                buf[origin, rows] = part
+                return part
+
+            total = None
+            ahead = gradient(0)
+            for index in range(chunks):
+                now = ahead
+                if index + 1 < chunks:
+                    ahead = gradient(index + 1)
+                columns = t_buf[:, index * chunk : (index + 1) * chunk]
+                part = jnp.dot(columns, now, preferred_element_type=f32)
+                total = part if total is None else total + part
+            df_buf[origin] = total.astype(bf16)
+
+            @pl.when(turn < n_dp - 1)
+            def _():
+                df_copy(turn).start()
+
+        local = pltpu.make_async_copy(df_buf.at[dp_at], d_ref.at[dp_at], df_own)
+        local.start()
+
+        def table_part(index):
+            first = pl.multiple_of(index * chunk, chunk)
+            part = jnp.concatenate([buf[origin, pl.ds(first, chunk)] for origin in range(n_dp)], axis=1)
+            return jnp.dot(part, h_ref[...], preferred_element_type=f32)
+
+        def pair_copy(turn):
+            return pltpu.make_async_remote_copy(
+                out_buf.at[turn],
+                got.at[turn],
+                pair_out.at[turn],
+                pair_in.at[turn],
+                device_id=partner,
+                device_id_type=MESH,
+            )
+
+        @pl.loop(0, turns)
+        def _(turn):
+            out_buf[turn] = table_part((1 - core) * turns + turn).astype(bf16)
+            pair_copy(turn).start()
+
+        def res_copy(turn):
+            return pltpu.make_async_copy(res.at[turn], half_ref.at[turn], res_sem.at[turn])
+
+        @pl.loop(0, turns)
+        def _(turn):
+            total = table_part(core * turns + turn)
+            pair_copy(turn).wait()
+            res[turn] = (total + got[turn].astype(f32)).astype(bf16)
+            res_copy(turn).start()
+
+        @pl.loop(0, turns)
+        def _(turn):
+            res_copy(turn).wait()
+
+        local.wait()
+
+        @pl.loop(0, n_dp - 1)
+        def _(turn):
+            df_copy(turn).wait()
+
+    def dma(*shape):
+        return pltpu.SemaphoreType.DMA(shape)
+
+    return pl.pallas_call(
+        body,
+        out_shape=(
+            jax.ShapeDtypeStruct((n_dp, width, n_pick), bf16),
+            jax.ShapeDtypeStruct((turns, chunk, width), bf16),
+            jax.ShapeDtypeStruct((2, n_dp, 1, n_pick), f32),
+        ),
+        in_specs=[HBM, VMEM, HBM, VMEM, VMEM, VMEM, VMEM],
+        out_specs=(HBM, HBM, VMEM),
+        scratch_shapes=[
+            pltpu.VMEM((n_dp, size, n_pick), bf16),
+            pltpu.VMEM((width, size), bf16),
+            pltpu.VMEM((n_dp, width, n_pick), bf16),
+            pltpu.VMEM((turns, chunk, width), bf16),
+            pltpu.VMEM((turns, chunk, width), bf16),
+            pltpu.VMEM((turns, chunk, width), bf16),
+            dma(n_dp),
+            pltpu.SemaphoreType.DMA,
+            dma(n_dp),
+            dma(n_dp),
+            pltpu.SemaphoreType.DMA,
+            dma(turns),
+            dma(turns),
+            dma(turns),
+        ],
+        compiler_params=pltpu.CompilerParams(
+            collective_id=call_id, has_side_effects=True, vmem_limit_bytes=62 << 20
+        ),
+    )(grown, heads.reshape(n_dp * n_pick, width), turned, tops, stats, targets, weights)
+
+
+def staged(work, ins, small, outs, temps, limit, buffers_of=(), pieces=None, eager=2):
+    n_in, n_small, n_out = len(ins), len(small), len(outs)
+    packed, places = ((), {}) if pieces is None else ((pieces[0],), pieces[1])
+
+    def body(*refs):
+        packed_refs, refs = refs[: len(packed)], refs[len(packed) :]
+        in_refs, small_refs, refs = refs[:n_in], refs[n_in : n_in + n_small], refs[n_in + n_small :]
+        out_refs, in_bufs, refs = refs[:n_out], refs[n_out : n_out + n_in], refs[n_out + n_in :]
+        out_bufs, (in_sem, out_sem), temp_refs = refs[:n_out], refs[n_out : n_out + 2], refs[n_out + 2 :]
+        loads = {}
+        names = list(ins)
+
+        def start(at):
+            name = names[at]
+            loads[name] = pltpu.make_async_copy(in_refs[at], in_bufs[at], in_sem.at[at])
+            if name not in places:
+                loads[name].start()
+                return
+            loads[name] = pltpu.make_async_copy(in_bufs[at], in_bufs[at], in_sem.at[at])
+            for source, target in places[name]:
+                pltpu.make_async_copy(
+                    packed_refs[0].at[source], in_bufs[at].at[target], in_sem.at[at]
+                ).start()
+
+        for at in range(eager):
+            start(at)
+        buffers = dict(zip(ins, in_bufs))
+        pending, sent = list(ins), []
+
+        def get(name):
+            if name in pending:
+                pending.remove(name)
+                loads[name].wait()
+                if name == names[eager - 1]:
+                    for at in range(eager, n_in):
+                        start(at)
+            return buffers[name]
+
+        def put(name, begin=0, count=None):
+            at = list(outs).index(name)
+            source, target = out_bufs[at], out_refs[at]
+            if count is not None:
+                source, target = source.at[:, pl.ds(0, count)], target.at[:, pl.ds(begin, count)]
+            copy = pltpu.make_async_copy(source, target, out_sem.at[len(sent)])
+            copy.start()
+            sent.append(copy)
+            return copy
+
+        def done(copy):
+            copy.wait()
+            sent[sent.index(copy)] = None
+
+        work(get, dict(zip(small, small_refs)), dict(zip(outs, out_bufs)), (put, done), temp_refs)
+        for name in list(pending):
+            get(name)
+        for copy in sent:
+            if copy is not None:
+                copy.wait()
+
+    def scratch(value):
+        return pltpu.VMEM(value.shape, value.dtype)
+
+    def refs_of(name, value):
+        return jnp.zeros((8, 128), value.dtype) if name in places else value
+
+    return pl.pallas_call(
+        body,
+        out_shape=tuple(outs.values()),
+        in_specs=[HBM] * (len(packed) + n_in) + [VMEM] * n_small,
+        out_specs=(HBM,) * n_out,
+        scratch_shapes=[scratch(value) for value in ins.values()]
+        + [scratch(dict(buffers_of).get(name, value)) for name, value in outs.items()]
+        + [pltpu.SemaphoreType.DMA((n_in,)), pltpu.SemaphoreType.DMA((n_out + 2,))]
+        + temps,
+        compiler_params=pltpu.CompilerParams(vmem_limit_bytes=limit << 20),
+        cost_estimate=pl.CostEstimate(flops=0, bytes_accessed=0, transcendentals=0),
+    )(*packed, *[refs_of(name, value) for name, value in ins.items()], *small.values())
+
+
+def dot(left, right, left_dim=1, right_dim=0):
+    return lax.dot_general(
+        left, right, (((left_dim,), (right_dim,)), ((), ())), preferred_element_type=f32
+    )
+
+
+def norm_parts(x):
+    centre = x - jnp.mean(x, axis=-1, keepdims=True)
+    scale = lax.rsqrt(jnp.mean(centre * centre, axis=-1, keepdims=True) + 1e-05)
+    return centre * scale, scale
+
+
+def norm_back(x, gain, grad):
+    unit, scale = norm_parts(x)
+    d_gain = jnp.sum(grad * unit, axis=0, keepdims=True)
+    d_shift = jnp.sum(grad, axis=0, keepdims=True)
+    inner = grad * gain
+    pull = jnp.mean(inner, axis=-1, keepdims=True)
+    pull = pull + unit * jnp.mean(inner * unit, axis=-1, keepdims=True)
+    return scale * (inner - pull), d_gain, d_shift
+
+
+def iota(shape, dim):
+    return lax.broadcasted_iota(i32, shape, dim)
+
+
+def flat(ref, columns=slice(None)):
+    value = ref[..., columns]
+    return value.reshape(-1, value.shape[-1])
+
+
+def row_block(ref, block, size):
+    first = block * size
+    if len(ref.shape) == 2:
+        return ref[first : first + size]
+    _, inner, rows, _ = ref.shape
+    if inner * rows <= size:
+        per = inner * rows
+        return flat(ref[first // per : (first + size) // per])
+    owner, first = divmod(first, inner * rows)
+    return flat(ref[owner, first // rows : (first + size) // rows])
+
+
+def split_three(x):
+    high = x.astype(bf16)
+    rest = x - high.astype(f32)
+    middle = rest.astype(bf16)
+    return high, middle, (rest - middle.astype(f32)).astype(bf16)
+
+
+def layer_forward(embedded, pos, w_in, w_out, w_up, w_down, vectors, picks, row_length, pieces):
+    length, model = embedded.shape
+    n_pick = picks.shape[0]
+    lanes = 128
+    groups = model // lanes
+    head_dim = model // H
+    per = lanes // head_dim
+
+    def work(get, small, out, moves, temps):
+        put, _ = moves
+        vec = small["vectors"]
+        v_turned, o_turned = temps
+        emb, pos_rows = get("emb"), get("pos")
+        start = emb[...].astype(f32) + flat(pos_rows).astype(f32)
+        unit, _ = norm_parts(start)
+        out["a"][...] = (unit * vec[0:1] + vec[1:2]).astype(bf16)
+        put("a")
+        chosen = jnp.where(small["pick_col"][...] - 1 == iota((n_pick, length), 1), 1.0, 0.0).astype(bf16)
+        start_picked = dot(chosen, emb[...]) + dot(chosen, flat(pos_rows))
+        w = get("w_in")
+        out["k"][...] = dot(out["a"][...], flat(w, slice(model, 2 * model))).astype(bf16)
+        put("k")
+        out["v"][...] = (dot(out["a"][...], flat(w, slice(2 * model, 3 * model))) + vec[7:8]).astype(bf16)
+        put("v")
+        a_picked = dot(chosen, out["a"][...]).astype(bf16)
+        out["q"][...] = (dot(a_picked, flat(w, slice(0, model))) + vec[6:7]).astype(bf16)
+        put("q")
+        keep = iota((length, n_pick), 0) < small["length"][0, 0]
+
+        @pl.loop(0, groups)
+        def _(group):
+            place = pl.ds(pl.multiple_of(group * lanes, lanes), lanes)
+            v_turned[...] = out["v"][:, place].T
+            q_pair, k_pair = out["q"][:, place], out["k"][:, place]
+            mixed = None
+            for j in range(per):
+                q_head = jnp.where(iota((n_pick, lanes), 1) // head_dim == j, q_pair, jnp.zeros_like(q_pair))
+                score = jnp.where(keep, dot(k_pair, q_head, 1, 1) * 0.125, mask_fill)
+                top = jnp.max(score, axis=0, keepdims=True)
+                grown = jnp.exp(score - top)
+                total = jnp.sum(grown, axis=0, keepdims=True)
+                out["lse"][group * per + j] = top + jnp.log(total)
+                probs = (grown * (1.0 / total)).astype(bf16)
+                part = dot(v_turned[...], probs)
+                mixed = part if mixed is None else jnp.where(iota((lanes, n_pick), 0) // head_dim == j, part, mixed)
+            o_turned[pl.ds(pl.multiple_of(group * lanes, lanes), lanes)] = mixed
+
+        out["o"][...] = o_turned[...].T.astype(bf16)
+        put("lse")
+        put("o")
+        x1 = start_picked + dot(out["o"][...], flat(get("w_out"))) + vec[8:9]
+        out["x1"][...] = x1
+        put("x1")
+        unit, _ = norm_parts(x1)
+        out["m"][...] = (unit * vec[2:3] + vec[3:4]).astype(bf16)
+        put("m")
+        up, down = get("w_up"), get("w_down")
+        x2 = x1 + vec[9:10]
+        for block in range(up.shape[-1] // model):
+            place = slice(block * model, (block + 1) * model)
+            u1 = dot(out["m"][...], flat(up, place)) + vec[10 + block : 11 + block]
+            x2 = x2 + dot(gelu_fn(u1).astype(bf16), row_block(down, block, model))
+        out["x2"][...] = x2
+        put("x2")
+        unit, _ = norm_parts(x2)
+        out["f"][...] = (unit * vec[4:5] + vec[5:6]).astype(bf16)
+        put("f")
+
+    def shape(rows, dtype):
+        return jax.ShapeDtypeStruct((rows, model), dtype)
+
+    outs = {
+        "a": shape(length, bf16),
+        "k": shape(length, bf16),
+        "v": shape(length, bf16),
+        "q": shape(n_pick, bf16),
+        "lse": jax.ShapeDtypeStruct((H, 1, n_pick), f32),
+        "o": shape(n_pick, bf16),
+        "x1": shape(n_pick, f32),
+        "m": shape(n_pick, bf16),
+        "x2": shape(n_pick, f32),
+        "f": shape(n_pick, bf16),
+    }
+    values = staged(
+        work,
+        {"emb": embedded, "pos": pos, "w_in": w_in, "w_out": w_out, "w_up": w_up, "w_down": w_down},
+        {"vectors": vectors, "pick_col": picks[:, None], "length": row_length.reshape(1, 1)},
+        outs,
+        [pltpu.VMEM((lanes, length), bf16), pltpu.VMEM((model, n_pick), f32)],
+        60,
+        pieces=pieces,
+    )
+    return dict(zip(outs, values))
+
+
+def layer_backward(
+    final_grad, kept, embedded, pos, weights, vectors, picks, spots, row_length, loss, n_dp, pieces
+):
+    length, model = embedded.shape
+    n_pick = picks.shape[0]
+    lanes = 128
+    groups = model // lanes
+    head_dim = model // H
+    per = lanes // head_dim
+    w_in, w_out, w_up, w_down = weights
+    hidden = w_up.shape[-1]
+    thick, long, n_place = model // n_dp, hidden // n_dp, spots[1]
+    wide = hidden // model
+    first_rows = 2 * long
+    last_rows = 4 * thick + length // n_dp
+
+    def work(get, small, out, moves, temps):
+        put, done = moves
+        vec, d_vec = small["vectors"], out["vec"]
+        dqkv, dq, d_mixed = temps
+        whole = out["whole"]
+
+        def rows_of(first, count, values):
+            values = values.astype(bf16)
+            for owner in range(n_dp):
+                whole[owner, first : first + count] = values[owner * count : (owner + 1) * count]
+
+        x2, dfin = get("x2"), get("dfin")
+        dx2, d_vec[4:5], d_vec[5:6] = norm_back(x2[...], vec[4:5], dfin[...])
+        dy2 = dx2.astype(bf16)
+        d_vec[9:10] = jnp.sum(dy2.astype(f32), axis=0, keepdims=True)
+        m, up, down = get("m"), get("w_up"), get("w_down")
+        m_turned = m[...].T
+        dm = None
+        for block in range(wide):
+            place = slice(block * model, (block + 1) * model)
+            u1 = dot(m[...], flat(up, place)) + vec[10 + block : 11 + block]
+            act, gelu_back = jax.vjp(gelu_fn, u1)
+            part = dot(act.astype(bf16).T, dy2).astype(bf16)
+            run = min(long, model)
+            for at in range(0, model, run):
+                owner, row = divmod(block * model + at, long)
+                whole[owner, row : row + run] = part[at : at + run]
+            du1 = gelu_back(dot(dy2, row_block(down, block, model), 1, 1))[0].astype(bf16)
+            d_vec[10 + block : 11 + block] = jnp.sum(du1.astype(f32), axis=0, keepdims=True)
+            rows_of(long + block * thick, thick, dot(m_turned, du1))
+            part = dot(du1, flat(up, place), 1, 1)
+            dm = part if dm is None else dm + part
+        first_out = put("whole", 0, first_rows)
+        dx1, d_vec[2:3], d_vec[3:4] = norm_back(get("x1")[...], vec[2:3], dm)
+        dx1 = dx2 + dx1
+        dy1 = dx1.astype(bf16)
+        d_vec[8:9] = jnp.sum(dy1.astype(f32), axis=0, keepdims=True)
+        done(first_out)
+        rows_of(0, thick, dot(get("o")[...].T, dy1))
+        d_mixed[...] = dot(dy1, flat(get("w_out")), 1, 1).astype(bf16)
+        keep = iota((length, n_pick), 0) < small["length"][0, 0]
+        q, k, v, lse = get("q"), get("k"), get("v"), small["lse"]
+
+        @pl.loop(0, groups)
+        def _(group):
+            def place(part):
+                return pl.ds(pl.multiple_of(part * model + group * lanes, lanes), lanes)
+
+            q_pair, k_pair, v_pair, d_pair = q[:, place(0)], k[:, place(0)], v[:, place(0)], d_mixed[:, place(0)]
+            k_turned = k_pair.T
+            sums = None
+            for j in range(per):
+                lane = iota((n_pick, lanes), 1) // head_dim == j
+                q_head = jnp.where(lane, q_pair, jnp.zeros_like(q_pair))
+                d_head = jnp.where(lane, d_pair, jnp.zeros_like(d_pair))
+                score = jnp.where(keep, dot(k_pair, q_head, 1, 1) * 0.125, mask_fill)
+                probs = jnp.exp(score - lse[group * per + j])
+                dp = dot(v_pair, d_head, 1, 1)
+                ds = (probs * (dp - jnp.sum(dp * probs, axis=0, keepdims=True))).astype(bf16)
+                parts = (dot(k_turned, ds), dot(ds, q_pair), dot(probs.astype(bf16), d_pair))
+                if sums is None:
+                    sums = parts
+                else:
+                    rows = iota((lanes, n_pick), 0) // head_dim == j
+                    columns = iota((length, lanes), 1) // head_dim == j
+                    sums = (
+                        jnp.where(rows, parts[0], sums[0]),
+                        jnp.where(columns, parts[1], sums[1]),
+                        jnp.where(columns, parts[2], sums[2]),
+                    )
+            dq[:, place(0)] = (sums[0] * 0.125).T.astype(bf16)
+            dqkv[:, place(1)] = (sums[1] * 0.125).astype(bf16)
+            dqkv[:, place(2)] = sums[2].astype(bf16)
+
+        chosen = jnp.where(small["pick_row"][...] - 1 == iota((length, n_pick), 0), 1.0, 0.0).astype(bf16)
+        dqkv[:, :model] = dot(chosen, dq[...]).astype(bf16)
+        d_vec[6:7] = jnp.sum(dq[...].astype(f32), axis=0, keepdims=True)
+        d_vec[7:8] = jnp.sum(dqkv[:, 2 * model :].astype(f32), axis=0, keepdims=True)
+        a_turned = get("a")[...].T
+        for part in range(3):
+            rows_of((1 + part) * thick, thick, dot(a_turned, dqkv[:, part * model : (part + 1) * model]))
+        da = dot(dqkv[...], flat(get("w_in")), 1, 1)
+        start = get("emb")[...].astype(f32) + flat(get("pos")).astype(f32)
+        dx0, d_vec[0:1], d_vec[1:2] = norm_back(start, vec[0:1], da)
+        for part in split_three(dx1):
+            dx0 = dx0 + dot(chosen, part)
+        rows_of(4 * thick, length // n_dp, dx0)
+        put("whole", first_rows, last_rows)
+        d_vec[14:15] = small["loss"][...]
+        d_vec[15:16] = jnp.zeros((1, model), f32)
+        put("vec")
+        out["low"][...] = dx0.astype(bf16)
+        put("low")
+        step = min(n_place, 512)
+        for first in range(0, n_place, step):
+            where = jnp.where(small["spots"][...] == iota((step, length), 0) + first, 1.0, 0.0).astype(bf16)
+            out["given"][first : first + step] = dot(where, out["low"][...]).astype(bf16)
+        put("given")
+
+    outs = {
+        "whole": jax.ShapeDtypeStruct((n_dp, first_rows + last_rows, model), bf16),
+        "vec": jax.ShapeDtypeStruct((16, model), f32),
+        "low": jax.ShapeDtypeStruct((length, model), bf16),
+        "given": jax.ShapeDtypeStruct((n_place, model), bf16),
+    }
+    ins = {
+        "x2": kept["x2"],
+        "dfin": final_grad,
+        "m": kept["m"],
+        "w_up": w_up,
+        "w_down": w_down,
+        "x1": kept["x1"],
+        "o": kept["o"],
+        "w_out": w_out,
+        "q": kept["q"],
+        "k": kept["k"],
+        "v": kept["v"],
+        "a": kept["a"],
+        "w_in": w_in,
+        "emb": embedded,
+        "pos": pos,
+    }
+    small = {
+        "vectors": vectors,
+        "lse": kept["lse"],
+        "pick_row": picks[None, :],
+        "spots": spots[0][None, :],
+        "length": row_length.reshape(1, 1),
+        "loss": jnp.full((1, model), loss),
+    }
+    temps = [
+        pltpu.VMEM((length, 3 * model), bf16),
+        pltpu.VMEM((n_pick, model), bf16),
+        pltpu.VMEM((n_pick, model), bf16),
+    ]
+    buffer = jax.ShapeDtypeStruct((n_dp, max(first_rows, last_rows), model), bf16)
+    return staged(work, ins, small, outs, temps, 62, {"whole": buffer}, pieces, 5)
+
+
+def table_forms(table, size, chunk):
+    count, width = table.shape
+
+    def body(t_ref, low_ref, turned_ref):
+        row = iota((chunk, width), 0) + pl.program_id(0) * chunk
+        value = jnp.where(row < count, t_ref[...], 0.0)
+        low_ref[...] = value.astype(bf16)
+        turned_ref[...] = value.T.astype(bf16)
+
+    return pl.pallas_call(
+        body,
+        grid=(size // chunk,),
+        in_specs=[pl.BlockSpec((chunk, width), lambda step: (step, 0))],
+        out_specs=(
+            pl.BlockSpec((chunk, width), lambda step: (step, 0)),
+            pl.BlockSpec((width, chunk), lambda step: (0, step)),
+        ),
+        out_shape=(
+            jax.ShapeDtypeStruct((size, width), bf16),
+            jax.ShapeDtypeStruct((width, size), bf16),
+        ),
+        compiler_params=pltpu.CompilerParams(vmem_limit_bytes=32 << 20),
+    )(table)
+
+
+def close_half(own, other, names, values, layer, tile):
+    half, width = own.shape
+    count = min(names.shape[1], 2048)
+    parts = names.shape[1] // count
+
+    def body(own_ref, other_ref, names_ref, values_ref, layer_ref, o_ref, square_ref, total):
+        step, part = pl.program_id(0), pl.program_id(1)
+
+        @pl.when(part == 0)
+        def _():
+            total[...] = own_ref[...].astype(f32) + other_ref[...].astype(f32)
+
+        row = iota((tile, count), 0) + step * tile
+        where = jnp.where(row == names_ref[...], 1.0, 0.0).astype(bf16)
+        total[...] += jnp.dot(where, values_ref[...], preferred_element_type=f32)
+
+        @pl.when((step == 0) & (part == 0))
+        def _():
+            layer_part = layer_ref[...].astype(f32)
+            square_ref[...] = jnp.sum(layer_part * layer_part, axis=0, keepdims=True)
+
+        @pl.when(part == parts - 1)
+        def _():
+            o_ref[...] = total[...].astype(bf16)
+            square_ref[...] += jnp.sum(total[...] * total[...], axis=0, keepdims=True)
+
+    rows = pl.BlockSpec((tile, width), lambda step, part: (step, 0))
+    return pl.pallas_call(
+        body,
+        grid=(half // tile, parts),
         in_specs=[
             rows,
             rows,
-            pl.BlockSpec((1, count), lambda step: (0, 0)),
-            pl.BlockSpec((count, width), lambda step: (0, 0)),
+            pl.BlockSpec((1, count), lambda step, part: (0, part)),
+            pl.BlockSpec((count, width), lambda step, part: (part, 0)),
+            pl.BlockSpec(layer.shape, lambda step, part: (0, 0)),
         ],
-        out_specs=(rows, pl.BlockSpec((1, width), lambda step: (0, 0))),
+        out_specs=(rows, pl.BlockSpec((1, width), lambda step, part: (0, 0))),
         out_shape=(jax.ShapeDtypeStruct((half, width), bf16), jax.ShapeDtypeStruct((1, width), f32)),
+        scratch_shapes=[pltpu.VMEM((tile, width), f32)],
         compiler_params=pltpu.CompilerParams(vmem_limit_bytes=48 << 20),
-    )(own, other, names, values)
-
-
-def adam_table(core, factor, weight, first, second, mine, other, tile):
-    size, width = weight.shape
-    turns = mine.shape[0] // tile
-
-    def body(core_ref, factor_ref, w_ref, m_ref, v_ref, mine_ref, other_ref, new_w, new_m, new_v):
-        from_mine = pl.program_id(0) // turns == core_ref[0]
+        cost_estimate=pl.CostEstimate(
+            flops=2 * half * names.shape[1] * width, bytes_accessed=8 * half * width, transcendentals=0
+        ),
+    )(own, other, names, values, layer)
+
+
+def adam_table(at, factor, weights, mine, other, tile, half, n_x, steps, done):
+    size, width = weights[0].shape
+    per_half, per_part = half // tile, half // n_x // tile
+    turns = len(steps) * per_part
+    first_step = steps[0]
+
+    def body(at_ref, factor_ref, w_ref, m_ref, v_ref, mine_ref, other_ref, *refs):
+        from_mine = pl.program_id(0) < turns
         grad = jnp.where(from_mine, mine_ref[...], other_ref[...]).astype(f32) * factor_ref[0]
+        new_w, new_m, new_v, token = refs[-4:]
+        token[...] = jnp.zeros_like(token)
         new_w[...], new_m[...], new_v[...] = adam_update(
             w_ref[...], grad, m_ref[...], v_ref[...], 0.1, 0.1
         )
 
-    def mine_at(step, core_ref, factor_ref):
-        return (jnp.clip(step - core_ref[0] * turns, 0, turns - 1), 0)
-
-    def other_at(step, core_ref, factor_ref):
-        return (jnp.clip(step - (1 - core_ref[0]) * turns, 0, turns - 1), 0)
-
-    rows = pl.BlockSpec((tile, width), lambda step, core_ref, factor_ref: (step, 0))
+    def row_at(step, at_ref, factor_ref):
+        core = lax.rem(at_ref[0] + step // turns, 2)
+        turn = lax.rem(step, turns)
+        x = lax.rem(at_ref[1] + n_x - (first_step + turn // per_part), n_x)
+        return (core * per_half + x * per_part + lax.rem(turn, per_part), 0)
+
+    def mine_at(step, at_ref, factor_ref):
+        return (jnp.minimum(step, turns - 1), 0)
+
+    def other_at(step, at_ref, factor_ref):
+        return (jnp.maximum(step - turns, 0), 0)
+
+    rows = pl.BlockSpec((tile, width), row_at)
+    done = () if done is None else done
     return pl.pallas_call(
         body,
         grid_spec=pltpu.PrefetchScalarGridSpec(
             num_scalar_prefetch=2,
-            grid=(pl.cdiv(size, tile),),
-            in_specs=[rows, rows, rows, pl.BlockSpec((tile, width), mine_at), pl.BlockSpec((tile, width), other_at)],
-            out_specs=(rows, rows, rows),
+            grid=(2 * turns,),
+            in_specs=[rows, rows, rows, pl.BlockSpec((tile, width), mine_at), pl.BlockSpec((tile, width), other_at)]
+            + [HBM] * len(done),
+            out_specs=(rows, rows, rows, pl.BlockSpec((8, 128), lambda *_: (0, 0))),
         ),
-        out_shape=(jax.ShapeDtypeStruct((size, width), f32),) * 3,
+        out_shape=(jax.ShapeDtypeStruct((size, width), f32),) * 3 + (jax.ShapeDtypeStruct((8, 128), f32),),
+        input_output_aliases={7 + index: index for index in range(len(done))},
         compiler_params=pltpu.CompilerParams(vmem_limit_bytes=56 << 20),
-    )(core.reshape(1), factor.reshape(1), weight, first, second, mine, other)
+        cost_estimate=pl.CostEstimate(
+            flops=40 * turns * tile * width, bytes_accessed=52 * turns * tile * width, transcendentals=0
+        ),
+    )(at, factor.reshape(1), *weights, mine, other, *done)
 
 
 def layer_norm(x, gain, shift):
@@ -581,9 +1328,8 @@
     n_pick = masked.shape[1] // sharers
     row_at = seq_at // sharers
     share = lax.rem(seq_at, sharers)
-    tiles = -(-vocab_part // 1056)
-    tile = -(-vocab_part // (32 * tiles)) * 16
-    half = tiles * tile
+    half = -(-vocab_part // 256) * 128
+    tile = 128 * max(count for count in range(1, 8) if half % (128 * count) == 0)
     n_x = n_seq // 2
     n_y = 1 << (n_dp.bit_length() - 1) // 2
     n_z = n_dp // n_y
@@ -592,29 +1338,65 @@
         piece = weight.shape[0] // n_seq
         return lax.dynamic_slice_in_dim(weight, seq_at * piece, piece, 0).astype(bf16)
 
-    thin = attn_in.shape[0] // n_seq
+    thick = attn_in.shape[0]
     hidden = mlp_in.shape[1]
-
-    def blocks_of(piece):
-        return [piece[:, at : at + model] for at in range(0, piece.shape[1], model)]
-
-    pieces = [piece_of(mlp_out), piece_of(positions)]
-    for weight in (attn_in, attn_out, mlp_in):
-        pieces += blocks_of(piece_of(weight))
+    blocks = 4
+    split = n_seq // blocks
+    thin = thick // split
+
+    def block_of(weights):
+        wide = [weight[:, at : at + model] for weight in weights for at in range(0, weight.shape[1], model)]
+        wide = jnp.stack(wide).reshape(n_seq, thin, model)
+        return lax.dynamic_index_in_dim(wide, seq_at, 0, False).astype(bf16)
+
+    given_rows = [block_of((attn_in, attn_out)), block_of((mlp_in,)), piece_of(mlp_out), piece_of(positions)]
     ends = [0]
-    for piece in pieces:
+    for piece in given_rows:
         ends.append(ends[-1] + piece.shape[0])
-    packed = lax.all_gather(jnp.concatenate(pieces), ("dp", "seq"))
-
-    def unpacked(begin, count):
-        parts = [packed[:, ends[at] : ends[at + 1]].reshape(-1, model) for at in range(begin, begin + count)]
-        return parts[0] if count == 1 else jnp.concatenate(parts, axis=1)
-
-    w_down = unpacked(0, 1)
-    pos_all = unpacked(1, 1)
-    w_in = unpacked(2, 3)
-    w_out = unpacked(5, 1)
-    w_up = unpacked(6, hidden // model)
+    long, some = ends[3] - ends[2], ends[4] - ends[3]
+    packed = lax.all_gather(jnp.concatenate(given_rows), ("dp", "seq")).reshape(n_dp, n_seq, -1, model)
+    if thin % 16 == 0 and some % 16 == 0 and split == 1:
+
+        def rows_at(part):
+            return pl.ds(ends[part], ends[part + 1] - ends[part])
+
+        def blocks_at(part, blocks):
+            return [
+                ((slice(None), block, rows_at(part)), (slice(None), slice(None), pl.ds(at * model, model)))
+                for at, block in enumerate(blocks)
+            ]
+
+        def all_at(part):
+            return [((slice(None), slice(None), rows_at(part)), (slice(None),))]
+
+        weight_pieces = (
+            packed,
+            {
+                "pos": all_at(3),
+                "w_in": blocks_at(0, range(3)),
+                "w_out": blocks_at(0, [3]),
+                "w_up": blocks_at(1, range(4)),
+                "w_down": all_at(2),
+            },
+        )
+
+        def shape(*dims):
+            return jax.ShapeDtypeStruct(dims, bf16)
+
+        pos_all, w_in, w_out = shape(n_dp, n_seq, some, model), shape(n_dp, thick, 3 * model), shape(n_dp, thick, model)
+        w_up, w_down = shape(n_dp, thick, hidden), shape(n_dp, n_seq, long, model)
+    else:
+        weight_pieces = None
+
+        def columns_of(part, block):
+            got = packed[:, block * split : (block + 1) * split, ends[part] : ends[part + 1]]
+            return got.reshape(-1, model)
+
+        w_in = jnp.concatenate([columns_of(0, block) for block in range(3)], axis=1)
+        w_out = columns_of(0, 3)
+        w_up = jnp.concatenate([columns_of(1, block) for block in range(4)], axis=1)
+        w_down = packed[:, :, ends[2] : ends[3]].reshape(hidden, model)
+        pos_all = packed[:, :, ends[3] :].reshape(length, model)
 
     all_rows = deliver(clean_ids, ("seq",), 1)
     row_ids = lax.dynamic_index_in_dim(all_rows, row_at, 1, keepdims=False).reshape(length)
@@ -671,7 +1453,8 @@
     def one_hot(spots, count):
         return (spots[:, None] == jnp.arange(count, dtype=i32)[None, :]).astype(bf16)
 
-    found = jnp.take(table, asks, axis=0).astype(bf16)
+    table_low, table_turned = table_forms(table, 2 * half, tile)
+    found = jnp.take(table_low, asks, axis=0)
     fetched = deliver(found, ("dp",), 3, lambda place: place[0]).reshape(n_dp * FETCH, model)
     embedded = jnp.dot(one_hot(spot, n_dp * FETCH), fetched, preferred_element_type=f32)
 
@@ -679,124 +1462,57 @@
         turn, total = state
         next_spot, next_ask = asked(owner, place, within, n_dp, FETCH, turn)
         wanted = lax.all_to_all(next_ask.reshape(n_dp, FETCH), "dp", 0, 0)
-        sent = jnp.take(table, wanted, axis=0).astype(bf16)
+        sent = jnp.take(table_low, wanted, axis=0)
         got = lax.all_to_all(sent, "dp", 0, 0).reshape(n_dp * FETCH, model)
         return turn + 1, total + jnp.dot(one_hot(next_spot, n_dp * FETCH), got, preferred_element_type=f32)
 
     _, embedded = lax.while_loop(lambda state: state[0] < turns[0], fetch_more, (jnp.int32(1), embedded))
 
-    start = embedded + pos_all.astype(f32)
-    attn_normed, norm_one_back = jax.vjp(layer_norm, start, vectors[0], vectors[1])
-    attn_low = attn_normed.astype(bf16)
-    in_bias = jnp.concatenate([vectors[6], jnp.zeros_like(vectors[6]), vectors[7]])
-    qkv = (jnp.dot(attn_low, w_in, preferred_element_type=f32) + in_bias).astype(bf16)
-    chosen = one_hot(picks - 1, length)
-    query = jnp.dot(chosen, qkv[:, :model], preferred_element_type=f32).astype(bf16)
-    start_picked = jnp.dot(chosen.astype(f32), start, precision=lax.Precision.HIGHEST)
-    q_heads = query.reshape(n_pick, H, head_dim)
-    k_heads = qkv[:, model : 2 * model].reshape(length, H, head_dim)
-    v_heads = qkv[:, 2 * model :].reshape(length, H, head_dim)
-    key_keep = (slot < row_length)[None, None, :]
-    raw = jnp.einsum("shd,khd->hsk", q_heads, k_heads, preferred_element_type=f32) * 0.125
-    scores = jnp.where(key_keep, raw, mask_fill)
-    log_total = jax.nn.logsumexp(scores, axis=-1, keepdims=True)
-    probs = jnp.exp(scores - log_total)
-    probs_low = probs.astype(bf16)
-    mixed = jnp.einsum("hsk,khd->shd", probs_low, v_heads, preferred_element_type=f32)
-    mixed = mixed.reshape(n_pick, model).astype(bf16)
-    after_attn = start_picked + jnp.dot(mixed, w_out, preferred_element_type=f32) + vectors[8]
-    mlp_normed, norm_two_back = jax.vjp(layer_norm, after_attn, vectors[2], vectors[3])
-    mlp_low = mlp_normed.astype(bf16)
-    up_pre = jnp.dot(mlp_low, w_up, preferred_element_type=f32) + vectors[10:14].reshape(-1)
-    activated, gelu_back = jax.vjp(gelu_fn, up_pre)
-    act_low = activated.astype(bf16)
-    final_in = after_attn + jnp.dot(act_low, w_down, preferred_element_type=f32) + vectors[9]
-    final_normed, norm_end_back = jax.vjp(layer_norm, final_in, vectors[4], vectors[5])
-    sources = final_normed.astype(bf16)
-
-    table_low = table.astype(bf16)
-    heads = deliver(sources, ("dp",), 9).reshape(n_dp * n_pick, model)
-    logits = jnp.einsum("nd,vd->nv", heads, table_low, preferred_element_type=f32)
-    flat_targets = all_targets.reshape(-1) - dp_at * vocab_part
+    embedded = embedded.astype(bf16)
+    kept = layer_forward(
+        embedded, pos_all, w_in, w_out, w_up, w_down, vectors, picks, row_length, weight_pieces
+    )
+    sources = kept["f"]
+
+    flat_targets = (all_targets - dp_at * vocab_part).reshape(n_dp, 1, n_pick)
+    flat_targets = jnp.where(flat_targets < vocab_part, flat_targets, -1)
     rows_here = valid_all.reshape(n_dp, rows, sharers, n_pick)
     rows_here = lax.dynamic_index_in_dim(rows_here, row_at, 1, False)
-    flat_valid = lax.dynamic_index_in_dim(rows_here, share, 1, False).reshape(-1)
-    hit_mask = flat_targets[:, None] == jnp.arange(vocab_part, dtype=i32)[None, :]
-    part_max = jnp.max(logits, axis=1)
-    part_sum = jnp.sum(jnp.exp(logits - part_max[:, None]), axis=1)
-    part_hit = jnp.sum(jnp.where(hit_mask, logits, 0.0), axis=1)
-    stats = jnp.stack([part_max, part_sum, part_hit]).reshape(3, -1, 128)
-    stats = deliver(stats, ("dp",), 5).reshape(n_dp, 3, -1)
-    top = jnp.max(stats[:, 0], axis=0)
-    summed = jnp.sum(stats[:, 1] * jnp.exp(stats[:, 0] - top[None]), axis=0)
-    log_norm = top + jnp.log(summed)
-    loss_group = jnp.sum(flat_valid * (log_norm - jnp.sum(stats[:, 2], axis=0)))
-    logit_grad = (
-        (flat_valid / masked_count)[:, None]
-        * (jnp.exp(logits - log_norm[:, None]) - hit_mask.astype(f32))
-    ).astype(bf16)
-    table_grad = jnp.einsum("nv,nd->vd", logit_grad, heads, preferred_element_type=f32)
-    table_grad = jnp.pad(table_grad, ((0, 2 * half - vocab_part), (0, 0)))
-    half_own = lax.dynamic_slice_in_dim(table_grad, core * half, half, 0)
-    half_other = lax.dynamic_slice_in_dim(table_grad, (1 - core) * half, half, 0).astype(bf16)
-    logit_grad, half_other = lax.optimization_barrier((logit_grad, half_other))
-    half_low = (half_own + from_peer(half_other, "seq", 1, 2, 1).astype(f32)).astype(bf16)
-    heads_grad = jnp.dot(logit_grad, table_low, preferred_element_type=f32).astype(bf16)
-    heads_grad, half_low = lax.optimization_barrier((heads_grad, half_low))
-    if n_x == 2:
-        half_across = from_peer(half_low, "seq", 2, 2, 1)
-    else:
-        groups = [list(range(at, n_seq, 2)) for at in range(2)]
-        half_low = jnp.sum(lax.all_gather(half_low, "seq", axis_index_groups=groups).astype(f32), axis=0)
-        half_across = jnp.zeros_like(half_low)
-    final_grad = heads_grad.reshape(n_dp, n_pick, model)
-    final_own = lax.dynamic_index_in_dim(final_grad, dp_at, 0, False).astype(f32)
-    for step in range(1, n_dp):
-        block = lax.dynamic_index_in_dim(final_grad, lax.rem(dp_at + step, n_dp), 0, False)
-        final_own = final_own + from_peer(block, "dp", 1, n_dp, step).astype(f32)
-    final_grad = final_own
-
-    final_in_grad, gain_end, shift_end = norm_end_back(final_grad)
-    down_grad = final_in_grad.astype(bf16)
-    w_down_grad = jnp.einsum("sf,sd->fd", act_low, down_grad, preferred_element_type=f32)
-    down_bias = jnp.sum(down_grad.astype(f32), axis=0)
-    act_grad = jnp.einsum("sd,fd->sf", down_grad, w_down, preferred_element_type=f32)
-    up_grad = gelu_back(act_grad)[0].astype(bf16)
-    up_bias = jnp.sum(up_grad.astype(f32), axis=0)
-    w_up_grad = jnp.einsum("sd,sf->df", mlp_low, up_grad, preferred_element_type=f32)
-    mlp_grad = jnp.einsum("sf,df->sd", up_grad, w_up, preferred_element_type=f32)
-    attn_res_grad, gain_two, shift_two = norm_two_back(mlp_grad)
-    after_grad = final_in_grad + attn_res_grad
-    out_grad = after_grad.astype(bf16)
-    out_bias = jnp.sum(out_grad.astype(f32), axis=0)
-    w_out_grad = jnp.einsum("se,sd->ed", mixed, out_grad, preferred_element_type=f32)
-    mixed_grad = jnp.einsum("sd,ed->se", out_grad, w_out, preferred_element_type=f32).astype(bf16)
-    mixed_grad = mixed_grad.reshape(n_pick, H, head_dim)
-    prob_grad = jnp.einsum("shd,khd->hsk", mixed_grad, v_heads, preferred_element_type=f32)
-    correction = jnp.sum(prob_grad * probs, axis=-1, keepdims=True)
-    score_grad = (probs * (prob_grad - correction)).astype(bf16)
-    query_grad = jnp.einsum("hsk,khd->shd", score_grad, k_heads, preferred_element_type=f32) * 0.125
-    key_grad = jnp.einsum("hsk,shd->khd", score_grad, q_heads, preferred_element_type=f32) * 0.125
-    value_grad = jnp.einsum("hsk,shd->khd", probs_low, mixed_grad, preferred_element_type=f32)
-    query_grad = query_grad.reshape(n_pick, model).astype(bf16)
-    query_full = jnp.einsum("st,sd->td", chosen, query_grad, preferred_element_type=f32).astype(bf16)
-    qkv_grad = jnp.concatenate(
-        [
-            query_full,
-            key_grad.reshape(length, model).astype(bf16),
-            value_grad.reshape(length, model).astype(bf16),
-        ],
-        axis=-1,
+    flat_valid = lax.dynamic_index_in_dim(rows_here, share, 1, False).reshape(n_dp, 1, n_pick)
+    grown, heads, tops, stats = read_heads(
+        sources, table_low, flat_targets, vocab_part, tile, n_y, n_z, 9
     )
-    qkv_bias = jnp.sum(qkv_grad.astype(f32), axis=0)
-    w_in_grad = jnp.einsum("sd,se->de", attn_low, qkv_grad, preferred_element_type=f32)
-    normed_grad = jnp.einsum("se,de->sd", qkv_grad, w_in, preferred_element_type=f32)
-    start_extra, gain_one, shift_one = norm_one_back(normed_grad)
-    after_full = jnp.einsum(
-        "st,sd->td", chosen.astype(f32), after_grad, precision=lax.Precision.HIGHEST
+    final_grad, half_low, logs = write_heads(
+        grown, heads, table_turned, tops, stats, flat_targets, flat_valid / masked_count, tile, 5
     )
-    start_grad = after_full + start_extra
-    start_grad_low = start_grad.astype(bf16)
+    loss_group = jnp.sum(flat_valid * (logs[0] - logs[1]))
+    final_grad = jnp.sum(final_grad.astype(f32), axis=0).T
+    half_low = half_low.reshape(half, model)
+    part = half // n_x
+    slab = 16 * max(count for count in range(1, 26) if part % (16 * count) == 0)
+    x_at = seq_at // 2
+
+    def part_of(step):
+        return lax.dynamic_slice_in_dim(half_low, lax.rem(x_at + step, n_x) * part, part, 0)
+
+    part_came = [from_peer(part_of(step), "seq", 2, n_x, step) for step in range(1, n_x)]
+    if n_x > 2:
+        part_came = [sum(came.astype(f32) for came in part_came).astype(bf16)]
+
+    whole, vec_grad, start_grad_low, first_given = layer_backward(
+        final_grad,
+        kept,
+        embedded,
+        pos_all,
+        (w_in, w_out, w_up, w_down),
+        vectors,
+        picks,
+        (spot_half, 2 * n_dp * GIVE),
+        row_length,
+        loss_group,
+        n_dp,
+        weight_pieces,
+    )
 
     def given(spots):
         summed_ids = jnp.einsum(
@@ -804,59 +1520,41 @@
         )
         return summed_ids.astype(bf16).reshape(2 * n_dp, GIVE, model)
 
-    vec_grad = jnp.concatenate(
-        [
-            jnp.stack(
-                [
-                    gain_one,
-                    shift_one,
-                    gain_two,
-                    shift_two,
-                    gain_end,
-                    shift_end,
-                    qkv_bias[:model],
-                    qkv_bias[2 * model :],
-                    out_bias,
-                    down_bias,
-                ]
-            ),
-            up_bias.reshape(-1, model),
-            jnp.full((1, model), loss_group),
-            jnp.zeros((1, model), f32),
-        ],
-        axis=0,
+    chunks = 4
+    layer_piece, came, vec_total = settle(
+        whole.reshape(n_dp, 2, n_x, chunks, -1, model),
+        first_given.reshape(2 * n_dp, GIVE, model),
+        vec_grad,
+        n_x,
+        n_y,
+        n_z,
+        7,
     )
-
-    def columns(grad):
-        return [part.astype(bf16).reshape(n_dp, -1, model) for part in blocks_of(grad)]
-
-    layer_parts = [w_down_grad, start_grad, w_in_grad, w_out_grad, w_up_grad]
-    whole = jnp.concatenate([part for grad in layer_parts for part in columns(grad)], axis=1)
-    chunks = 4
-    layer_sum, came, vec_total = settle(
-        whole.reshape(n_dp, 2, n_x, chunks, -1, model), given(spot_half), vec_grad, n_x, n_y, n_z, 7
-    )
+    layer_piece = layer_piece.reshape(-1, model)
+
     def give_more(state):
         turn, total, _ = state
         next_spot, next_ask = asked(owner_half, place_half, within_half, 2 * n_dp, GIVE, turn)
         names = lax.all_gather(next_ask.reshape(2 * n_dp, GIVE), ("dp", "seq"))
-        names = lax.dynamic_index_in_dim(names, half_at, 1, False).reshape(1, -1)
+        names = lax.dynamic_index_in_dim(names, half_at, 1, False).reshape(1, -1) - x_at * part
         sent = given(next_spot).reshape(n_dp, 1, 2, GIVE, model)
         sent = jnp.broadcast_to(sent, (n_dp, n_x, 2, GIVE, model)).reshape(-1, GIVE, model)
         got = lax.all_to_all(sent, ("dp", "seq"), 0, 0).reshape(-1, model)
-        total, squares = close_half(total, jnp.zeros_like(total), names, got, tile)
+        total, squares = close_half(
+            total, jnp.zeros_like(total), names, got, layer_piece, slab
+        )
         return turn + 1, total, jnp.sum(squares)
 
-    names = asks_half.reshape(1, -1)
+    names = asks_half.reshape(1, -1) - x_at * part
     values = came.reshape(-1, model)
-    half_own, squares_own = close_half(half_low, half_across, names, values, tile)
-    half_square = jnp.sum(squares_own)
-
-    _, half_own, half_square = lax.while_loop(
-        lambda state: state[0] < turns[1], give_more, (jnp.int32(1), half_own, half_square)
+    part_own, squares_own = close_half(
+        part_of(0), part_came[0], names, values, layer_piece, slab
     )
-    layer_sum = layer_sum.reshape(-1, model).astype(f32)
-    layer_square = jnp.sum(layer_sum * layer_sum)
+    _, part_own, part_square = lax.while_loop(
+        lambda state: state[0] < turns[1], give_more, (jnp.int32(1), part_own, jnp.sum(squares_own))
+    )
+    layer_sum = group_join(layer_piece, 0, "seq", 2, n_x).reshape(-1, model)
+    layer_sum = group_join(layer_sum, 0, "seq", 1, 2).reshape(-1, model).astype(f32)
     loss_sum = vec_total[14, 0] / n_dp
     vec_total = vec_total[:14]
 
@@ -864,14 +1562,17 @@
         return jnp.concatenate(jnp.split(rows_of, count, axis=0), axis=1)
 
     ends = [0]
-    for grad in layer_parts:
-        ends.append(ends[-1] + grad.shape[0] * grad.shape[1] // (model * n_dp))
-    g_down, g_pos, g_in, g_out, g_up = [layer_sum[begin:end] for begin, end in zip(ends, ends[1:])]
+    for count in (mlp_out.shape[0], hidden // model * thick, thick, 3 * thick, positions.shape[0]):
+        ends.append(ends[-1] + count)
+    g_down, g_up, g_out, g_in, g_pos = [layer_sum[begin:end] for begin, end in zip(ends, ends[1:])]
     g_in = side_by_side(g_in, 3)
     g_up = side_by_side(g_up, hidden // model)
-    half_other = from_peer(half_own, "seq", 1, 2, 1)
-    said = jnp.full((8, 128), half_square / n_x + layer_square / n_seq)
+    said = jnp.full((8, 128), part_square)
     square_total = jnp.sum(deliver(said, ("dp", "seq"), 8)[:, 0, 0])
+    part_own, square_total = lax.optimization_barrier((part_own, square_total))
+    far_own = [from_peer(part_own, "seq", 2, n_x, step) for step in range(1, n_x)]
+    far_own = far_own[0] if n_x == 2 else jnp.concatenate(far_own)
+    part_pair = from_peer(part_own, "seq", 1, 2, 1)
     grad_norm = jnp.sqrt(square_total + jnp.sum(vec_total * vec_total))
     factor = clip_at / jnp.maximum(grad_norm, clip_at)
     weights = (attn_in, attn_out, mlp_in, mlp_out, table, positions, vectors)
@@ -898,8 +1599,14 @@
     for index in range(7):
         rate, decay = (1.0, 0.0) if index == 6 else (0.1, 0.1)
         if index == 4:
-            new_w, new_m, new_v = adam_table(
-                core, factor, table, first_table, second_table, half_own, half_other, tile
+            state = (table, first_table, second_table)
+            at = jnp.stack([core, x_at])
+            *near, token = adam_table(at, factor, state, part_own, part_pair, slab, half, n_x, (0,), None)
+            far_own = far_own + token[0, 0].astype(bf16)
+            far_pair = from_peer(far_own, "seq", 1, 2, 1)
+            far_steps = tuple(range(1, n_x))
+            new_w, new_m, new_v, _ = adam_table(
+                at, factor, state, far_own, far_pair, slab, half, n_x, far_steps, near
             )
         else:
             new_w, new_m, new_v = adam_update(

time: 871 us -> 700 us (0.80)
  Pallas kernels: 366 us -> 526 us
  matrix products: 158 us -> 4.45 us
  other arithmetic: 134 us -> 44 us
  local copies, waits for them, and re-layouts: 86.6 us -> 38.5 us
  starting transfers between devices: 24.5 us -> 4.57 us
  waiting for transfers between devices: 63.9 us -> 47.5 us
    pallas_call x2 -> x7, Pallas kernels: 150 us -> 396 us  [the longest x1 150 us: settle(): pl.pallas_call(body, out_shape=(jax.ShapeDtypeStruct((chunks, height, wid...]
    dot_general x26 -> x0, matrix products: 154 us -> none  [the longest x1 31.6 us: on_device(): jnp.einsum('nd,vd->nv', heads, table_low, preferred_element_type=f32)]
    pallas_call x6 -> x4, Pallas kernels: 170 us -> 78.4 us  [deliver(): pl.pallas_call(body, out_shape=jax.ShapeDtypeStruct((count,) + block, x.d...]
    reduce_sum x18 -> x3, other arithmetic: 44.1 us -> 1.67 us  [the longest x1 0.62 us: on_device(): loss_group = jnp.sum(flat_valid * (logs[0] - logs[1]))]
    convert_element_type x6 -> x3, other arithmetic: 47.6 us -> 5.78 us  [the longest x1 3.25 us: on_device(): embedded = embedded.astype(bf16)]
    slice x11 -> x1, local copies, waits for them, and re-layouts: 23.4 us -> 0.51 us  [on_device(): far_own = far_own + token[0, 0].astype(bf16)]
    unnamed x263 -> x61, local copies, waits for them, and re-layouts: 31.2 us -> 10.4 us
    ppermute x10 -> x6, starting transfers between devices: 24.4 us -> 4.53 us  [from_peer(): return lax.ppermute(x, axis, pairs)]
  transfers between devices with their start and end apart: 11 -> 7, of which waited for: 4 -> 3; matrix products, arithmetic and copies ran while one was open for 21% -> 9% of each run, Pallas kernels for 26% -> 47%
where the time goes in v3:
time: 700 us; the launch traced here: 691 us
  Pallas kernels  526 us (75%)
  waiting for transfers between devices  47.5 us (7%)
  other arithmetic  44 us (6%)
  local copies, waits for them, and re-layouts  38.5 us (6%)
  between operations  24 us (3%)
    pallas_call x1, Pallas kernels, settle(): pl.pallas_call(body, out_shape=(jax.ShapeDtypeStruct((chunks, height, wid...  150 us
    pallas_call x2, Pallas kernels, staged(): pl.pallas_call(body, out_shape=tuple(outs.values()), in_specs=[HBM] * (le...  84.6 us
    pallas_call x4, Pallas kernels, deliver(): pl.pallas_call(body, out_shape=jax.ShapeDtypeStruct((count,) + block, x.d...  78.4 us
    pallas_call x1, Pallas kernels, read_heads(): pl.pallas_call(body, out_shape=(jax.ShapeDtypeStruct((n_dp, size, n_pick)...  76.3 us
    pallas_call x1, Pallas kernels, write_heads(): pl.pallas_call(body, out_shape=(jax.ShapeDtypeStruct((n_dp, width, n_pick...  61.2 us
    pallas_call x2, Pallas kernels, adam_table(): pl.pallas_call(body, grid_spec=pltpu.PrefetchScalarGridSpec(num_scalar_pr...  52.1 us
    ppermute x6, waiting for transfers between devices, from_peer(): return lax.ppermute(x, axis, pairs)  30 us
    all_gather x1, waiting for transfers between devices, on_device(): lax.all_gather(jnp.concatenate(given_rows), ('dp', 'seq'))  17.5 us
  transfers between devices with their start and end apart: 7, of which 3 were waited for; matrix products, arithmetic and copies ran while one was open for 9% of the time, Pallas kernels for 47%

profile of v3, /device:TPU:0, one launch (start us, length us, event | category | flops | bytes accessed | tf_op | source)
XLA Modules:
  0.0 690.7 jit_solution(800134120979555741)
XLA Ops:
  12.8 5.0 shard_map.415
  32.0 16.7 %shard_map.416 = s32[32,32,128]{2,1,0:T(8,128)} custom-call(s32[32,128]{1,0:T(8,128)} %pad_add_fusion.x_ref), custom_call_target="tpu_custom_call" | custom-call | tf_op jit(solution)/shard_map/pallas_call | solution.py:88
  50.1 13.6 %shard_map.417 = (bf16[6400,768]{1,0:T(8,128)(2,1)}, bf16[768,6400]{1,0:T(8,128)(2,1)S(1)}) custom-call(f32[6288,768]{1,0:T(8,128)} %w_ref.3), custom_call_target="tpu_custom_call" | custom-call | tf_op jit(solution)/shard_map/pallas_call | solution.py:1155
  63.8 3.9 copy-done
  67.7 8.4 %gather_fusion.1 = bf16[768,768]{1,0:T(8,128)(2,1)S(1)} fusion(bf16[6400,768]{1,0:T(8,128)(2,1)} %get-tuple-element.752.t_ref, s32[1024]{0:T(1024)S(1)} %pad_clamp_fusion.1), kind=kCustom, calls=%fused_computation.1 | custom fusion | bytes 2362368 | tf_op jit(solution)/shard_map/jit(_take)/gather | solution.py:1457
  77.3 45.5 %shard_map.418 = bf16[8,96,768]{2,1,0:T(8,128)(2,1)} custom-call(bf16[8,96,768]{2,1,0:T(8,128)(2,1)} %broadcast_select_fusion.1.x_ref), custom_call_target="tpu_custom_call" | custom-call | tf_op jit(solution)/shard_map/pallas_call | solution.py:88
  123.4 4.5 fusion.18
  128.8 3.2 convert_element_type.82.refs_1_.refs_14_
  136.1 17.5 %all-gather.3.cloned.1.call-done = bf16[10240,768]{1,0:T(8,128)(2,1)} async-done(((bf16[320,768]{1,0:T(8,128)(2,1)}), bf16[10240,768]{1,0:T(8,128)(2,1)}) %all-gather.3.cloned.1.call-update) | async-done | bytes 15728656 | tf_op jit(solution)/shard_map/all_gather | solution.py:1357
  154.1 35.6 %shard_map.419 = (bf16[1024,768]{1,0:T(8,128)(2,1)}, bf16[1024,768]{1,0:T(8,128)(2,1)}, bf16[1024,768]{1,0:T(8,128)(2,1)}, bf16[256,768]{1,0:T(8,128)(2,1)}, f32...) custom-call(bf16[8,4,320,768]{3,2,1,0:T(8,128)(2,1)} %bitcast.145, ...), custom_call_target="tpu_custom_call" | custom-call | tf_op jit(solution)/shard_map/pallas_call | solution.py:832
  189.7 76.3 %shard_map.420 = (bf16[8,6400,256]{2,1,0:T(8,128)(2,1)}, bf16[8,256,768]{2,1,0:T(8,128)(2,1)}, f32[8,10,8,256]{3,2,1,0:T(8,128)}, f32[8,8,8,256]{3,2,1,0:T(8,128)}) custom-call(bf16[256,768]{1,0:T(8,128)(2,1)} %get-tuple-element.410.s_ref, bf16[6400,768]{1,0:T(8,128)(2,1)} %get-tuple-element.834, s32[8,1,256]{2,1,0:T(1,128)} %compare_select_fusion.3.target_ref), custom_call_target="tpu_custom_call" | custom-call | tf_op jit(solution)/shard_map/pallas_call | solution.py:562
  266.0 61.2 %shard_map.421 = (bf16[8,768,256]{2,1,0:T(8,128)(2,1)}, bf16[5,640,768]{2,1,0:T(8,128)(2,1)}, f32[2,8,1,256]{3,2,1,0:T(1,128)}) custom-call(bf16[8,6400,256]{2,1,0:T(8,128)(2,1)} %get-tuple-element.411.e_ref, bf16[2048,768]{1,0:T(8,128)(2,1)} %bitcast.154, bf16[768,6400]{1,0:T(8,128)(2,1)} %copy-done, f32[8,10,8,256]{3,2,1,0:T(8,128)} %get-tuple-element.414.m_ref, ...), custom_call_target="tpu_custom_call" | custom-call | tf_op jit(solution)/shard_map/pallas_call | solution.py:736
  327.2 5.2 constant_dynamic-slice_fusion.1
  332.4 3.8 collective-permute-start.2
  340.3 49.1 %shard_map.422 = (bf16[8,1280,768]{2,1,0:T(8,128)(2,1)}, f32[16,768]{1,0:T(8,128)}, bf16[1024,768]{1,0:T(8,128)(2,1)}, bf16[1024,768]{1,0:T(8,128)(2,1)}) custom-call(bf16[8,4,320,768]{3,2,1,0:T(8,128)(2,1)} %bitcast.146, f32[256,768]{1,0:T(8,128)} %get-tuple-element.409.refs_1_, f32[256,768]{1,0:T(8,128)} %bitcast.153, ...), custom_call_target="tpu_custom_call" | custom-call | tf_op jit(solution)/shard_map/pallas_call | solution.py:832
  391.5 150.2 %shard_map.423 = (bf16[4,80,768]{2,1,0:T(8,128)(2,1)}, bf16[32,64,768]{2,1,0:T(8,128)(2,1)S(1)}, f32[16,768]{1,0:T(8,128)S(1)}) custom-call(bf16[8,2,2,4,80,768]{5,4,3,2,1,0:T(8,128)(2,1)} %bitcast.149, bf16[16,64,768]{2,1,0:T(8,128)(2,1)S(1)} %bitcast.142, f32[16,768]{1,0:T(8,128)S(1)} %copy-done.3), custom_call_target="tpu_custom_call" | custom-call | tf_op jit(solution)/shard_map/pallas_call | solution.py:382
  543.7 12.7 %collective-permute-done = bf16[320,768]{1,0:T(8,128)(2,1)S(1)} collective-permute-done((bf16[320,768]{1,0:T(8,128)(2,1)}, bf16[320,768]{1,0:T(8,128)(2,1)S(1)}, u32[]{:S(2)}, u32[]{:S(2)}) %collective-permute-start) | collective-permute-done | bytes 491552 | tf_op jit(solution)/shard_map/ppermute | solution.py:107
  557.7 9.6 %shard_map.424 = (bf16[1600,768]{1,0:T(8,128)(2,1)}, f32[1,768]{1,0:T(1,128)S(1)}) custom-call(bf16[1600,768]{1,0:T(8,128)(2,1)S(1)} %copy-done.1, bf16[1600,768]{1,0:T(8,128)(2,1)} %collective-permute-done.2.other_ref, s32[1,2048]{1,0:T(1,128)S(1)} %sub.144.names_ref, bf16[2048,768]{1,0:T(8,128)(2,1)} %bitcast.143, bf16[320,768]{1,0:T(8,128)(2,1)} %bitcast.47.layer_ref), custom_call_target="tpu_custom_call" | custom-call | flops 5033164800 | bytes 9830400 | tf_op jit(solution)/shard_map/pallas_call | solution.py:1198
  571.0 11.1 %shard_map.425 = f32[32,8,128]{2,1,0:T(8,128)} custom-call(f32[8,128]{1,0:T(8,128)} %broadcast_in_dim.226.x_ref), custom_call_target="tpu_custom_call" | custom-call | tf_op jit(solution)/shard_map/pallas_call | solution.py:88
  591.9 3.1 fusion.53
  595.0 26.1 %shard_map.426 = (f32[6288,768]{1,0:T(8,128)}, f32[6288,768]{1,0:T(8,128)}, f32[6288,768]{1,0:T(8,128)}, f32[8,128]{1,0:T(8,128)}) custom-call(s32[2]{0:T(128)} %pad_add_fusion.2.at_ref, f32[1]{0:T(128)} %bitcast.61.factor_ref, f32[6288,768]{1,0:T(8,128)} %w_ref.3, f32[6288,768]{1,0:T(8,128)} %m_ref.3, f32[6288,768]{1,0:T(8,128)} %v_ref.3, ...), custom_call_target="tpu_custom_call" | custom-call | flops 49152000 | bytes 63897600 | tf_op jit(solution)/shard_map/pallas_call | solution.py:1247
  622.3 17.3 %collective-permute-done.3 = bf16[1600,768]{1,0:T(8,128)(2,1)S(1)} collective-permute-done((bf16[1600,768]{1,0:T(8,128)(2,1)}, bf16[1600,768]{1,0:T(8,128)(2,1)S(1)}, u32[]{:S(2)}, u32[]{:S(2)}) %collective-permute-start.3) | collective-permute-done | bytes 2457632 | tf_op jit(solution)/shard_map/ppermute | solution.py:107
  644.5 3.8 multiply_subtract_fusion
  655.2 26.0 %shard_map.427 = (f32[6288,768]{1,0:T(8,128)}, f32[6288,768]{1,0:T(8,128)}, f32[6288,768]{1,0:T(8,128)}, f32[8,128]{1,0:T(8,128)}) custom-call(s32[2]{0:T(128)} %pad_add_fusion.2.at_ref, f32[1]{0:T(128)} %bitcast.61.factor_ref, f32[6288,768]{1,0:T(8,128)} %w_ref.3, f32[6288,768]{1,0:T(8,128)} %m_ref.3, ...), custom_call_target="tpu_custom_call", output_to_operand_aliasing={{0}: (7, {}), {1}: (8, {}), {2}: (9, {})} | custom-call | flops 49152000 | bytes 63897600 | tf_op jit(solution)/shard_map/pallas_call | solution.py:1247
  (145 shorter events, 58.5 us)
Async XLA Ops:
  7.2 4.5 copy-start.12
  7.2 146.3 %all-gather.3.cloned.1.call-start = ((), (), s32[]{:S(2)}) async-start(), calls=%async_computation.3 | async-start | bytes 16220160 | tf_op jit(solution)/shard_map/all_gather | solution.py:1357
  11.7 6.2 copy-start.25
  17.9 45.9 %copy-start.26 = (s32[1,256]{1,0:T(1,128)}, s32[1,256]{1,0:T(1,128)S(1)}, u32[]{:S(2)}) copy-start(s32[1,256]{1,0:T(1,128)S(1)} %constant_dynamic-slice_fusion.6.refs_18_) | copy-start | bytes 3076
  63.8 3.9 copy-start
  128.8 3.3 copy-start.28
  327.2 9.6 %copy-start.7 = (bf16[8,768,256]{2,1,0:T(8,128)(2,1)S(1)}, bf16[8,768,256]{2,1,0:T(8,128)(2,1)}, u32[]{:S(2)}) copy-start(bf16[8,768,256]{2,1,0:T(8,128)(2,1)} %get-tuple-element.416) | copy-start | bytes 9437188
  332.4 225.3 %collective-permute-start.2 = (bf16[1600,768]{1,0:T(8,128)(2,1)}, bf16[1600,768]{1,0:T(8,128)(2,1)}, u32[]{:S(2)}, u32[]{:S(2)}) collective-permute-start(bf16[1600,768]{1,0:T(8,128)(2,1)} %get-tuple-element.529), channel_id=1, source_target_pairs={{0,2},{1,3},{2,0},{3,1},{4,6},{5,7},{6,4},{7,5},{8,10},{9,11},{10,... | collective-permute-start | bytes 7372808 | tf_op jit(solution)/shard_map/ppermute | solution.py:107
  543.4 12.9 %collective-permute-start = (bf16[320,768]{1,0:T(8,128)(2,1)}, bf16[320,768]{1,0:T(8,128)(2,1)S(1)}, u32[]{:S(2)}, u32[]{:S(2)}) collective-permute-start(bf16[320,768]{1,0:T(8,128)(2,1)} %bitcast.47.layer_ref), channel_id=1, source_target_pairs={{0,2},{1,3},{2,0},{3,1},{4,6},{5,7},{6,4},{7,5},{8,10},{9,11},{10,... | collective-permute-start | bytes 1474568 | tf_op jit(solution)/shard_map/ppermute | solution.py:107
  543.7 14.0 %copy-start.1 = (bf16[1600,768]{1,0:T(8,128)(2,1)S(1)}, bf16[1600,768]{1,0:T(8,128)(2,1)}, u32[]{:S(2)}) copy-start(bf16[1600,768]{1,0:T(8,128)(2,1)} %get-tuple-element.530.own_ref) | copy-start | bytes 7372804
  557.6 29.1 %collective-permute-start.1 = (bf16[640,768]{1,0:T(8,128)(2,1)S(1)}, bf16[640,768]{1,0:T(8,128)(2,1)}, u32[]{:S(2)}, u32[]{:S(2)}) collective-permute-start(bf16[640,768]{1,0:T(8,128)(2,1)S(1)} %bitcast.152), channel_id=1, source_target_pairs={{0,1},{1,0},{2,3},{3,2},{4,5},{5,4},{6,7},{7,6},{8,9},{9,8},{10,11... | collective-permute-start | bytes 2949128 | tf_op jit(solution)/shard_map/ppermute | solution.py:107
  583.7 11.3 %collective-permute-start.4 = (bf16[1600,768]{1,0:T(8,128)(2,1)}, bf16[1600,768]{1,0:T(8,128)(2,1)}, u32[]{:S(2)}, u32[]{:S(2)}) collective-permute-start(bf16[1600,768]{1,0:T(8,128)(2,1)} %get-tuple-element.439.mine_ref), channel_id=1, source_target_pairs={{0,1},{1,0},{2,3},{3,2},{4,5},{5,4},{6,7},{7,6},{8,9},{9,8},{10,11... | collective-permute-start | bytes 7372808 | tf_op jit(solution)/shard_map/ppermute | solution.py:107
  583.7 56.0 %collective-permute-start.3 = (bf16[1600,768]{1,0:T(8,128)(2,1)}, bf16[1600,768]{1,0:T(8,128)(2,1)S(1)}, u32[]{:S(2)}, u32[]{:S(2)}) collective-permute-start(bf16[1600,768]{1,0:T(8,128)(2,1)} %get-tuple-element.439.mine_ref), channel_id=1, source_target_pairs={{0,2},{1,3},{2,0},{3,1},{4,6},{5,7},{6,4},{7,5},{8,10},{9,11},{10,... | collective-permute-start | bytes 7372808 | tf_op jit(solution)/shard_map/ppermute | solution.py:107
  591.9 3.1 copy-start.5
  639.7 4.8 copy-start.14
  640.6 7.7 %copy-start.6 = (bf16[1600,768]{1,0:T(8,128)(2,1)}, bf16[1600,768]{1,0:T(8,128)(2,1)S(1)}, u32[]{:S(2)}) copy-start(bf16[1600,768]{1,0:T(8,128)(2,1)S(1)} %broadcast_add_fusion.mine_ref) | copy-start | bytes 7372804
  640.7 3.8 copy-start.11
  640.7 3.8 copy-start.13
  640.7 13.1 %collective-permute-start.5 = (bf16[1600,768]{1,0:T(8,128)(2,1)S(1)}, bf16[1600,768]{1,0:T(8,128)(2,1)S(1)}, u32[]{:S(2)}, u32[]{:S(2)}) collective-permute-start(bf16[1600,768]{1,0:T(8,128)(2,1)S(1)} %broadcast_add_fusion.mine_ref), channel_id=1, source_target_pairs={{0,1},{1,0},{2,3},{3,2},{4,5},{5,4},{6,7},{7,6},{8,9},{9,8},{10,11... | collective-permute-start | bytes 7372808 | tf_op jit(solution)/shard_map/ppermute | solution.py:107
  644.5 3.9 copy-start.10
  644.5 3.8 copy-start.17
  644.5 3.8 copy-start.18
  648.4 2.6 copy-start.15
  648.4 2.9 copy-start.16
  (12 other events, 17.3 us)
Sparse Core Ops, SparseCore 0:
  12.9 140.5 all-gather.2

commit v4 on v3

--- a/solution.py
+++ b/solution.py
@@ -141,7 +141,8 @@
         v_core, v_x, v_y, v_z = scratch[5:9]
         core_out, core_in, core_own = scratch[9:12]
         one_out, one_in, two_out, two_in, three_out, three_in = scratch[12:18]
-        last_own, e_out, e_in, far_out, far_in, v_out, v_in, side_own = scratch[18:]
+        x_out, x_in, pair_out, pair_in, last_own = scratch[18:23]
+        e_out, e_in, far_out, far_in, v_out, v_in, side_own = scratch[23:]
         dp_at, seq_at = lax.axis_index("dp"), lax.axis_index("seq")
         x_at, c_at = seq_at // 2, lax.rem(seq_at, 2)
         z_at, y_at = dp_at // n_y, lax.rem(dp_at, n_y)
@@ -163,7 +164,7 @@
             pl.semaphore_signal(barrier, inc=1, device_id=peer, device_id_type=MESH)
 
         def x_first(chunk):
-            return chunk % 2 == 0
+            return chunk % 2 == 1
 
         def order(chunk):
             return (n_x, x_at, n_y, y_at) if x_first(chunk) else (n_y, y_at, n_x, x_at)
@@ -360,9 +361,30 @@
             for step in range(1, n_z):
                 total = total + third[chunk, step - 1].astype(f32)
             own[chunk, here] = total.astype(bf16)
-            copy = pltpu.make_async_copy(own.at[chunk, here], o_ref.at[chunk], last_own.at[chunk])
+            result = o_ref.at[c_at, x_at, chunk]
+            copy = pltpu.make_async_copy(own.at[chunk, here], result, last_own.at[chunk])
             copy.start()
             kept[0, chunk] = copy
+            for step in range(1, n_x):
+                to = lax.rem(x_at + step, n_x)
+                kept[4, chunk, step] = send(
+                    own.at[chunk, here],
+                    result,
+                    x_out.at[chunk, step - 1],
+                    x_in.at[chunk, step - 1],
+                    {"seq": to * 2 + c_at},
+                )
+            kept[5, chunk, 0] = send(
+                own.at[chunk, here], result, pair_out.at[chunk, 0], pair_in.at[chunk, 0], partner
+            )
+        for chunk in range(chunks):
+            for step in range(1, n_x):
+                kept[4, chunk, step].wait_recv()
+                origin = lax.rem(x_at + n_x - step, n_x)
+                piece = o_ref.at[c_at, origin, chunk]
+                kept[5, chunk, step] = send(
+                    piece, piece, pair_out.at[chunk, step], pair_in.at[chunk, step], partner
+                )
 
         @pl.loop(0, near)
         def _(step):
@@ -371,8 +393,10 @@
 
         for chunk in range(chunks):
             kept[0, chunk].wait()
+            for step in range(n_x):
+                kept[5, chunk, step].wait()
         for key, copy in kept.items():
-            if key[0] > 0:
+            if 1 <= key[0] <= 4:
                 copy.wait_send()
 
     def dma(*shape):
@@ -382,7 +406,7 @@
     return pl.pallas_call(
         body,
         out_shape=(
-            jax.ShapeDtypeStruct((chunks, height, width), bf16),
+            jax.ShapeDtypeStruct((2, n_x, chunks, height, width), bf16),
             jax.ShapeDtypeStruct((count,) + given.shape[1:], given.dtype),
             jax.ShapeDtypeStruct(vector.shape, vector.dtype),
         ),
@@ -407,6 +431,10 @@
             dma(chunks, n_most - 1),
             dma(chunks, n_z - 1),
             dma(chunks, n_z - 1),
+            dma(chunks, n_x - 1),
+            dma(chunks, n_x - 1),
+            dma(chunks, n_x),
+            dma(chunks, n_x),
             dma(chunks),
             dma(near),
             dma(near),
@@ -591,13 +619,16 @@
     )(source, table_low, targets)
 
 
-def write_heads(grown, heads, turned, tops, stats, targets, weights, chunk, call_id):
+def write_heads(grown, heads, turned, tops, stats, targets, weights, chunk, n_x, call_id):
     n_dp, size, n_pick = grown.shape
     width = heads.shape[2]
     chunks = size // chunk
     turns = chunks // 2
-
-    def body(e_ref, h_ref, t_ref, m_ref, stat_ref, target_ref, w_ref, d_ref, half_ref, log_ref, *scratch):
+    part = size // 2 // n_x
+    block = math.gcd(chunk, part)
+
+    def body(e_ref, h_ref, t_ref, m_ref, stat_ref, target_ref, w_ref, d_ref, log_ref, *refs):
+        part_refs, scratch = refs[:n_x], refs[n_x:]
         buf, t_buf, df_buf, out_buf, got, res = scratch[:6]
         e_sem, t_sem, df_out, df_in, df_own, pair_out, pair_in, res_sem = scratch[6:]
         dp_at, seq_at = lax.axis_index("dp"), lax.axis_index("seq")
@@ -710,19 +741,29 @@
             out_buf[turn] = table_part((1 - core) * turns + turn).astype(bf16)
             pair_copy(turn).start()
 
-        def res_copy(turn):
-            return pltpu.make_async_copy(res.at[turn], half_ref.at[turn], res_sem.at[turn])
+        def res_out(turn):
+            for index in range(chunk // block):
+                at = turn * (chunk // block) + index
+                rows = pl.ds(pl.multiple_of(lax.rem(at, part // block) * block, block), block)
+                slot = lax.rem(at // (part // block) + n_x - seq_at // 2, n_x)
+                for place in range(n_x):
+
+                    @pl.when(slot == place)
+                    def _():
+                        pltpu.make_async_copy(
+                            res.at[turn, pl.ds(index * block, block)], part_refs[place].at[rows], res_sem.at[turn]
+                        ).start()
 
         @pl.loop(0, turns)
         def _(turn):
             total = table_part(core * turns + turn)
             pair_copy(turn).wait()
             res[turn] = (total + got[turn].astype(f32)).astype(bf16)
-            res_copy(turn).start()
+            res_out(turn)
 
         @pl.loop(0, turns)
         def _(turn):
-            res_copy(turn).wait()
+            pltpu.make_async_copy(res.at[turn], res.at[turn], res_sem.at[turn]).wait()
 
         local.wait()
 
@@ -737,11 +778,11 @@
         body,
         out_shape=(
             jax.ShapeDtypeStruct((n_dp, width, n_pick), bf16),
-            jax.ShapeDtypeStruct((turns, chunk, width), bf16),
             jax.ShapeDtypeStruct((2, n_dp, 1, n_pick), f32),
-        ),
+        )
+        + (jax.ShapeDtypeStruct((part, width), bf16),) * n_x,
         in_specs=[HBM, VMEM, HBM, VMEM, VMEM, VMEM, VMEM],
-        out_specs=(HBM, HBM, VMEM),
+        out_specs=(HBM, VMEM) + (HBM,) * n_x,
         scratch_shapes=[
             pltpu.VMEM((n_dp, size, n_pick), bf16),
             pltpu.VMEM((width, size), bf16),
@@ -1168,7 +1209,7 @@
     )(table)
 
 
-def close_half(own, other, names, values, layer, tile):
+def close_half(own, other, names, values, layer, share, tile):
     half, width = own.shape
     count = min(names.shape[1], 2048)
     parts = names.shape[1] // count
@@ -1187,7 +1228,7 @@
         @pl.when((step == 0) & (part == 0))
         def _():
             layer_part = layer_ref[...].astype(f32)
-            square_ref[...] = jnp.sum(layer_part * layer_part, axis=0, keepdims=True)
+            square_ref[...] = jnp.sum(layer_part * layer_part, axis=0, keepdims=True) * share
 
         @pl.when(part == parts - 1)
         def _():
@@ -1209,37 +1250,43 @@
         out_shape=(jax.ShapeDtypeStruct((half, width), bf16), jax.ShapeDtypeStruct((1, width), f32)),
         scratch_shapes=[pltpu.VMEM((tile, width), f32)],
         compiler_params=pltpu.CompilerParams(vmem_limit_bytes=48 << 20),
-        cost_estimate=pl.CostEstimate(
-            flops=2 * half * names.shape[1] * width, bytes_accessed=8 * half * width, transcendentals=0
-        ),
+        cost_estimate=pl.CostEstimate(flops=0, bytes_accessed=0, transcendentals=0),
     )(own, other, names, values, layer)
 
 
-def adam_table(at, factor, weights, mine, other, tile, half, n_x, steps, done):
+def adam_table(at, squares, vector, weights, mine, other, tile, half, n_x, steps, done):
     size, width = weights[0].shape
     per_half, per_part = half // tile, half // n_x // tile
     turns = len(steps) * per_part
     first_step = steps[0]
 
-    def body(at_ref, factor_ref, w_ref, m_ref, v_ref, mine_ref, other_ref, *refs):
+    def body(at_ref, square_ref, vec_ref, w_ref, m_ref, v_ref, mine_ref, other_ref, *refs):
+        new_w, new_m, new_v, token, factor = refs[-5:]
+
+        @pl.when(pl.program_id(0) == 0)
+        def _():
+            squares = jnp.sum(square_ref[...], axis=0)[0:1, 0:1]
+            row = jnp.sum(vec_ref[...] * vec_ref[...], axis=0, keepdims=True)
+            norm = jnp.sqrt(squares + jnp.sum(row, axis=1, keepdims=True))
+            factor[...] = jnp.broadcast_to(clip_at / jnp.maximum(norm, clip_at), factor.shape)
+            token[...] = jnp.zeros_like(token)
+
         from_mine = pl.program_id(0) < turns
-        grad = jnp.where(from_mine, mine_ref[...], other_ref[...]).astype(f32) * factor_ref[0]
-        new_w, new_m, new_v, token = refs[-4:]
-        token[...] = jnp.zeros_like(token)
+        grad = jnp.where(from_mine, mine_ref[...], other_ref[...]).astype(f32) * factor[0:1, 0:1]
         new_w[...], new_m[...], new_v[...] = adam_update(
             w_ref[...], grad, m_ref[...], v_ref[...], 0.1, 0.1
         )
 
-    def row_at(step, at_ref, factor_ref):
+    def row_at(step, at_ref):
         core = lax.rem(at_ref[0] + step // turns, 2)
         turn = lax.rem(step, turns)
         x = lax.rem(at_ref[1] + n_x - (first_step + turn // per_part), n_x)
         return (core * per_half + x * per_part + lax.rem(turn, per_part), 0)
 
-    def mine_at(step, at_ref, factor_ref):
+    def mine_at(step, at_ref):
         return (jnp.minimum(step, turns - 1), 0)
 
-    def other_at(step, at_ref, factor_ref):
+    def other_at(step, at_ref):
         return (jnp.maximum(step - turns, 0), 0)
 
     rows = pl.BlockSpec((tile, width), row_at)
@@ -1247,19 +1294,54 @@
     return pl.pallas_call(
         body,
         grid_spec=pltpu.PrefetchScalarGridSpec(
-            num_scalar_prefetch=2,
+            num_scalar_prefetch=1,
             grid=(2 * turns,),
-            in_specs=[rows, rows, rows, pl.BlockSpec((tile, width), mine_at), pl.BlockSpec((tile, width), other_at)]
+            in_specs=[VMEM, VMEM, rows, rows, rows, pl.BlockSpec((tile, width), mine_at), pl.BlockSpec((tile, width), other_at)]
             + [HBM] * len(done),
             out_specs=(rows, rows, rows, pl.BlockSpec((8, 128), lambda *_: (0, 0))),
+            scratch_shapes=[pltpu.VMEM((8, 128), f32)],
         ),
         out_shape=(jax.ShapeDtypeStruct((size, width), f32),) * 3 + (jax.ShapeDtypeStruct((8, 128), f32),),
-        input_output_aliases={7 + index: index for index in range(len(done))},
+        input_output_aliases={8 + index: index for index in range(len(done))},
         compiler_params=pltpu.CompilerParams(vmem_limit_bytes=56 << 20),
-        cost_estimate=pl.CostEstimate(
-            flops=40 * turns * tile * width, bytes_accessed=52 * turns * tile * width, transcendentals=0
-        ),
-    )(at, factor.reshape(1), *weights, mine, other, *done)
+        cost_estimate=pl.CostEstimate(flops=0, bytes_accessed=0, transcendentals=0),
+    )(at, squares, vector, *weights, mine, other, *done)
+
+
+def update_layer(factor, grads, weights, firsts, seconds):
+    steps = 4 if all(weight.shape[0] % 32 == 0 for weight in weights) else 1
+    count = len(weights)
+
+    def body(factor_ref, *refs):
+        grad_refs, refs = refs[:count], refs[count:]
+        ins, outs, token = refs[: 3 * count], refs[3 * count : 6 * count], refs[6 * count]
+        token[...] = jnp.zeros_like(token)
+        for index, grad in enumerate(grad_refs):
+            for block in range(grad.shape[0]):
+                columns = slice(block * grad.shape[2], (block + 1) * grad.shape[2])
+                w, m, v = (ins[index + kind * count][:, columns] for kind in range(3))
+                new = adam_update(w, grad[block] * factor_ref[0:1, 0:1], m, v, 0.1, 0.1)
+                for kind in range(3):
+                    outs[index + kind * count][:, columns] = new[kind]
+
+    def rows(value):
+        return pl.BlockSpec((value.shape[0] // steps, value.shape[1]), lambda step: (step, 0))
+
+    def blocks(value):
+        return pl.BlockSpec((value.shape[0], value.shape[1] // steps, value.shape[2]), lambda step: (0, step, 0))
+
+    states = (*weights, *firsts, *seconds)
+    *news, token = pl.pallas_call(
+        body,
+        grid=(steps,),
+        in_specs=[VMEM] + [blocks(grad) for grad in grads] + [rows(value) for value in states],
+        out_specs=tuple(rows(value) for value in states) + (pl.BlockSpec((8, 128), lambda step: (0, 0)),),
+        out_shape=tuple(jax.ShapeDtypeStruct(value.shape, f32) for value in states)
+        + (jax.ShapeDtypeStruct((8, 128), f32),),
+        compiler_params=pltpu.CompilerParams(vmem_limit_bytes=56 << 20),
+        cost_estimate=pl.CostEstimate(flops=0, bytes_accessed=0, transcendentals=0),
+    )(factor, *grads, *states)
+    return [news[index::count] for index in range(count)], token
 
 
 def layer_norm(x, gain, shift):
@@ -1482,20 +1564,16 @@
     grown, heads, tops, stats = read_heads(
         sources, table_low, flat_targets, vocab_part, tile, n_y, n_z, 9
     )
-    final_grad, half_low, logs = write_heads(
-        grown, heads, table_turned, tops, stats, flat_targets, flat_valid / masked_count, tile, 5
+    final_grad, logs, *half_parts = write_heads(
+        grown, heads, table_turned, tops, stats, flat_targets, flat_valid / masked_count, tile, n_x, 5
     )
     loss_group = jnp.sum(flat_valid * (logs[0] - logs[1]))
     final_grad = jnp.sum(final_grad.astype(f32), axis=0).T
-    half_low = half_low.reshape(half, model)
     part = half // n_x
     slab = 16 * max(count for count in range(1, 26) if part % (16 * count) == 0)
     x_at = seq_at // 2
 
-    def part_of(step):
-        return lax.dynamic_slice_in_dim(half_low, lax.rem(x_at + step, n_x) * part, part, 0)
-
-    part_came = [from_peer(part_of(step), "seq", 2, n_x, step) for step in range(1, n_x)]
+    part_came = [from_peer(half_parts[step], "seq", 2, n_x, step) for step in range(1, n_x)]
     if n_x > 2:
         part_came = [sum(came.astype(f32) for came in part_came).astype(bf16)]
 
@@ -1520,8 +1598,8 @@
         )
         return summed_ids.astype(bf16).reshape(2 * n_dp, GIVE, model)
 
-    chunks = 4
-    layer_piece, came, vec_total = settle(
+    chunks = 5
+    layer_sum, came, vec_total = settle(
         whole.reshape(n_dp, 2, n_x, chunks, -1, model),
         first_given.reshape(2 * n_dp, GIVE, model),
         vec_grad,
@@ -1530,7 +1608,7 @@
         n_z,
         7,
     )
-    layer_piece = layer_piece.reshape(-1, model)
+    layer_sum = layer_sum.reshape(-1, model)
 
     def give_more(state):
         turn, total, _ = state
@@ -1541,80 +1619,65 @@
         sent = jnp.broadcast_to(sent, (n_dp, n_x, 2, GIVE, model)).reshape(-1, GIVE, model)
         got = lax.all_to_all(sent, ("dp", "seq"), 0, 0).reshape(-1, model)
         total, squares = close_half(
-            total, jnp.zeros_like(total), names, got, layer_piece, slab
+            total, jnp.zeros_like(total), names, got, layer_sum, 1.0 / n_seq, slab
         )
         return turn + 1, total, jnp.sum(squares)
 
     names = asks_half.reshape(1, -1) - x_at * part
     values = came.reshape(-1, model)
     part_own, squares_own = close_half(
-        part_of(0), part_came[0], names, values, layer_piece, slab
+        half_parts[0], part_came[0], names, values, layer_sum, 1.0 / n_seq, slab
     )
     _, part_own, part_square = lax.while_loop(
         lambda state: state[0] < turns[1], give_more, (jnp.int32(1), part_own, jnp.sum(squares_own))
     )
-    layer_sum = group_join(layer_piece, 0, "seq", 2, n_x).reshape(-1, model)
-    layer_sum = group_join(layer_sum, 0, "seq", 1, 2).reshape(-1, model).astype(f32)
     loss_sum = vec_total[14, 0] / n_dp
     vec_total = vec_total[:14]
 
-    def side_by_side(rows_of, count):
-        return jnp.concatenate(jnp.split(rows_of, count, axis=0), axis=1)
-
+    said = jnp.where(jnp.arange(8)[:, None] == 0, part_square, jnp.zeros((8, 128), f32))
+    told_squares = deliver(said, ("seq",), 8)
+    zero = told_squares[0, 1, 0].astype(bf16)
+    far_out = part_own + zero
+    far_own = [from_peer(far_out, "seq", 2, n_x, step) for step in range(1, n_x)]
+    far_own = far_own[0] if n_x == 2 else jnp.concatenate(far_own)
+    part_pair = from_peer(part_own, "seq", 1, 2, 1)
+    told_squares = deliver(jnp.sum(told_squares, axis=0), ("dp",), 4)
+    square_total = jnp.sum(told_squares[:, 0, 0])
+    grad_norm = jnp.sqrt(square_total + jnp.sum(vec_total * vec_total))
+    factor = clip_at / jnp.maximum(grad_norm, clip_at)
+    state = (table, first_table, second_table)
+    at = jnp.stack([core, x_at])
+    *near, token = adam_table(
+        at, told_squares, vec_total, state, part_own, part_pair, slab, half, n_x, (0,), None
+    )
+    layer_sum = layer_sum.astype(f32)
     ends = [0]
     for count in (mlp_out.shape[0], hidden // model * thick, thick, 3 * thick, positions.shape[0]):
         ends.append(ends[-1] + count)
     g_down, g_up, g_out, g_in, g_pos = [layer_sum[begin:end] for begin, end in zip(ends, ends[1:])]
-    g_in = side_by_side(g_in, 3)
-    g_up = side_by_side(g_up, hidden // model)
-    said = jnp.full((8, 128), part_square)
-    square_total = jnp.sum(deliver(said, ("dp", "seq"), 8)[:, 0, 0])
-    part_own, square_total = lax.optimization_barrier((part_own, square_total))
-    far_own = [from_peer(part_own, "seq", 2, n_x, step) for step in range(1, n_x)]
-    far_own = far_own[0] if n_x == 2 else jnp.concatenate(far_own)
-    part_pair = from_peer(part_own, "seq", 1, 2, 1)
-    grad_norm = jnp.sqrt(square_total + jnp.sum(vec_total * vec_total))
-    factor = clip_at / jnp.maximum(grad_norm, clip_at)
-    weights = (attn_in, attn_out, mlp_in, mlp_out, table, positions, vectors)
-    all_grads = (g_in, g_out, g_up, g_down, None, g_pos, vec_total)
-    firsts = (
-        first_attn_in,
-        first_attn_out,
-        first_mlp_in,
-        first_mlp_out,
-        first_table,
-        first_positions,
-        first_vectors,
+    layer_grads = (
+        g_in.reshape(3, thick, model),
+        g_out[None],
+        g_up.reshape(-1, thick, model),
+        g_down[None],
+        g_pos[None],
     )
-    seconds = (
-        second_attn_in,
-        second_attn_out,
-        second_mlp_in,
-        second_mlp_out,
-        second_table,
-        second_positions,
-        second_vectors,
+    updates, layer_token = update_layer(
+        (factor + token[0, 0]).reshape(1, 1),
+        layer_grads,
+        (attn_in, attn_out, mlp_in, mlp_out, positions),
+        (first_attn_in, first_attn_out, first_mlp_in, first_mlp_out, first_positions),
+        (second_attn_in, second_attn_out, second_mlp_in, second_mlp_out, second_positions),
     )
-    news, moments, squares = ([], [], [])
-    for index in range(7):
-        rate, decay = (1.0, 0.0) if index == 6 else (0.1, 0.1)
-        if index == 4:
-            state = (table, first_table, second_table)
-            at = jnp.stack([core, x_at])
-            *near, token = adam_table(at, factor, state, part_own, part_pair, slab, half, n_x, (0,), None)
-            far_own = far_own + token[0, 0].astype(bf16)
-            far_pair = from_peer(far_own, "seq", 1, 2, 1)
-            far_steps = tuple(range(1, n_x))
-            new_w, new_m, new_v, _ = adam_table(
-                at, factor, state, far_own, far_pair, slab, half, n_x, far_steps, near
-            )
-        else:
-            new_w, new_m, new_v = adam_update(
-                weights[index], all_grads[index] * factor, firsts[index], seconds[index], rate, decay
-            )
-        news.append(new_w)
-        moments.append(new_m)
-        squares.append(new_v)
+    results = dict(zip((0, 1, 2, 3, 5), updates))
+    results[6] = adam_update(vectors, vec_total * factor, first_vectors, second_vectors, 1.0, 0.0)
+    far_own = far_own + (token[0, 0] + layer_token[0, 0]).astype(bf16)
+    far_pair = from_peer(far_own, "seq", 1, 2, 1)
+    far_steps = tuple(range(1, n_x))
+    *results[4], _ = adam_table(
+        at, told_squares, vec_total, state, far_own, far_pair, slab, half, n_x, far_steps, near
+    )
+    news, moments, squares = zip(*(results[index] for index in range(7)))
     return (*news, *moments, *squares, loss_sum, masked_count, grad_norm)
 
 

time: 700 us -> 679 us (0.970)
  waiting for transfers between devices: 47.5 us -> 13.9 us
  Pallas kernels: 526 us -> 547 us
  other arithmetic: 44 us -> 32.7 us
    ppermute x6 -> x4, waiting for transfers between devices: 30 us -> 3.39 us  [from_peer(): return lax.ppermute(x, axis, pairs)]
    sub x5 -> x1, other arithmetic: 11.8 us -> 0.68 us  [adam_update(): weight - rate * (mhat / (jnp.sqrt(vhat) + adam_eps) + decay * weight)]
    pallas_call x1 -> x2, Pallas kernels: 150 us -> 158 us  [the longest x1 148 us: settle(): pl.pallas_call(body, out_shape=(jax.ShapeDtypeStruct((2, n_x, chunks, hei...]
    pallas_call x4 -> x5, Pallas kernels: 78.4 us -> 84.7 us  [deliver(): pl.pallas_call(body, out_shape=jax.ShapeDtypeStruct((count,) + block, x.d...]
  transfers between devices with their start and end apart: 7 -> 5, of which waited for: 3 -> 2; matrix products, arithmetic and copies ran while one was open for 9% -> 8% of each run, Pallas kernels for 47% -> 49%
where the time goes in v4:
time: 679 us; the launch traced here: 669 us
  Pallas kernels  547 us (81%)
  local copies, waits for them, and re-layouts  39 us (6%)
  other arithmetic  32.7 us (5%)
  between operations  25.9 us (4%)
  waiting for transfers between devices  13.9 us (2%)
    pallas_call x1, Pallas kernels, settle(): pl.pallas_call(body, out_shape=(jax.ShapeDtypeStruct((2, n_x, chunks, hei...  148 us
    pallas_call x5, Pallas kernels, deliver(): pl.pallas_call(body, out_shape=jax.ShapeDtypeStruct((count,) + block, x.d...  84.7 us
    pallas_call x2, Pallas kernels, staged(): pl.pallas_call(body, out_shape=tuple(outs.values()), in_specs=[HBM] * (le...  84.6 us
    pallas_call x1, Pallas kernels, read_heads(): pl.pallas_call(body, out_shape=(jax.ShapeDtypeStruct((n_dp, size, n_pick)...  80.4 us
    pallas_call x1, Pallas kernels, write_heads(): pl.pallas_call(body, out_shape=(jax.ShapeDtypeStruct((n_dp, width, n_pick...  61.2 us
    pallas_call x2, Pallas kernels, adam_table(): pl.pallas_call(body, grid_spec=pltpu.PrefetchScalarGridSpec(num_scalar_pr...  54 us
    pallas_call x1, Pallas kernels, table_forms(): pl.pallas_call(body, grid=(size // chunk,), in_specs=[pl.BlockSpec((chunk...  13.7 us
  transfers between devices with their start and end apart: 5, of which 2 were waited for; matrix products, arithmetic and copies ran while one was open for 8% of the time, Pallas kernels for 49%

profile of v4, /device:TPU:0, one launch (start us, length us, event | category | flops | bytes accessed | tf_op | source)
XLA Modules:
  0.0 669.3 jit_solution(2519425112043590162)
XLA Ops:
  12.7 5.8 shard_map.415
  20.3 2.4 convert_reduce_fusion.2
  34.7 20.9 %shard_map.416 = s32[32,32,128]{2,1,0:T(8,128)} custom-call(s32[32,128]{1,0:T(8,128)} %pad_add_fusion.x_ref), custom_call_target="tpu_custom_call" | custom-call | tf_op jit(solution)/shard_map/pallas_call | solution.py:88
  57.2 13.7 %shard_map.417 = (bf16[6400,768]{1,0:T(8,128)(2,1)}, bf16[768,6400]{1,0:T(8,128)(2,1)S(1)}) custom-call(f32[6288,768]{1,0:T(8,128)} %w_ref.3), custom_call_target="tpu_custom_call" | custom-call | tf_op jit(solution)/shard_map/pallas_call | solution.py:1196
  70.8 3.9 copy-done
  74.7 8.4 %gather_fusion.1 = bf16[768,768]{1,0:T(8,128)(2,1)S(1)} fusion(bf16[6400,768]{1,0:T(8,128)(2,1)} %get-tuple-element.754.t_ref, s32[1024]{0:T(1024)S(1)} %pad_clamp_fusion.1), kind=kCustom, calls=%fused_computation.1 | custom fusion | bytes 2362368 | tf_op jit(solution)/shard_map/jit(_take)/gather | solution.py:1539
  84.3 45.8 %shard_map.418 = bf16[8,96,768]{2,1,0:T(8,128)(2,1)} custom-call(bf16[8,96,768]{2,1,0:T(8,128)(2,1)} %broadcast_select_fusion.1.x_ref), custom_call_target="tpu_custom_call" | custom-call | tf_op jit(solution)/shard_map/pallas_call | solution.py:88
  130.6 4.5 fusion.18
  136.0 3.5 convert_element_type.82.refs_1_.refs_14_
  141.4 10.5 %all-gather.3.cloned.1.call-done = bf16[10240,768]{1,0:T(8,128)(2,1)} async-done(((bf16[320,768]{1,0:T(8,128)(2,1)}), bf16[10240,768]{1,0:T(8,128)(2,1)}) %all-gather.3.cloned.1.call-update) | async-done | bytes 15728656 | tf_op jit(solution)/shard_map/all_gather | solution.py:1439
  152.4 35.6 %shard_map.419 = (bf16[1024,768]{1,0:T(8,128)(2,1)}, bf16[1024,768]{1,0:T(8,128)(2,1)}, bf16[1024,768]{1,0:T(8,128)(2,1)}, bf16[256,768]{1,0:T(8,128)(2,1)}, f32...) custom-call(bf16[8,4,320,768]{3,2,1,0:T(8,128)(2,1)} %bitcast.142, ...), custom_call_target="tpu_custom_call" | custom-call | tf_op jit(solution)/shard_map/pallas_call | solution.py:873
  188.0 80.4 %shard_map.420 = (bf16[8,6400,256]{2,1,0:T(8,128)(2,1)}, bf16[8,256,768]{2,1,0:T(8,128)(2,1)}, f32[8,10,8,256]{3,2,1,0:T(8,128)}, f32[8,8,8,256]{3,2,1,0:T(8,128)}) custom-call(bf16[256,768]{1,0:T(8,128)(2,1)} %get-tuple-element.424.s_ref, bf16[6400,768]{1,0:T(8,128)(2,1)} %get-tuple-element.836, s32[8,1,256]{2,1,0:T(1,128)} %compare_select_fusion.3.target_ref), custom_call_target="tpu_custom_call" | custom-call | tf_op jit(solution)/shard_map/pallas_call | solution.py:590
  268.4 61.2 %shard_map.421 = (bf16[8,768,256]{2,1,0:T(8,128)(2,1)}, f32[2,8,1,256]{3,2,1,0:T(1,128)}, bf16[1600,768]{1,0:T(8,128)(2,1)}, bf16[1600,768]{1,0:T(8,128)(2,1)}) custom-call(bf16[8,6400,256]{2,1,0:T(8,128)(2,1)} %get-tuple-element.425.e_ref, bf16[2048,768]{1,0:T(8,128)(2,1)} %bitcast.151, bf16[768,6400]{1,0:T(8,128)(2,1)} %copy-done, ...), custom_call_target="tpu_custom_call" | custom-call | tf_op jit(solution)/shard_map/pallas_call | solution.py:777
  329.6 2.8 collective-permute-start
  338.8 49.0 %shard_map.422 = (bf16[8,1280,768]{2,1,0:T(8,128)(2,1)}, f32[16,768]{1,0:T(8,128)}, bf16[1024,768]{1,0:T(8,128)(2,1)}, bf16[1024,768]{1,0:T(8,128)(2,1)}) custom-call(bf16[8,4,320,768]{3,2,1,0:T(8,128)(2,1)} %bitcast.143, f32[256,768]{1,0:T(8,128)} %get-tuple-element.432.refs_1_, f32[256,768]{1,0:T(8,128)} %bitcast.150, ...), custom_call_target="tpu_custom_call" | custom-call | tf_op jit(solution)/shard_map/pallas_call | solution.py:873
  390.0 147.7 %shard_map.423 = (bf16[2,2,5,64,768]{4,3,2,1,0:T(8,128)(2,1)S(1)}, bf16[32,64,768]{2,1,0:T(8,128)(2,1)S(1)}, f32[16,768]{1,0:T(8,128)S(1)}) custom-call(bf16[8,2,2,5,64,768]{5,4,3,2,1,0:T(8,128)(2,1)} %bitcast.146, bf16[16,64,768]{2,1,0:T(8,128)(2,1)S(1)} %bitcast.137, f32[16,768]{1,0:T(8,128)S(1)} %copy-done.4), custom_call_target="tpu_custom_call" | custom-call | tf_op jit(solution)/shard_map/pallas_call | solution.py:406
  539.4 10.2 %shard_map.424 = (bf16[1600,768]{1,0:T(8,128)(2,1)}, f32[1,768]{1,0:T(1,128)S(1)}) custom-call(bf16[1600,768]{1,0:T(8,128)(2,1)S(1)} %copy-done.2, bf16[1600,768]{1,0:T(8,128)(2,1)} %collective-permute-done.other_ref, s32[1,2048]{1,0:T(1,128)S(1)} %sub.122.names_ref, bf16[2048,768]{1,0:T(8,128)(2,1)} %bitcast.136, bf16[1280,768]{1,0:T(8,128)(2,1)S(1)} %bitcast.139), custom_call_target="tpu_custom_call" | custom-call | tf_op jit(solution)/shard_map/pallas_call | solution.py:1239
  553.5 4.3 shard_map.425
  559.1 3.9 broadcast_add_fusion.1
  571.0 7.9 %shard_map.426.square_ref = f32[8,8,128]{2,1,0:T(8,128)} custom-call(f32[8,128]{1,0:T(8,128)} %reduce_sum.178.x_ref), custom_call_target="tpu_custom_call" | custom-call | tf_op jit(solution)/shard_map/pallas_call | solution.py:88
  582.4 27.1 %shard_map.427 = (f32[6288,768]{1,0:T(8,128)}, f32[6288,768]{1,0:T(8,128)}, f32[6288,768]{1,0:T(8,128)}, f32[8,128]{1,0:T(8,128)}) custom-call(s32[2]{0:T(128)} %pad_add_fusion.2.at_ref, f32[8,8,128]{2,1,0:T(8,128)} %shard_map.426.square_ref, f32[14,768]{1,0:T(8,128)} %get-tuple-element.557.vec_ref, f32[6288,768]{1,0:T(8,128)} %w_ref.3, f32[6288,768]{1,0:T(8,128)} %m_ref.3, ...), custom_call_target="tpu_custom_call" | custom-call | tf_op jit(solution)/shard_map/pallas_call | solution.py:1294
  611.4 10.7 %shard_map.428 = (f32[96,2304]{1,0:T(8,128)}, f32[96,768]{1,0:T(8,128)}, f32[96,3072]{1,0:T(8,128)}, f32[384,768]{1,0:T(8,128)}, f32[128,768]{1,0:T(8,128)}, /*i...) custom-call(f32[1,1]{1,0:T(1,128)} %bitcast.54.factor_ref, ...), custom_call_target="tpu_custom_call" | custom-call | tf_op jit(solution)/shard_map/pallas_call | solution.py:1334
  627.9 3.4 collective-permute-done.3.other_ref
  632.7 27.0 %shard_map.429 = (f32[6288,768]{1,0:T(8,128)}, f32[6288,768]{1,0:T(8,128)}, f32[6288,768]{1,0:T(8,128)}, f32[8,128]{1,0:T(8,128)}) custom-call(s32[2]{0:T(128)} %pad_add_fusion.2.at_ref, f32[8,8,128]{2,1,0:T(8,128)} %shard_map.426.square_ref, f32[14,768]{1,0:T(8,128)} %get-tuple-element.557.vec_ref, ...), custom_call_target="tpu_custom_call", output_to_operand_aliasing={{0}: (8, {}), {1}: (9, {}), {2}: (10, {})} | custom-call | tf_op jit(solution)/shard_map/pallas_call | solution.py:1294
  (119 shorter events, 54.2 us)
Async XLA Ops:
  7.2 11.3 %copy-start.15 = (s32[32,256]{1,0:T(8,128)S(1)}, s32[32,256]{1,0:T(8,128)}, u32[]{:S(2)}) copy-start(s32[32,256]{1,0:T(8,128)} %param.30) | copy-start | bytes 98308
  7.2 22.1 %copy-start.18 = (s32[32]{0:T(128)S(1)}, s32[32]{0:T(128)}, u32[]{:S(2)}) copy-start(s32[32]{0:T(128)} %param.29) | copy-start | bytes 388
  7.2 144.6 %all-gather.3.cloned.1.call-start = ((), (), s32[]{:S(2)}) async-start(), calls=%async_computation.3 | async-start | bytes 16220160 | tf_op jit(solution)/shard_map/all_gather | solution.py:1439
  18.5 52.3 %copy-start.16 = (s32[1,256]{1,0:T(1,128)}, s32[1,256]{1,0:T(1,128)S(1)}, u32[]{:S(2)}) copy-start(s32[1,256]{1,0:T(1,128)S(1)} %constant_dynamic-slice_fusion.4.refs_18_) | copy-start | bytes 3076
  70.8 3.9 copy-start
  329.6 7.3 %copy-start.17 = (f32[2,8,1,256]{3,2,1,0:T(1,128)S(1)}, f32[2,8,1,256]{3,2,1,0:T(1,128)}, u32[]{:S(2)}) copy-start(f32[2,8,1,256]{3,2,1,0:T(1,128)} %get-tuple-element.442) | copy-start | bytes 49156
  329.6 209.8 %collective-permute-start = (bf16[1600,768]{1,0:T(8,128)(2,1)}, bf16[1600,768]{1,0:T(8,128)(2,1)}, u32[]{:S(2)}, u32[]{:S(2)}) collective-permute-start(bf16[1600,768]{1,0:T(8,128)(2,1)} %get-tuple-element.431), channel_id=1, source_target_pairs={{0,2},{1,3},{2,0},{3,1},{4,6},{5,7},{6,4},{7,5},{8,10},{9,11},{10,... | collective-permute-start | bytes 7372808 | tf_op jit(solution)/shard_map/ppermute | solution.py:107
  387.8 1.4 copy-start.3
  389.2 0.8 copy-start.4
  390.0 149.4 %copy-start.2 = (bf16[1600,768]{1,0:T(8,128)(2,1)S(1)}, bf16[1600,768]{1,0:T(8,128)(2,1)}, u32[]{:S(2)}) copy-start(bf16[1600,768]{1,0:T(8,128)(2,1)} %get-tuple-element.430.own_ref) | copy-start | bytes 7372804
  537.7 1.7 copy-start.1
  539.4 10.2 %copy-start.6 = (bf16[2,2,5,64,768]{4,3,2,1,0:T(8,128)(2,1)}, bf16[2,2,5,64,768]{4,3,2,1,0:T(8,128)(2,1)S(1)}, u32[]{:S(2)}) copy-start(bf16[2,2,5,64,768]{4,3,2,1,0:T(8,128)(2,1)S(1)} %get-tuple-element.447) | copy-start | bytes 5898244
  552.1 13.2 %copy-start.8 = (bf16[1280,768]{1,0:T(8,128)(2,1)S(1)}, bf16[1280,768]{1,0:T(8,128)(2,1)}, u32[]{:S(2)}) copy-start(bf16[1280,768]{1,0:T(8,128)(2,1)} %get-tuple-element.838) | copy-start | bytes 5898244
  559.0 23.4 %collective-permute-start.1 = (bf16[1600,768]{1,0:T(8,128)(2,1)}, bf16[1600,768]{1,0:T(8,128)(2,1)}, u32[]{:S(2)}, u32[]{:S(2)}) collective-permute-start(bf16[1600,768]{1,0:T(8,128)(2,1)} %get-tuple-element.453.mine_ref), channel_id=1, source_target_pairs={{0,1},{1,0},{2,3},{3,2},{4,5},{5,4},{6,7},{7,6},{8,9},{9,8},{10,11... | collective-permute-start | bytes 7372808 | tf_op jit(solution)/shard_map/ppermute | solution.py:107
  563.1 61.6 %collective-permute-start.2 = (bf16[1600,768]{1,0:T(8,128)(2,1)}, bf16[1600,768]{1,0:T(8,128)(2,1)}, u32[]{:S(2)}, u32[]{:S(2)}) collective-permute-start(bf16[1600,768]{1,0:T(8,128)(2,1)} %broadcast_add_fusion.1), channel_id=1, source_target_pairs={{0,2},{1,3},{2,0},{3,1},{4,6},{5,7},{6,4},{7,5},{8,10},{9,11},{10,... | collective-permute-start | bytes 7372808 | tf_op jit(solution)/shard_map/ppermute | solution.py:107
  566.6 3.8 copy-start.12
  566.6 15.1 %copy-start.11 = (f32[14,768]{1,0:T(8,128)S(1)}, f32[14,768]{1,0:T(8,128)}, u32[]{:S(2)}) copy-start(f32[14,768]{1,0:T(8,128)} %refs_16_.2) | copy-start | bytes 129028
  566.6 15.1 %copy-start.13 = (f32[14,768]{1,0:T(8,128)S(1)}, f32[14,768]{1,0:T(8,128)}, u32[]{:S(2)}) copy-start(f32[14,768]{1,0:T(8,128)} %param.44) | copy-start | bytes 129028
  566.6 15.1 %copy-start.14 = (f32[14,768]{1,0:T(8,128)S(1)}, f32[14,768]{1,0:T(8,128)}, u32[]{:S(2)}) copy-start(f32[14,768]{1,0:T(8,128)} %param.51) | copy-start | bytes 129028
  567.3 15.2 %copy-start.5 = (bf16[1600,768]{1,0:T(8,128)(2,1)S(1)}, bf16[1600,768]{1,0:T(8,128)(2,1)}, u32[]{:S(2)}) copy-start(bf16[1600,768]{1,0:T(8,128)(2,1)} %get-tuple-element.453.mine_ref) | copy-start | bytes 7372804
  626.6 4.8 copy-start.9
  626.6 4.7 collective-permute-start.3
  631.3 1.4 copy-start.10
Sparse Core Ops, SparseCore 0:
  12.8 138.9 all-gather.2

commit v5 on v4

--- a/solution.py
+++ b/solution.py
@@ -910,9 +910,15 @@
     return lax.broadcasted_iota(i32, shape, dim)
 
 
-def flat(ref, columns=slice(None)):
-    value = ref[..., columns]
+def flat(ref):
+    value = ref[...]
     return value.reshape(-1, value.shape[-1])
+
+
+def column_block(ref, block, size):
+    if len(ref.shape) == 2:
+        return ref[:, block * size : (block + 1) * size]
+    return flat(ref.at[block])
 
 
 def row_block(ref, block, size):
@@ -922,9 +928,9 @@
     _, inner, rows, _ = ref.shape
     if inner * rows <= size:
         per = inner * rows
-        return flat(ref[first // per : (first + size) // per])
+        return flat(ref.at[pl.ds(first // per, size // per)])
     owner, first = divmod(first, inner * rows)
-    return flat(ref[owner, first // rows : (first + size) // rows])
+    return flat(ref.at[owner, pl.ds(first // rows, size // rows)])
 
 
 def split_three(x):
@@ -954,12 +960,12 @@
         chosen = jnp.where(small["pick_col"][...] - 1 == iota((n_pick, length), 1), 1.0, 0.0).astype(bf16)
         start_picked = dot(chosen, emb[...]) + dot(chosen, flat(pos_rows))
         w = get("w_in")
-        out["k"][...] = dot(out["a"][...], flat(w, slice(model, 2 * model))).astype(bf16)
+        out["k"][...] = dot(out["a"][...], column_block(w, 1, model)).astype(bf16)
         put("k")
-        out["v"][...] = (dot(out["a"][...], flat(w, slice(2 * model, 3 * model))) + vec[7:8]).astype(bf16)
+        out["v"][...] = (dot(out["a"][...], column_block(w, 2, model)) + vec[7:8]).astype(bf16)
         put("v")
         a_picked = dot(chosen, out["a"][...]).astype(bf16)
-        out["q"][...] = (dot(a_picked, flat(w, slice(0, model))) + vec[6:7]).astype(bf16)
+        out["q"][...] = (dot(a_picked, column_block(w, 0, model)) + vec[6:7]).astype(bf16)
         put("q")
         keep = iota((length, n_pick), 0) < small["length"][0, 0]
 
@@ -992,9 +998,8 @@
         put("m")
         up, down = get("w_up"), get("w_down")
         x2 = x1 + vec[9:10]
-        for block in range(up.shape[-1] // model):
-            place = slice(block * model, (block + 1) * model)
-            u1 = dot(out["m"][...], flat(up, place)) + vec[10 + block : 11 + block]
+        for block in range(vectors.shape[0] - 10):
+            u1 = dot(out["m"][...], column_block(up, block, model)) + vec[10 + block : 11 + block]
             x2 = x2 + dot(gelu_fn(u1).astype(bf16), row_block(down, block, model))
         out["x2"][...] = x2
         put("x2")
@@ -1039,9 +1044,9 @@
     head_dim = model // H
     per = lanes // head_dim
     w_in, w_out, w_up, w_down = weights
-    hidden = w_up.shape[-1]
+    wide = vectors.shape[0] - 10
+    hidden = wide * model
     thick, long, n_place = model // n_dp, hidden // n_dp, spots[1]
-    wide = hidden // model
     first_rows = 2 * long
     last_rows = 4 * thick + length // n_dp
 
@@ -1064,8 +1069,7 @@
         m_turned = m[...].T
         dm = None
         for block in range(wide):
-            place = slice(block * model, (block + 1) * model)
-            u1 = dot(m[...], flat(up, place)) + vec[10 + block : 11 + block]
+            u1 = dot(m[...], column_block(up, block, model)) + vec[10 + block : 11 + block]
             act, gelu_back = jax.vjp(gelu_fn, u1)
             part = dot(act.astype(bf16).T, dy2).astype(bf16)
             run = min(long, model)
@@ -1075,7 +1079,7 @@
             du1 = gelu_back(dot(dy2, row_block(down, block, model), 1, 1))[0].astype(bf16)
             d_vec[10 + block : 11 + block] = jnp.sum(du1.astype(f32), axis=0, keepdims=True)
             rows_of(long + block * thick, thick, dot(m_turned, du1))
-            part = dot(du1, flat(up, place), 1, 1)
+            part = dot(du1, column_block(up, block, model), 1, 1)
             dm = part if dm is None else dm + part
         first_out = put("whole", 0, first_rows)
         dx1, d_vec[2:3], d_vec[3:4] = norm_back(get("x1")[...], vec[2:3], dm)
@@ -1126,7 +1130,10 @@
         a_turned = get("a")[...].T
         for part in range(3):
             rows_of((1 + part) * thick, thick, dot(a_turned, dqkv[:, part * model : (part + 1) * model]))
-        da = dot(dqkv[...], flat(get("w_in")), 1, 1)
+        w = get("w_in")
+        da = dot(dqkv[:, :model], column_block(w, 0, model), 1, 1)
+        for part in range(1, 3):
+            da = da + dot(dqkv[:, part * model : (part + 1) * model], column_block(w, part, model), 1, 1)
         start = get("emb")[...].astype(f32) + flat(get("pos")).astype(f32)
         dx0, d_vec[0:1], d_vec[1:2] = norm_back(start, vec[0:1], da)
         for part in split_three(dx1):
@@ -1314,8 +1321,7 @@
 
     def body(factor_ref, *refs):
         grad_refs, refs = refs[:count], refs[count:]
-        ins, outs, token = refs[: 3 * count], refs[3 * count : 6 * count], refs[6 * count]
-        token[...] = jnp.zeros_like(token)
+        ins, outs = refs[: 3 * count], refs[3 * count :]
         for index, grad in enumerate(grad_refs):
             for block in range(grad.shape[0]):
                 columns = slice(block * grad.shape[2], (block + 1) * grad.shape[2])
@@ -1331,17 +1337,16 @@
         return pl.BlockSpec((value.shape[0], value.shape[1] // steps, value.shape[2]), lambda step: (0, step, 0))
 
     states = (*weights, *firsts, *seconds)
-    *news, token = pl.pallas_call(
+    news = pl.pallas_call(
         body,
         grid=(steps,),
         in_specs=[VMEM] + [blocks(grad) for grad in grads] + [rows(value) for value in states],
-        out_specs=tuple(rows(value) for value in states) + (pl.BlockSpec((8, 128), lambda step: (0, 0)),),
-        out_shape=tuple(jax.ShapeDtypeStruct(value.shape, f32) for value in states)
-        + (jax.ShapeDtypeStruct((8, 128), f32),),
+        out_specs=tuple(rows(value) for value in states),
+        out_shape=tuple(jax.ShapeDtypeStruct(value.shape, f32) for value in states),
         compiler_params=pltpu.CompilerParams(vmem_limit_bytes=56 << 20),
         cost_estimate=pl.CostEstimate(flops=0, bytes_accessed=0, transcendentals=0),
     )(factor, *grads, *states)
-    return [news[index::count] for index in range(count)], token
+    return [news[index::count] for index in range(count)]
 
 
 def layer_norm(x, gain, shift):
@@ -1444,7 +1449,7 @@
 
         def blocks_at(part, blocks):
             return [
-                ((slice(None), block, rows_at(part)), (slice(None), slice(None), pl.ds(at * model, model)))
+                ((slice(None), block, rows_at(part)), (at,))
                 for at, block in enumerate(blocks)
             ]
 
@@ -1456,7 +1461,7 @@
             {
                 "pos": all_at(3),
                 "w_in": blocks_at(0, range(3)),
-                "w_out": blocks_at(0, [3]),
+                "w_out": [((slice(None), 3, rows_at(0)), (slice(None),))],
                 "w_up": blocks_at(1, range(4)),
                 "w_down": all_at(2),
             },
@@ -1465,8 +1470,8 @@
         def shape(*dims):
             return jax.ShapeDtypeStruct(dims, bf16)
 
-        pos_all, w_in, w_out = shape(n_dp, n_seq, some, model), shape(n_dp, thick, 3 * model), shape(n_dp, thick, model)
-        w_up, w_down = shape(n_dp, thick, hidden), shape(n_dp, n_seq, long, model)
+        pos_all, w_in, w_out = shape(n_dp, n_seq, some, model), shape(3, n_dp, thick, model), shape(n_dp, thick, model)
+        w_up, w_down = shape(4, n_dp, thick, model), shape(n_dp, n_seq, long, model)
     else:
         weight_pieces = None
 
@@ -1650,7 +1655,7 @@
     *near, token = adam_table(
         at, told_squares, vec_total, state, part_own, part_pair, slab, half, n_x, (0,), None
     )
-    layer_sum = layer_sum.astype(f32)
+    layer_sum = layer_sum.astype(f32) + token[0, 0]
     ends = [0]
     for count in (mlp_out.shape[0], hidden // model * thick, thick, 3 * thick, positions.shape[0]):
         ends.append(ends[-1] + count)
@@ -1662,8 +1667,11 @@
         g_down[None],
         g_pos[None],
     )
-    updates, layer_token = update_layer(
-        (factor + token[0, 0]).reshape(1, 1),
+    far_own = far_own + token[0, 0].astype(bf16)
+    far_pair = from_peer(far_own, "seq", 1, 2, 1)
+    held = jnp.minimum(jnp.abs(far_own[0, 0].astype(f32)), 0.0)
+    updates = update_layer(
+        (factor + held).reshape(1, 1),
         layer_grads,
         (attn_in, attn_out, mlp_in, mlp_out, positions),
         (first_attn_in, first_attn_out, first_mlp_in, first_mlp_out, first_positions),
@@ -1671,8 +1679,6 @@
     )
     results = dict(zip((0, 1, 2, 3, 5), updates))
     results[6] = adam_update(vectors, vec_total * factor, first_vectors, second_vectors, 1.0, 0.0)
-    far_own = far_own + (token[0, 0] + layer_token[0, 0]).astype(bf16)
-    far_pair = from_peer(far_own, "seq", 1, 2, 1)
     far_steps = tuple(range(1, n_x))
     *results[4], _ = adam_table(
         at, told_squares, vec_total, state, far_own, far_pair, slab, half, n_x, far_steps, near

time: 679 us -> 692 us (1.019)
  waiting for transfers between devices: 13.9 us -> 29.7 us
  Pallas kernels: 547 us -> 538 us
    ppermute x4, waiting for transfers between devices: 3.39 us -> 12.1 us  [from_peer(): return lax.ppermute(x, axis, pairs)]
    all_gather x1, waiting for transfers between devices: 10.5 us -> 17.5 us  [on_device(): lax.all_gather(jnp.concatenate(given_rows), ('dp', 'seq'))]
  transfers between devices with their start and end apart: 5 -> 5, of which waited for: 2 -> 2; matrix products, arithmetic and copies ran while one was open for 8% -> 9% of each run, Pallas kernels for 49% -> 47%
where the time goes in v5:
time: 692 us; the launch traced here: 682 us
  Pallas kernels  538 us (78%)
  local copies, waits for them, and re-layouts  43 us (6%)
  other arithmetic  34.5 us (5%)
  waiting for transfers between devices  29.7 us (4%)
  between operations  25.2 us (4%)
    pallas_call x1, Pallas kernels, settle(): pl.pallas_call(body, out_shape=(jax.ShapeDtypeStruct((2, n_x, chunks, hei...  148 us
    pallas_call x2, Pallas kernels, staged(): pl.pallas_call(body, out_shape=tuple(outs.values()), in_specs=[HBM] * (le...  84.2 us
    pallas_call x5, Pallas kernels, deliver(): pl.pallas_call(body, out_shape=jax.ShapeDtypeStruct((count,) + block, x.d...  80 us
    pallas_call x1, Pallas kernels, read_heads(): pl.pallas_call(body, out_shape=(jax.ShapeDtypeStruct((n_dp, size, n_pick)...  76.3 us
    pallas_call x1, Pallas kernels, write_heads(): pl.pallas_call(body, out_shape=(jax.ShapeDtypeStruct((n_dp, width, n_pick...  61.2 us
    pallas_call x2, Pallas kernels, adam_table(): pl.pallas_call(body, grid_spec=pltpu.PrefetchScalarGridSpec(num_scalar_pr...  54.1 us
    all_gather x1, waiting for transfers between devices, on_device(): lax.all_gather(jnp.concatenate(given_rows), ('dp', 'seq'))  17.5 us
  transfers between devices with their start and end apart: 5, of which 2 were waited for; matrix products, arithmetic and copies ran while one was open for 9% of the time, Pallas kernels for 47%

profile of v5, /device:TPU:0, one launch (start us, length us, event | category | flops | bytes accessed | tf_op | source)
XLA Modules:
  0.0 681.6 jit_solution(9315097729880219153)
XLA Ops:
  12.7 5.8 shard_map.415
  32.6 16.4 %shard_map.416 = s32[32,32,128]{2,1,0:T(8,128)} custom-call(s32[32,128]{1,0:T(8,128)} %pad_add_fusion.x_ref), custom_call_target="tpu_custom_call" | custom-call | tf_op jit(solution)/shard_map/pallas_call | solution.py:88
  50.4 13.6 %shard_map.417 = (bf16[6400,768]{1,0:T(8,128)(2,1)}, bf16[768,6400]{1,0:T(8,128)(2,1)S(1)}) custom-call(f32[6288,768]{1,0:T(8,128)} %w_ref.3), custom_call_target="tpu_custom_call" | custom-call | tf_op jit(solution)/shard_map/pallas_call | solution.py:1203
  64.1 3.9 copy-done
  68.0 8.4 %gather_fusion.1 = bf16[768,768]{1,0:T(8,128)(2,1)S(1)} fusion(bf16[6400,768]{1,0:T(8,128)(2,1)} %get-tuple-element.752.t_ref, s32[1024]{0:T(1024)S(1)} %pad_clamp_fusion.1), kind=kCustom, calls=%fused_computation.1 | custom fusion | bytes 2362368 | tf_op jit(solution)/shard_map/jit(_take)/gather | solution.py:1544
  77.6 45.6 %shard_map.418 = bf16[8,96,768]{2,1,0:T(8,128)(2,1)} custom-call(bf16[8,96,768]{2,1,0:T(8,128)(2,1)} %broadcast_select_fusion.1.x_ref), custom_call_target="tpu_custom_call" | custom-call | tf_op jit(solution)/shard_map/pallas_call | solution.py:88
  123.7 4.5 fusion.18
  136.4 17.5 %all-gather.3.cloned.1.call-done = bf16[10240,768]{1,0:T(8,128)(2,1)} async-done(((bf16[320,768]{1,0:T(8,128)(2,1)}), bf16[10240,768]{1,0:T(8,128)(2,1)}) %all-gather.3.cloned.1.call-update) | async-done | bytes 15728656 | tf_op jit(solution)/shard_map/all_gather | solution.py:1444
  154.5 35.5 %shard_map.419 = (bf16[1024,768]{1,0:T(8,128)(2,1)}, bf16[1024,768]{1,0:T(8,128)(2,1)}, bf16[1024,768]{1,0:T(8,128)(2,1)}, bf16[256,768]{1,0:T(8,128)(2,1)}, f32...) custom-call(bf16[8,4,320,768]{3,2,1,0:T(8,128)(2,1)} %bitcast.142, ...), custom_call_target="tpu_custom_call" | custom-call | tf_op jit(solution)/shard_map/pallas_call | solution.py:873
  190.0 76.3 %shard_map.420 = (bf16[8,6400,256]{2,1,0:T(8,128)(2,1)}, bf16[8,256,768]{2,1,0:T(8,128)(2,1)}, f32[8,10,8,256]{3,2,1,0:T(8,128)}, f32[8,8,8,256]{3,2,1,0:T(8,128)}) custom-call(bf16[256,768]{1,0:T(8,128)(2,1)} %get-tuple-element.423.s_ref, bf16[6400,768]{1,0:T(8,128)(2,1)} %get-tuple-element.834, s32[8,1,256]{2,1,0:T(1,128)} %compare_select_fusion.3.target_ref), custom_call_target="tpu_custom_call" | custom-call | tf_op jit(solution)/shard_map/pallas_call | solution.py:590
  266.3 61.2 %shard_map.421 = (bf16[8,768,256]{2,1,0:T(8,128)(2,1)}, f32[2,8,1,256]{3,2,1,0:T(1,128)}, bf16[1600,768]{1,0:T(8,128)(2,1)}, bf16[1600,768]{1,0:T(8,128)(2,1)}) custom-call(bf16[8,6400,256]{2,1,0:T(8,128)(2,1)} %get-tuple-element.424.e_ref, bf16[2048,768]{1,0:T(8,128)(2,1)} %bitcast.151, bf16[768,6400]{1,0:T(8,128)(2,1)} %copy-done, ...), custom_call_target="tpu_custom_call" | custom-call | tf_op jit(solution)/shard_map/pallas_call | solution.py:777
  327.5 3.8 collective-permute-start
  337.6 48.7 %shard_map.422 = (bf16[8,1280,768]{2,1,0:T(8,128)(2,1)}, f32[16,768]{1,0:T(8,128)}, bf16[1024,768]{1,0:T(8,128)(2,1)}, bf16[1024,768]{1,0:T(8,128)(2,1)}) custom-call(bf16[8,4,320,768]{3,2,1,0:T(8,128)(2,1)} %bitcast.143, f32[256,768]{1,0:T(8,128)} %get-tuple-element.431.refs_1_, f32[256,768]{1,0:T(8,128)} %bitcast.150, ...), custom_call_target="tpu_custom_call" | custom-call | tf_op jit(solution)/shard_map/pallas_call | solution.py:873
  388.5 147.7 %shard_map.423 = (bf16[2,2,5,64,768]{4,3,2,1,0:T(8,128)(2,1)S(1)}, bf16[32,64,768]{2,1,0:T(8,128)(2,1)S(1)}, f32[16,768]{1,0:T(8,128)S(1)}) custom-call(bf16[8,2,2,5,64,768]{5,4,3,2,1,0:T(8,128)(2,1)} %bitcast.146, bf16[16,64,768]{2,1,0:T(8,128)(2,1)S(1)} %bitcast.137, f32[16,768]{1,0:T(8,128)S(1)} %copy-done.4), custom_call_target="tpu_custom_call" | custom-call | tf_op jit(solution)/shard_map/pallas_call | solution.py:406
  537.8 10.2 %shard_map.424 = (bf16[1600,768]{1,0:T(8,128)(2,1)}, f32[1,768]{1,0:T(1,128)S(1)}) custom-call(bf16[1600,768]{1,0:T(8,128)(2,1)S(1)} %copy-done.2, bf16[1600,768]{1,0:T(8,128)(2,1)} %collective-permute-done.other_ref, s32[1,2048]{1,0:T(1,128)S(1)} %sub.122.names_ref, bf16[2048,768]{1,0:T(8,128)(2,1)} %bitcast.136, bf16[1280,768]{1,0:T(8,128)(2,1)S(1)} %bitcast.139), custom_call_target="tpu_custom_call" | custom-call | tf_op jit(solution)/shard_map/pallas_call | solution.py:1246
  552.0 4.3 shard_map.425
  557.7 3.9 broadcast_add_fusion.1
  565.0 8.0 %shard_map.426.square_ref = f32[8,8,128]{2,1,0:T(8,128)} custom-call(f32[8,128]{1,0:T(8,128)} %reduce_sum.178.x_ref), custom_call_target="tpu_custom_call" | custom-call | tf_op jit(solution)/shard_map/pallas_call | solution.py:88
  576.4 27.1 %shard_map.427 = (f32[6288,768]{1,0:T(8,128)}, f32[6288,768]{1,0:T(8,128)}, f32[6288,768]{1,0:T(8,128)}, f32[8,128]{1,0:T(8,128)}) custom-call(s32[2]{0:T(128)} %pad_add_fusion.2.at_ref, f32[8,8,128]{2,1,0:T(8,128)} %shard_map.426.square_ref, f32[14,768]{1,0:T(8,128)} %get-tuple-element.555.vec_ref, f32[6288,768]{1,0:T(8,128)} %w_ref.3, f32[6288,768]{1,0:T(8,128)} %m_ref.3, ...), custom_call_target="tpu_custom_call" | custom-call | tf_op jit(solution)/shard_map/pallas_call | solution.py:1301
  605.5 12.1 %collective-permute-done.1 = bf16[1600,768]{1,0:T(8,128)(2,1)} collective-permute-done((bf16[1600,768]{1,0:T(8,128)(2,1)}, bf16[1600,768]{1,0:T(8,128)(2,1)}, u32[]{:S(2)}, u32[]{:S(2)}) %collective-permute-start.1) | collective-permute-done | bytes 2457632 | tf_op jit(solution)/shard_map/ppermute | solution.py:107
  617.6 3.3 broadcast_add_fusion.mine_ref
  631.2 3.3 slice_bitcast_fusion
  634.5 10.6 %shard_map.428 = (f32[96,2304]{1,0:T(8,128)}, f32[96,768]{1,0:T(8,128)}, f32[96,3072]{1,0:T(8,128)}, f32[384,768]{1,0:T(8,128)}, f32[128,768]{1,0:T(8,128)}, /*i...) custom-call(f32[1,1]{1,0:T(1,128)} %bitcast.56.factor_ref, ...), custom_call_target="tpu_custom_call" | custom-call | tf_op jit(solution)/shard_map/pallas_call | solution.py:1340
  645.1 27.0 %shard_map.429 = (f32[6288,768]{1,0:T(8,128)}, f32[6288,768]{1,0:T(8,128)}, f32[6288,768]{1,0:T(8,128)}, f32[8,128]{1,0:T(8,128)}) custom-call(s32[2]{0:T(128)} %pad_add_fusion.2.at_ref, f32[8,8,128]{2,1,0:T(8,128)} %shard_map.426.square_ref, f32[14,768]{1,0:T(8,128)} %get-tuple-element.555.vec_ref, ...), custom_call_target="tpu_custom_call", output_to_operand_aliasing={{0}: (8, {}), {1}: (9, {}), {2}: (10, {})} | custom-call | tf_op jit(solution)/shard_map/pallas_call | solution.py:1301
  (117 shorter events, 59.3 us)
Async XLA Ops:
  7.2 11.3 %copy-start.14 = (s32[32,256]{1,0:T(8,128)S(1)}, s32[32,256]{1,0:T(8,128)}, u32[]{:S(2)}) copy-start(s32[32,256]{1,0:T(8,128)} %param.30) | copy-start | bytes 98308
  7.2 146.7 %all-gather.3.cloned.1.call-start = ((), (), s32[]{:S(2)}) async-start(), calls=%async_computation.3 | async-start | bytes 16220160 | tf_op jit(solution)/shard_map/all_gather | solution.py:1444
  18.5 45.6 %copy-start.15 = (s32[1,256]{1,0:T(1,128)}, s32[1,256]{1,0:T(1,128)S(1)}, u32[]{:S(2)}) copy-start(s32[1,256]{1,0:T(1,128)S(1)} %constant_dynamic-slice_fusion.4.refs_18_) | copy-start | bytes 3076
  64.1 3.9 copy-start
  129.1 3.2 copy-start.17
  327.5 8.2 %copy-start.16 = (f32[2,8,1,256]{3,2,1,0:T(1,128)S(1)}, f32[2,8,1,256]{3,2,1,0:T(1,128)}, u32[]{:S(2)}) copy-start(f32[2,8,1,256]{3,2,1,0:T(1,128)} %get-tuple-element.441) | copy-start | bytes 49156
  327.5 210.3 %collective-permute-start = (bf16[1600,768]{1,0:T(8,128)(2,1)}, bf16[1600,768]{1,0:T(8,128)(2,1)}, u32[]{:S(2)}, u32[]{:S(2)}) collective-permute-start(bf16[1600,768]{1,0:T(8,128)(2,1)} %get-tuple-element.430), channel_id=1, source_target_pairs={{0,2},{1,3},{2,0},{3,1},{4,6},{5,7},{6,4},{7,5},{8,10},{9,11},{10,... | collective-permute-start | bytes 7372808 | tf_op jit(solution)/shard_map/ppermute | solution.py:107
  386.2 1.4 copy-start.3
  387.7 0.8 copy-start.4
  388.5 149.4 %copy-start.2 = (bf16[1600,768]{1,0:T(8,128)(2,1)S(1)}, bf16[1600,768]{1,0:T(8,128)(2,1)}, u32[]{:S(2)}) copy-start(bf16[1600,768]{1,0:T(8,128)(2,1)} %get-tuple-element.429.own_ref) | copy-start | bytes 7372804
  536.2 1.7 copy-start.1
  537.8 10.2 %copy-start.6 = (bf16[2,2,5,64,768]{4,3,2,1,0:T(8,128)(2,1)}, bf16[2,2,5,64,768]{4,3,2,1,0:T(8,128)(2,1)S(1)}, u32[]{:S(2)}) copy-start(bf16[2,2,5,64,768]{4,3,2,1,0:T(8,128)(2,1)S(1)} %get-tuple-element.446) | copy-start | bytes 5898244
  550.5 25.2 %copy-start.10 = (f32[14,768]{1,0:T(8,128)S(1)}, f32[14,768]{1,0:T(8,128)}, u32[]{:S(2)}) copy-start(f32[14,768]{1,0:T(8,128)} %refs_16_.2) | copy-start | bytes 129028
  550.5 25.2 %copy-start.12 = (f32[14,768]{1,0:T(8,128)S(1)}, f32[14,768]{1,0:T(8,128)}, u32[]{:S(2)}) copy-start(f32[14,768]{1,0:T(8,128)} %param.44) | copy-start | bytes 129028
  550.6 25.2 %copy-start.13 = (f32[14,768]{1,0:T(8,128)S(1)}, f32[14,768]{1,0:T(8,128)}, u32[]{:S(2)}) copy-start(f32[14,768]{1,0:T(8,128)} %param.51) | copy-start | bytes 129028
  550.6 25.9 %copy-start.5 = (bf16[1600,768]{1,0:T(8,128)(2,1)S(1)}, bf16[1600,768]{1,0:T(8,128)(2,1)}, u32[]{:S(2)}) copy-start(bf16[1600,768]{1,0:T(8,128)(2,1)} %get-tuple-element.452.mine_ref) | copy-start | bytes 7372804
  556.3 8.1 %copy-start.11 = (f32[4,8,128]{2,1,0:T(8,128)S(1)}, f32[4,8,128]{2,1,0:T(8,128)}, u32[]{:S(2)}) copy-start(f32[4,8,128]{2,1,0:T(8,128)} %shard_map.425) | copy-start | bytes 49156
  556.3 20.1 %collective-permute-start.2 = (bf16[1600,768]{1,0:T(8,128)(2,1)}, bf16[1600,768]{1,0:T(8,128)(2,1)}, u32[]{:S(2)}, u32[]{:S(2)}) collective-permute-start(bf16[1600,768]{1,0:T(8,128)(2,1)} %get-tuple-element.452.mine_ref), channel_id=1, source_target_pairs={{0,1},{1,0},{2,3},{3,2},{4,5},{5,4},{6,7},{7,6},{8,9},{9,8},{10,11... | collective-permute-start | bytes 7372808 | tf_op jit(solution)/shard_map/ppermute | solution.py:107
  561.6 56.0 %collective-permute-start.1 = (bf16[1600,768]{1,0:T(8,128)(2,1)}, bf16[1600,768]{1,0:T(8,128)(2,1)}, u32[]{:S(2)}, u32[]{:S(2)}) collective-permute-start(bf16[1600,768]{1,0:T(8,128)(2,1)} %broadcast_add_fusion.1), channel_id=1, source_target_pairs={{0,2},{1,3},{2,0},{3,1},{4,6},{5,7},{6,4},{7,5},{8,10},{9,11},{10,... | collective-permute-start | bytes 7372808 | tf_op jit(solution)/shard_map/ppermute | solution.py:107
  603.5 19.7 %copy-start.8 = (bf16[1280,768]{1,0:T(8,128)(2,1)S(1)}, bf16[1280,768]{1,0:T(8,128)(2,1)}, u32[]{:S(2)}) copy-start(bf16[1280,768]{1,0:T(8,128)(2,1)} %get-tuple-element.836) | copy-start | bytes 5898244
  620.9 24.2 %collective-permute-start.3 = (bf16[1600,768]{1,0:T(8,128)(2,1)}, bf16[1600,768]{1,0:T(8,128)(2,1)}, u32[]{:S(2)}, u32[]{:S(2)}) collective-permute-start(bf16[1600,768]{1,0:T(8,128)(2,1)} %broadcast_add_fusion.mine_ref), channel_id=1, source_target_pairs={{0,1},{1,0},{2,3},{3,2},{4,5},{5,4},{6,7},{7,6},{8,9},{9,8},{10,11... | collective-permute-start | bytes 7372808 | tf_op jit(solution)/shard_map/ppermute | solution.py:107
  624.3 1.9 copy-start.9
Sparse Core Ops, SparseCore 0:
  12.8 140.9 all-gather.2
